TPU v7x, 32 devices: a whole 2x2x4 slice. The times are simulated.
32 devices in a mesh: ep: 8 (over z, y), tp: 4 (over x, core).
Axes of the slice: x: 2, y: 2, z: 4, core: 2. Of those that a mesh axis runs over, the one named last changes fastest.
Arguments:
- block_in: bfloat16 [4096, 2048], P('ep'), may hold values from -6 to 6
- input_norm: float32 [2048], replicated, may hold values from 0.25 to 1.75
- q_weight: bfloat16 [2048, 4096], P(None, 'tp'), may hold values from -0.125 to 0.125
- k_weight: bfloat16 [2048, 512], P(None, 'tp'), may hold values from -0.125 to 0.125
- v_weight: bfloat16 [2048, 512], P(None, 'tp'), may hold values from -0.125 to 0.125
- q_gain: float32 [128], replicated, may hold values from 1 to 2
- k_gain: float32 [128], replicated, may hold values from 1 to 1.6
- o_weight: bfloat16 [4096, 2048], P('tp'), may hold values from -0.375 to 0.375
- post_norm: float32 [2048], replicated, may hold values from 0.25 to 1.75
- router: bfloat16 [2048, 32], replicated, may hold values from -0.0625 to 0.0625
- expert_gate: bfloat16 [32, 2048, 768], P('ep', None, 'tp'), may hold values from -0.125 to 0.125
- expert_up: bfloat16 [32, 2048, 768], P('ep', None, 'tp'), may hold values from -0.125 to 0.125
- expert_down: bfloat16 [32, 768, 2048], P('ep', 'tp'), may hold values from -0.875 to 0.875
- expert_ids: int32 [4096, 8], P('ep'), may hold values from 0 to 31, all different within a row; in each aligned block of 512 rows (0 to 511, 512 to 1023, ...) at most 192 rows name the same one
- prefix_len: int32 [2], replicated, may hold values from 204 to 1024
- out_grad: bfloat16 [4096, 2048], P('ep'), may hold values from -6 to 6
Outputs:
- block_out: bfloat16 [4096, 2048], P('ep', 'tp')
- input_grad: bfloat16 [4096, 2048], P('ep')
- input_norm_grad: float32 [2048], replicated
- q_weight_grad: float32 [2048, 4096], P(None, 'tp')
- k_weight_grad: float32 [2048, 512], P(None, 'tp')
- v_weight_grad: float32 [2048, 512], P(None, 'tp')
- q_gain_grad: float32 [128], replicated
- k_gain_grad: float32 [128], replicated
- o_weight_grad: float32 [4096, 2048], P('tp')
- post_norm_grad: float32 [2048], replicated
- router_grad: float32 [2048, 32], replicated
- gate_grad: float32 [32, 2048, 768], P('ep', None, 'tp')
- up_grad: float32 [32, 2048, 768], P('ep', None, 'tp')
- down_grad: float32 [32, 768, 2048], P('ep', 'tp')
Inputs may be any that keep to these rules, and one draw needn't show every extreme that they name: `expert_ids`: each token names 8 different experts. Among the 512 tokens of one index of ep no expert is named more than 192 times, and in every draw some expert is named exactly 192 times by the tokens of some index.
All inputs are finite; a program needn't handle non-finite values.
Results may differ from a plain program's by a relative error of at most 0.028.
Values may be sent and summed in bfloat16 or wider, within the bound.
No kernel may reach another device: no remote copies, remote signals or barrier semaphores. Data moves between devices by JAX's collectives and lax.ppermute only.
A program may use at most 512 MiB of HBM per device.

v0:
```python
import jax
import jax.numpy as jnp
from jax import lax
from jax.sharding import PartitionSpec as P

SPAN = 4


EPSILON = 1e-06
THETA = 1000000.0
MASKED = -1e30


def shifted(block, axis, distance):
    devices = range(lax.axis_size(axis))
    route = [(i - distance, i) for i in devices if i - distance in devices]
    return lax.ppermute(block, axis, route)


def rms_scale(values, scales):
    return values * lax.rsqrt(jnp.mean(values * values, axis=-1, keepdims=True) + EPSILON) * scales


def rotary_tables(positions, head_width):
    half_width = head_width // 2
    exponents = jnp.arange(half_width, dtype=jnp.float32) * (-2.0 / head_width)
    angles = positions.astype(jnp.float32)[:, None] * (THETA**exponents)[None, :]
    return (jnp.cos(angles), jnp.sin(angles))


def rotate(values, cos_table, sin_table):
    half_width = values.shape[-1] // 2
    shape_rows = (values.shape[0],) + (1,) * (values.ndim - 2) + (half_width,)
    cos_rows = cos_table.reshape(shape_rows)
    sin_rows = sin_table.reshape(shape_rows)
    lead_half = values[..., :half_width]
    tail_half = values[..., half_width:]
    return jnp.concatenate(
        [lead_half * cos_rows - tail_half * sin_rows, tail_half * cos_rows + lead_half * sin_rows],
        axis=-1,
    )


def fetch_rows(pair_rows, distance):
    return shifted((pair_rows[0], pair_rows[1]), "ep", distance)


def return_grads(pair_grads, distance):
    return (
        shifted(pair_grads[0].astype(jnp.bfloat16), "ep", distance).astype(jnp.float32),
        shifted(pair_grads[1].astype(jnp.bfloat16), "ep", distance).astype(jnp.float32),
    )


def to_owners(row_block):
    return lax.all_to_all(row_block, "ep", split_axis=0, concat_axis=0, tiled=True)


def from_owners(row_block):
    return lax.all_to_all(row_block, "ep", split_axis=0, concat_axis=0, tiled=True)


def owner_sum(values):
    return lax.psum_scatter(
        values.astype(jnp.bfloat16), "tp", scatter_dimension=3, tiled=True
    ).astype(jnp.float32)


def body(
    block_in,
    input_norm,
    q_weight,
    k_weight,
    v_weight,
    q_gain,
    k_gain,
    o_weight,
    post_norm,
    router,
    expert_gate,
    expert_up,
    expert_down,
    expert_ids,
    prefix_len,
    out_grad,
):
    tokens = block_in.shape[0]
    model_width = block_in.shape[1]
    head_width = q_gain.shape[0]
    kv_heads = k_weight.shape[1] // head_width
    group_size = q_weight.shape[1] // head_width // kv_heads
    tp_count = lax.axis_size("tp")
    tp_rank = lax.axis_index("tp")
    ep_count = lax.axis_size("ep")
    ep_rank = lax.axis_index("ep")
    share_width = model_width // tp_count
    seq_span = SPAN
    dev_slot = ep_rank % seq_span
    block_pos = (dev_slot + seq_span - 1) % seq_span
    prefix = lax.dynamic_index_in_dim(prefix_len, ep_rank // seq_span, keepdims=False)
    row_index = jnp.arange(tokens, dtype=jnp.int32)
    positions = block_pos * tokens + row_index
    score_scale = head_width ** (-0.5)

    def column_share(full_rows):
        return lax.dynamic_slice_in_dim(full_rows, tp_rank * share_width, share_width, 1)

    x_full = block_in.astype(jnp.float32)
    attn_in, input_norm_back = jax.vjp(rms_scale, x_full, input_norm)
    attn_low = attn_in.astype(jnp.bfloat16)
    q_lin = jnp.dot(attn_low, q_weight, preferred_element_type=jnp.float32).reshape(
        tokens, kv_heads, group_size, head_width
    )
    k_lin = jnp.dot(attn_low, k_weight, preferred_element_type=jnp.float32).reshape(
        tokens, kv_heads, head_width
    )
    v_lin = jnp.dot(attn_low, v_weight, preferred_element_type=jnp.float32).reshape(
        tokens, kv_heads, head_width
    )
    cos_table, sin_table = rotary_tables(positions, head_width)

    def head_path(lin_rows, scales):
        return rotate(rms_scale(lin_rows, scales), cos_table, sin_table)

    q_rot, q_back = jax.vjp(head_path, q_lin, q_gain)
    k_rot, k_back = jax.vjp(head_path, k_lin, k_gain)
    q_low = q_rot.astype(jnp.bfloat16)
    k_low = k_rot.astype(jnp.bfloat16)
    v_low = v_lin.astype(jnp.bfloat16)
    distances = list(range(seq_span))
    key_blocks = []
    allowed_blocks = []
    for distance in distances:
        if distance == 0:
            pair_rows = (k_low, v_low)
        else:
            below = fetch_rows((k_low, v_low), distance)
            above = fetch_rows((k_low, v_low), distance - seq_span)
            use_below = dev_slot >= distance
            pair_rows = (
                jnp.where(use_below, below[0], above[0]),
                jnp.where(use_below, below[1], above[1]),
            )
        source_slot = (dev_slot - distance) % seq_span
        source_pos = (source_slot + seq_span - 1) % seq_span
        key_pos = source_pos * tokens + row_index
        allowed = (key_pos[None, :] <= positions[:, None]) | (key_pos[None, :] < prefix)
        key_blocks.append(pair_rows)
        allowed_blocks.append(allowed)

    def block_scores(pair_rows, allowed):
        raw_scores = (
            jnp.einsum("tkgd,ukd->kgtu", q_low, pair_rows[0], preferred_element_type=jnp.float32)
            * score_scale
        )
        return jnp.where(allowed[None, None], raw_scores, MASKED)

    def block_probs(pair_rows, allowed, log_total):
        return jnp.where(
            allowed[None, None],
            jnp.exp(block_scores(pair_rows, allowed) - log_total[..., None]),
            0.0,
        )

    log_total = jnp.full((kv_heads, group_size, tokens), MASKED, jnp.float32)
    for pair_rows, allowed in zip(key_blocks, allowed_blocks):
        log_total = jnp.logaddexp(
            log_total, jax.nn.logsumexp(block_scores(pair_rows, allowed), axis=-1)
        )
    attn_acc = jnp.zeros((tokens, kv_heads, group_size, head_width), jnp.float32)
    for pair_rows, allowed in zip(key_blocks, allowed_blocks):
        prob_low = block_probs(pair_rows, allowed, log_total).astype(jnp.bfloat16)
        attn_acc = attn_acc + jnp.einsum(
            "kgtu,ukd->tkgd", prob_low, pair_rows[1], preferred_element_type=jnp.float32
        )
    o_low = attn_acc.reshape(tokens, -1).astype(jnp.bfloat16)
    head_part = jnp.dot(o_low, o_weight, preferred_element_type=jnp.float32)
    x_mid = x_full + lax.psum(head_part.astype(jnp.bfloat16), "tp").astype(jnp.float32)
    ffn_in, post_norm_back = jax.vjp(rms_scale, x_mid, post_norm)
    ffn_low = ffn_in.astype(jnp.bfloat16)
    logits = jnp.dot(ffn_low, router, preferred_element_type=jnp.float32)
    experts_all = router.shape[1]
    top_count = expert_ids.shape[1]
    chosen = expert_ids[:, :, None] == jnp.arange(experts_all, dtype=jnp.int32)[None, None, :]

    def route_gates(logit_rows):
        picked = jnp.sum(jnp.where(chosen, logit_rows[:, None, :], 0.0), axis=-1)
        return jax.nn.softmax(picked, axis=-1)

    gate_probs, gates_back = jax.vjp(route_gates, logits)
    local_experts = expert_gate.shape[0]
    capacity = 3 * tokens * top_count // (2 * experts_all)
    assigned = tokens * top_count
    flat_ids = expert_ids.reshape(-1)
    expert_hits = (flat_ids[:, None] == jnp.arange(experts_all, dtype=jnp.int32)[None, :]).astype(
        jnp.int32
    )
    slot_ranks = jnp.sum(expert_hits * (jnp.cumsum(expert_hits, axis=0) - 1), axis=1)
    slot_index = flat_ids * capacity + slot_ranks
    owners = (
        jnp.full((experts_all * capacity,), assigned, jnp.int32)
        .at[slot_index]
        .set(jnp.arange(assigned, dtype=jnp.int32))
    )
    slot_tokens = owners // top_count
    slot_gates = jnp.concatenate([gate_probs.reshape(-1), jnp.zeros((1,), jnp.float32)])[owners]
    padded_rows = jnp.concatenate([ffn_low, jnp.zeros((1, model_width), jnp.bfloat16)], axis=0)
    send_forward = padded_rows[slot_tokens].reshape(ep_count, local_experts, capacity, -1)
    arrived = to_owners(send_forward)
    gate_pre = jnp.einsum(
        "secd,edf->secf", arrived, expert_gate, preferred_element_type=jnp.float32
    )
    up_pre = jnp.einsum("secd,edf->secf", arrived, expert_up, preferred_element_type=jnp.float32)
    gate_sig = jax.nn.sigmoid(gate_pre)
    silu_vals = gate_pre * gate_sig
    hidden_low = (silu_vals * up_pre).astype(jnp.bfloat16)
    expert_out = jnp.einsum(
        "secf,efd->secd", hidden_low, expert_down, preferred_element_type=jnp.float32
    )
    out_low = owner_sum(expert_out).astype(jnp.bfloat16)
    returned = from_owners(out_low).reshape(experts_all * capacity, share_width)
    mixed_rows = returned[slot_index].reshape(tokens, top_count, share_width).astype(jnp.float32)
    x_share = column_share(x_mid)
    block_out = (x_share + jnp.sum(gate_probs[:, :, None] * mixed_rows, axis=1)).astype(
        jnp.bfloat16
    )
    grad_full = out_grad.astype(jnp.float32)
    grad_share = column_share(grad_full)
    gate_dots = lax.psum(jnp.sum(grad_share[:, None, :] * mixed_rows, axis=-1), "tp")
    (d_logits,) = gates_back(gate_dots)
    dlog_low = d_logits.astype(jnp.bfloat16)
    grad_rows = jnp.concatenate([grad_full, jnp.zeros((1, model_width), jnp.float32)], axis=0)
    send_backward = (
        (grad_rows[slot_tokens] * slot_gates[:, None])
        .astype(jnp.bfloat16)
        .reshape(ep_count, local_experts, capacity, -1)
    )
    arrived_grad = to_owners(send_backward)
    d_hidden = jnp.einsum(
        "secd,efd->secf", arrived_grad, expert_down, preferred_element_type=jnp.float32
    )
    down_grad = jnp.einsum(
        "secf,secd->efd", hidden_low, arrived_grad, preferred_element_type=jnp.float32
    )
    d_gate_low = (d_hidden * up_pre * gate_sig * (1.0 + gate_pre * (1.0 - gate_sig))).astype(
        jnp.bfloat16
    )
    d_up_low = (d_hidden * silu_vals).astype(jnp.bfloat16)
    gate_grad = jnp.einsum(
        "secd,secf->edf", arrived, d_gate_low, preferred_element_type=jnp.float32
    )
    up_grad = jnp.einsum("secd,secf->edf", arrived, d_up_low, preferred_element_type=jnp.float32)
    row_grads = jnp.einsum(
        "secf,edf->secd", d_gate_low, expert_gate, preferred_element_type=jnp.float32
    )
    row_grads = row_grads + jnp.einsum(
        "secf,edf->secd", d_up_low, expert_up, preferred_element_type=jnp.float32
    )
    grads_low = owner_sum(row_grads).astype(jnp.bfloat16)
    returned_grad = from_owners(grads_low).reshape(experts_all * capacity, share_width)
    d_ffn_share = jnp.sum(
        returned_grad[slot_index].reshape(tokens, top_count, share_width).astype(jnp.float32),
        axis=1,
    )
    router_share = lax.dynamic_slice_in_dim(router, tp_rank * share_width, share_width, 0)
    d_ffn_share = d_ffn_share + jnp.einsum(
        "te,qe->tq", dlog_low, router_share, preferred_element_type=jnp.float32
    )
    d_ffn = lax.all_gather(d_ffn_share.astype(jnp.bfloat16), "tp", axis=1, tiled=True).astype(
        d_ffn_share.dtype
    )
    router_grad = jnp.einsum("td,te->de", ffn_low, dlog_low, preferred_element_type=jnp.float32)
    d_mid_norm, post_norm_grad = post_norm_back(d_ffn)
    d_mid = grad_full + d_mid_norm
    d_mid_low = d_mid.astype(jnp.bfloat16)
    o_weight_grad = jnp.einsum("tj,td->jd", o_low, d_mid_low, preferred_element_type=jnp.float32)
    d_attn_low = (
        jnp.einsum("td,jd->tj", d_mid_low, o_weight, preferred_element_type=jnp.float32)
        .astype(jnp.bfloat16)
        .reshape(tokens, kv_heads, group_size, head_width)
    )
    row_delta = jnp.sum(d_attn_low.astype(jnp.float32) * attn_acc, axis=-1).transpose(1, 2, 0)
    q_grad_rot = jnp.zeros((tokens, kv_heads, group_size, head_width), jnp.float32)
    k_grad_rot = jnp.zeros((tokens, kv_heads, head_width), jnp.float32)
    v_grad_sum = jnp.zeros((tokens, kv_heads, head_width), jnp.float32)
    for distance, pair_rows, allowed in zip(distances, key_blocks, allowed_blocks):
        probs = block_probs(pair_rows, allowed, log_total)
        d_probs = jnp.einsum(
            "tkgd,ukd->kgtu", d_attn_low, pair_rows[1], preferred_element_type=jnp.float32
        )
        d_scores = (probs * (d_probs - row_delta[..., None])).astype(jnp.bfloat16)
        q_grad_rot = (
            q_grad_rot
            + jnp.einsum(
                "kgtu,ukd->tkgd", d_scores, pair_rows[0], preferred_element_type=jnp.float32
            )
            * score_scale
        )
        key_grad = (
            jnp.einsum("kgtu,tkgd->ukd", d_scores, q_low, preferred_element_type=jnp.float32)
            * score_scale
        )
        value_grad = jnp.einsum(
            "kgtu,tkgd->ukd",
            probs.astype(jnp.bfloat16),
            d_attn_low,
            preferred_element_type=jnp.float32,
        )
        if distance == 0:
            k_grad_rot = key_grad
            v_grad_sum = value_grad
        else:
            use_below = dev_slot >= distance
            back_below = return_grads(
                (jnp.where(use_below, key_grad, 0.0), jnp.where(use_below, value_grad, 0.0)),
                -distance,
            )
            back_above = return_grads(
                (jnp.where(use_below, 0.0, key_grad), jnp.where(use_below, 0.0, value_grad)),
                seq_span - distance,
            )
            k_grad_rot = k_grad_rot + back_below[0] + back_above[0]
            v_grad_sum = v_grad_sum + back_below[1] + back_above[1]
    dq_lin, q_gain_grad = q_back(q_grad_rot)
    dk_lin, k_gain_grad = k_back(k_grad_rot)
    dq_low = dq_lin.reshape(tokens, -1).astype(jnp.bfloat16)
    dk_low = dk_lin.reshape(tokens, -1).astype(jnp.bfloat16)
    dv_low = v_grad_sum.reshape(tokens, -1).astype(jnp.bfloat16)
    q_weight_grad = jnp.einsum("td,tj->dj", attn_low, dq_low, preferred_element_type=jnp.float32)
    k_weight_grad = jnp.einsum("td,tj->dj", attn_low, dk_low, preferred_element_type=jnp.float32)
    v_weight_grad = jnp.einsum("td,tj->dj", attn_low, dv_low, preferred_element_type=jnp.float32)
    d_attn_in = jnp.einsum("tj,dj->td", dq_low, q_weight, preferred_element_type=jnp.float32)
    d_attn_in = d_attn_in + jnp.einsum(
        "tj,dj->td", dk_low, k_weight, preferred_element_type=jnp.float32
    )
    d_attn_in = d_attn_in + jnp.einsum(
        "tj,dj->td", dv_low, v_weight, preferred_element_type=jnp.float32
    )
    d_attn_in, q_gain_grad, k_gain_grad = (
        lax.psum(d_attn_in.astype(jnp.bfloat16), "tp").astype(jnp.float32),
        lax.psum(q_gain_grad.astype(jnp.bfloat16), "tp").astype(jnp.float32),
        lax.psum(k_gain_grad.astype(jnp.bfloat16), "tp").astype(jnp.float32),
    )
    d_in_norm, input_norm_grad = input_norm_back(d_attn_in)
    input_grad = (d_mid + d_in_norm).astype(jnp.bfloat16)
    (
        q_weight_grad,
        k_weight_grad,
        v_weight_grad,
        o_weight_grad,
        router_grad,
        input_norm_grad,
        post_norm_grad,
        q_gain_grad,
        k_gain_grad,
    ) = (
        lax.psum(q_weight_grad.astype(jnp.bfloat16), "ep").astype(jnp.float32),
        lax.psum(k_weight_grad.astype(jnp.bfloat16), "ep").astype(jnp.float32),
        lax.psum(v_weight_grad.astype(jnp.bfloat16), "ep").astype(jnp.float32),
        lax.psum(o_weight_grad.astype(jnp.bfloat16), "ep").astype(jnp.float32),
        lax.psum(router_grad.astype(jnp.bfloat16), "ep").astype(jnp.float32),
        lax.psum(input_norm_grad.astype(jnp.bfloat16), "ep").astype(jnp.float32),
        lax.psum(post_norm_grad.astype(jnp.bfloat16), "ep").astype(jnp.float32),
        lax.psum(q_gain_grad.astype(jnp.bfloat16), "ep").astype(jnp.float32),
        lax.psum(k_gain_grad.astype(jnp.bfloat16), "ep").astype(jnp.float32),
    )
    return (
        block_out,
        input_grad,
        input_norm_grad,
        q_weight_grad,
        k_weight_grad,
        v_weight_grad,
        q_gain_grad,
        k_gain_grad,
        o_weight_grad,
        post_norm_grad,
        router_grad,
        gate_grad,
        up_grad,
        down_grad,
    )


def solution(mesh):
    in_specs = (
        P("ep", None),
        P(),
        P(None, "tp"),
        P(None, "tp"),
        P(None, "tp"),
        P(),
        P(),
        P("tp", None),
        P(),
        P(),
        P("ep", None, "tp"),
        P("ep", None, "tp"),
        P("ep", "tp", None),
        P("ep", None),
        P(),
        P("ep", None),
    )
    out_specs = (
        P("ep", "tp"),
        P("ep", None),
        P(),
        P(None, "tp"),
        P(None, "tp"),
        P(None, "tp"),
        P(),
        P(),
        P("tp", None),
        P(),
        P(),
        P("ep", None, "tp"),
        P("ep", None, "tp"),
        P("ep", "tp", None),
    )
    return jax.shard_map(body, mesh=mesh, in_specs=in_specs, out_specs=out_specs, check_vma=False)
```

profile of v0, /device:TPU:0, one launch (start us, length us, event | category | flops | bytes accessed | tf_op | source)
XLA Modules:
  0.0 2517.0 jit_solution(15215753802171052642)
XLA Ops:
  34.4 7.9 collective-permute-start.4
  58.2 18.1 reduce-window.6
  142.0 14.1 fusion.47
  178.2 15.5 scatter_custom_fusion
  194.4 36.6 %all-reduce.13.cloned.1.call-done = bf16[512,2048]{1,0:T(8,128)(2,1)} async-done(((bf16[512,2048]{1,0:T(8,128)(2,1)}), bf16[512,2048]{1,0:T(8,128)(2,1)}) %all-reduce.13.cloned.1.call-update) | async-done | bytes 2097168 | tf_op jit(solution)/shard_map/psum | solution.py:178
  238.7 48.2 %gather_fusion = bf16[6144,2048]{1,0:T(8,128)(2,1)} fusion(bf16[513,2048]{1,0:T(8,128)(2,1)} %concatenate.55, s32[6144]{0:T(1024)S(1)} %get-tuple-element.61), kind=kCustom, calls=%fused_computation | custom fusion | bytes 50356224 | tf_op jit(solution)/shard_map/gather | solution.py:208
  297.6 49.0 %gather_fusion.2 = f32[6144,2048]{1,0:T(8,128)} fusion(f32[513,2048]{1,0:T(8,128)} %concatenate.56, s32[6144]{0:T(1024)S(1)} %get-tuple-element.61), kind=kCustom, calls=%fused_computation.2 | custom fusion | bytes 100687872 | tf_op jit(solution)/shard_map/gather | solution.py:234
  351.2 34.3 %gather_fusion.3 = f32[6144]{0:T(1024)S(1)} fusion(f32[4097]{0:T(1024)S(1)} %pad_maximum_fusion.2, s32[6144]{0:T(1024)S(1)} %copy-done.84), kind=kCustom, calls=%fused_computation.3 | custom fusion | bytes 73728 | tf_op jit(solution)/shard_map/gather | solution.py:206
  385.6 25.8 %multiply_convert_fusion = bf16[8,4,192,2048]{3,2,1,0:T(8,128)(2,1)} fusion(f32[8,4,192,2048]{3,2,1,0:T(8,128)} %bitcast.527, f32[8,4,192]{2,1,0:T(4,128)S(1)} %mul.678), kind=kLoop, calls=%fused_computation.7 | loop fusion | flops 25165824 | bytes 75522048 | tf_op jit(solution)/shard_map/convert_element_type | solution.py:235
  411.3 424.8 %all-to-all-done = bf16[8,4,192,2048]{3,2,1,0:T(8,128)(2,1)} async-done(((bf16[8,4,192,2048]{3,2,1,0:T(8,128)(2,1)}), bf16[8,4,192,2048]{3,2,1,0:T(8,128)(2,1)}, u32[]{:S(2)}, u32[]{:S(2)}) %all-to-all-start) | async-done | bytes 25165856 | tf_op jit(solution)/shard_map/all_to_all | solution.py:56
  843.0 14.2 fusion.5
  857.1 14.2 fusion.7
  871.3 513.4 %all-to-all-done.2 = bf16[8,4,192,2048]{3,2,1,0:T(8,128)(2,1)} async-done(((bf16[8,4,192,2048]{3,2,1,0:T(8,128)(2,1)}), bf16[8,4,192,2048]{3,2,1,0:T(8,128)(2,1)}, u32[]{:S(2)}, u32[]{:S(2)}) %all-to-all-start.2) | async-done | bytes 25165856 | tf_op jit(solution)/shard_map/all_to_all | solution.py:56
  1384.7 19.4 fusion.26
  1404.1 14.0 convert_bitcast_fusion
  1418.2 33.3 %fusion.64 = f32[4,8,192,2048]{3,2,1,0:T(8,128)} fusion(bf16[8,4,192,192]{3,2,0,1:T(8,128)(2,1)} %get-tuple-element.36, bf16[4,2048,192]{1,2,0:T(8,128)(2,1)} %param.26), kind=kOutput, calls=%fused_computation.114 | convolution fusion | flops 4831838208 | bytes 55836672 | tf_op jit(solution)/shard_map/secf,edf->secd/dot_general | solution.py:253
  1451.4 29.5 %fusion = bf16[8,4,192,2048]{3,2,0,1:T(8,128)(2,1)} fusion(f32[4,8,192,2048]{3,2,1,0:T(8,128)} %fusion.64, bf16[8,4,192,192]{3,2,0,1:T(8,128)(2,1)} %get-tuple-element.35, bf16[4,2048,192]{1,2,0:T(8,128)(2,1)} %param.27), kind=kOutput, calls=%fused_computation.8 | convolution fusion | flops 4857004032 | bytes 81002496 | tf_op jit(solution)/shard_map/secf,edf->secd/dot_general | solution.py:256
  1480.9 116.2 %reduce-scatter.3.cloned.1.call-done = bf16[8,4,192,512]{3,2,0,1:T(8,128)(2,1)} async-done(((bf16[8,4,192,2048]{3,2,0,1:T(8,128)(2,1)}), bf16[8,4,192,512]{3,2,0,1:T(8,128)(2,1)}) %reduce-scatter.3.cloned.1.call-update) | async-done | bytes 6291472 | tf_op jit(solution)/shard_map/reduce_scatter | solution.py:64
  1608.8 171.4 %reduce-scatter.5.cloned.1.call-done = bf16[8,4,192,512]{3,2,0,1:T(8,128)(2,1)} async-done(((bf16[8,4,192,2048]{3,2,0,1:T(8,128)(2,1)}), bf16[8,4,192,512]{3,2,0,1:T(8,128)(2,1)}) %reduce-scatter.5.cloned.1.call-update) | async-done | bytes 6291472 | tf_op jit(solution)/shard_map/reduce_scatter | solution.py:64
  1798.4 21.3 gather_fusion.1
  1827.7 10.9 psum.99
  1838.8 91.4 %all-to-all-done.3 = bf16[8,4,192,512]{3,2,1,0:T(8,128)(2,1)} async-done(((bf16[8,4,192,512]{3,2,1,0:T(8,128)(2,1)}), bf16[8,4,192,512]{3,2,1,0:T(8,128)(2,1)}, u32[]{:S(2)}, u32[]{:S(2)}) %all-to-all-start.3) | async-done | bytes 6291488 | tf_op jit(solution)/shard_map/all_to_all | solution.py:60
  1930.2 21.0 gather_fusion.4
  1958.2 8.4 copy.516
  1966.6 8.0 copy.519
  1974.6 8.0 copy.522
  1982.6 8.0 copy.514
  2137.2 15.0 convolution_bitcast_fusion
  2152.2 14.8 convolution_bitcast_fusion.1
  2167.0 13.8 fusion.57
  2190.5 23.2 all-reduce.6
  2224.1 268.6 %all-reduce.17.cloned.1.call-done = (bf16[2048,1024]{1,0:T(8,128)(2,1)}, bf16[2048,128]{1,0:T(8,128)(2,1)}, bf16[2048,128]{1,0:T(8,128)(2,1)}, bf16[1024,2048]{1,0:T(8,128)(2,1)}, bf16[2048,32]{0,1:T(8,128)(2,1)}) async-done(((bf16[2048,1024]{1,0:T(8,128)(2,1)}, bf16[2048,128]{1,0:T(8,128)(2,1)}, bf16[2048,128]{1,0:T(8,128)(2,1)}, bf16[1024,2048]{1,0:T(8,128)(2,1)}, bf16[2048,32]{0,1:T(8,128)(2,1)}), ...) | async-done | bytes 9568272 | tf_op jit(solution)/shard_map/psum | solution.py:357
  (484 shorter events, 387.9 us)
Async XLA Ops:
  7.2 223.7 %all-reduce.13.cloned.1.call-start = ((), (), s32[]{:S(2)}) async-start(), calls=%async_computation.6 | async-start | bytes 4194304 | tf_op jit(solution)/shard_map/psum | solution.py:178
  13.2 155.7 %collective-permute-start.11 = (bf16[512,1,128]{2,0,1:T(8,128)(2,1)}, bf16[512,1,128]{2,0,1:T(8,128)(2,1)}, u32[]{:S(2)}, u32[]{:S(2)}) collective-permute-start(bf16[512,1,128]{2,0,1:T(8,128)(2,1)} %bitcast.23), channel_id=1, source_target_pairs={{4,0},{8,4},{12,8},{16,12},{20,16},{24,20},{28,24},{5,1},{9,5},{13... | collective-permute-start | bytes 393224 | tf_op jit(solution)/shard_map/ppermute | solution.py:17
  14.6 154.3 %collective-permute-start.10 = (bf16[512,1,128]{2,0,1:T(8,128)(2,1)}, bf16[512,1,128]{2,0,1:T(8,128)(2,1)}, u32[]{:S(2)}, u32[]{:S(2)}) collective-permute-start(bf16[512,1,128]{2,0,1:T(8,128)(2,1)} %bitcast.23), channel_id=1, source_target_pairs={{0,12},{4,16},{8,20},{12,24},{16,28},{1,13},{5,17},{9,21},{13,25},... | collective-permute-start | bytes 393224 | tf_op jit(solution)/shard_map/ppermute | solution.py:17
  22.3 143.0 %collective-permute-start.9 = (bf16[512,1,128]{2,0,1:T(8,128)(2,1)}, bf16[512,1,128]{2,0,1:T(8,128)(2,1)}, u32[]{:S(2)}, u32[]{:S(2)}) collective-permute-start(bf16[512,1,128]{2,0,1:T(8,128)(2,1)} %bitcast.23), channel_id=1, source_target_pairs={{8,0},{12,4},{16,8},{20,12},{24,16},{28,20},{9,1},{13,5},{17,9},{2... | collective-permute-start | bytes 393224 | tf_op jit(solution)/shard_map/ppermute | solution.py:17
  33.2 66.7 %collective-permute-start.5 = (bf16[512,1,128]{2,0,1:T(8,128)(2,1)}, bf16[512,1,128]{2,0,1:T(8,128)(2,1)}, u32[]{:S(2)}, u32[]{:S(2)}) collective-permute-start(bf16[512,1,128]{2,0,1:T(8,128)(2,1)} %pad_maximum_fusion.1), channel_id=1, source_target_pairs={{4,0},{8,4},{12,8},{16,12},{20,16},{24,20},{28,24},{5,1},{9,5},{13... | collective-permute-start | bytes 393224 | tf_op jit(solution)/shard_map/ppermute | solution.py:17
  34.4 66.7 %collective-permute-start.4 = (bf16[512,1,128]{2,0,1:T(8,128)(2,1)}, bf16[512,1,128]{2,0,1:T(8,128)(2,1)}, u32[]{:S(2)}, u32[]{:S(2)}) collective-permute-start(bf16[512,1,128]{2,0,1:T(8,128)(2,1)} %pad_maximum_fusion.1), channel_id=1, source_target_pairs={{0,12},{4,16},{8,20},{12,24},{16,28},{1,13},{5,17},{9,21},{13,25},... | collective-permute-start | bytes 393224 | tf_op jit(solution)/shard_map/ppermute | solution.py:17
  101.1 8.9 collective-permute-start.2
  108.7 11.1 collective-permute-start.1
  110.0 11.1 collective-permute-start
  119.9 36.2 %collective-permute-start.7 = (bf16[512,1,128]{2,0,1:T(8,128)(2,1)}, bf16[512,1,128]{2,0,1:T(8,128)(2,1)S(1)}, u32[]{:S(2)}, u32[]{:S(2)}) collective-permute-start(bf16[512,1,128]{2,0,1:T(8,128)(2,1)} %bitcast.23), channel_id=1, source_target_pairs={{12,0},{16,4},{20,8},{24,12},{28,16},{13,1},{17,5},{21,9},{25,13},... | collective-permute-start | bytes 393224 | tf_op jit(solution)/shard_map/ppermute | solution.py:17
  121.2 41.1 %collective-permute-start.6 = (bf16[512,1,128]{2,0,1:T(8,128)(2,1)}, bf16[512,1,128]{2,0,1:T(8,128)(2,1)S(1)}, u32[]{:S(2)}, u32[]{:S(2)}) collective-permute-start(bf16[512,1,128]{2,0,1:T(8,128)(2,1)} %bitcast.23), channel_id=1, source_target_pairs={{0,4},{4,8},{8,12},{12,16},{16,20},{20,24},{24,28},{1,5},{5,9},{9,... | collective-permute-start | bytes 393224 | tf_op jit(solution)/shard_map/ppermute | solution.py:17
  156.1 9.2 collective-permute-start.8
  286.9 549.3 %all-to-all-start = ((bf16[8,4,192,2048]{3,2,1,0:T(8,128)(2,1)}), bf16[8,4,192,2048]{3,2,1,0:T(8,128)(2,1)}, u32[]{:S(2)}, u32[]{:S(2)}) async-start(bf16[8,4,192,2048]{3,2,1,0:T(8,128)(2,1)} %bitcast.528), calls=%async_computation | async-start | bytes 50331648 | tf_op jit(solution)/shard_map/all_to_all | solution.py:56
  836.2 548.5 %all-to-all-start.2 = ((bf16[8,4,192,2048]{3,2,1,0:T(8,128)(2,1)}), bf16[8,4,192,2048]{3,2,1,0:T(8,128)(2,1)}, u32[]{:S(2)}, u32[]{:S(2)}) async-start(bf16[8,4,192,2048]{3,2,1,0:T(8,128)(2,1)} %multiply_convert_fusion), calls=%async_computation.3 | async-start | bytes 50331648 | tf_op jit(solution)/shard_map/all_to_all | solution.py:56
  842.7 754.5 %reduce-scatter.3.cloned.1.call-start = ((), (), s32[]{:S(2)}) async-start(), calls=%async_computation.7 | async-start | bytes 31457280 | tf_op jit(solution)/shard_map/reduce_scatter | solution.py:64
  1418.1 362.1 %reduce-scatter.5.cloned.1.call-start = ((), (), s32[]{:S(2)}) async-start(), calls=%async_computation.8 | async-start | bytes 31457280 | tf_op jit(solution)/shard_map/reduce_scatter | solution.py:64
  1603.3 183.1 %all-to-all-start.1 = ((bf16[8,4,192,512]{3,2,1,0:T(8,128)(2,1)}), bf16[8,4,192,512]{3,2,1,0:T(8,128)(2,1)}, u32[]{:S(2)}, u32[]{:S(2)}) async-start(bf16[8,4,192,512]{3,2,1,0:T(8,128)(2,1)} %copy.475), calls=%async_computation.2 | async-start | bytes 12582912 | tf_op jit(solution)/shard_map/all_to_all | solution.py:60
  1786.4 143.8 %all-to-all-start.3 = ((bf16[8,4,192,512]{3,2,1,0:T(8,128)(2,1)}), bf16[8,4,192,512]{3,2,1,0:T(8,128)(2,1)}, u32[]{:S(2)}, u32[]{:S(2)}) async-start(bf16[8,4,192,512]{3,2,1,0:T(8,128)(2,1)} %copy.478), calls=%async_computation.5 | async-start | bytes 12582912 | tf_op jit(solution)/shard_map/all_to_all | solution.py:60
  1791.9 201.4 %all-gather.2.cloned.1.call-start = ((), (), s32[]{:S(2)}) async-start(), calls=%async_computation.9 | async-start | bytes 2621440 | tf_op jit(solution)/shard_map/all_gather | solution.py:269
  1958.1 228.4 %all-reduce.15.cloned.1.call-start = ((), (), s32[]{:S(2)}) async-start(), calls=%async_computation.10 | async-start | bytes 4194304 | tf_op jit(solution)/shard_map/psum | solution.py:340
  2029.6 60.9 %collective-permute-start.16 = (bf16[512,1,128]{2,0,1:T(8,128)(2,1)}, bf16[512,1,128]{2,0,1:T(8,128)(2,1)S(1)}, u32[]{:S(2)}, u32[]{:S(2)}) collective-permute-start(bf16[512,1,128]{2,0,1:T(8,128)(2,1)} %get-tuple-element.58), channel_id=1, source_target_pairs={{12,0},{16,4},{20,8},{24,12},{28,16},{13,1},{17,5},{21,9},{25,13},... | collective-permute-start | bytes 393224 | tf_op jit(solution)/shard_map/ppermute | solution.py:17
  2030.9 66.9 %collective-permute-start.17 = (bf16[512,1,128]{2,0,1:T(8,128)(2,1)}, bf16[512,1,128]{2,0,1:T(8,128)(2,1)S(1)}, u32[]{:S(2)}, u32[]{:S(2)}) collective-permute-start(bf16[512,1,128]{2,0,1:T(8,128)(2,1)} %get-tuple-element.59), channel_id=1, source_target_pairs={{0,4},{4,8},{8,12},{12,16},{16,20},{20,24},{24,28},{1,5},{5,9},{9,... | collective-permute-start | bytes 393224 | tf_op jit(solution)/shard_map/ppermute | solution.py:17
  2044.8 54.5 %collective-permute-start.14 = (bf16[512,1,128]{2,0,1:T(8,128)(2,1)}, bf16[512,1,128]{2,0,1:T(8,128)(2,1)S(1)}, u32[]{:S(2)}, u32[]{:S(2)}) collective-permute-start(bf16[512,1,128]{2,0,1:T(8,128)(2,1)} %get-tuple-element.56), channel_id=1, source_target_pairs={{8,0},{12,4},{16,8},{20,12},{24,16},{28,20},{9,1},{13,5},{17,9},{2... | collective-permute-start | bytes 393224 | tf_op jit(solution)/shard_map/ppermute | solution.py:17
  2046.1 58.7 %collective-permute-start.15 = (bf16[512,1,128]{2,0,1:T(8,128)(2,1)}, bf16[512,1,128]{2,0,1:T(8,128)(2,1)}, u32[]{:S(2)}, u32[]{:S(2)}) collective-permute-start(bf16[512,1,128]{2,0,1:T(8,128)(2,1)} %get-tuple-element.57), channel_id=1, source_target_pairs={{0,8},{4,12},{8,16},{12,20},{16,24},{20,28},{1,9},{5,13},{9,17},{1... | collective-permute-start | bytes 393224 | tf_op jit(solution)/shard_map/ppermute | solution.py:17
  2056.7 49.4 %collective-permute-start.12 = (bf16[512,1,128]{2,0,1:T(8,128)(2,1)}, bf16[512,1,128]{2,0,1:T(8,128)(2,1)}, u32[]{:S(2)}, u32[]{:S(2)}) collective-permute-start(bf16[512,1,128]{2,0,1:T(8,128)(2,1)} %get-tuple-element.54), channel_id=1, source_target_pairs={{4,0},{8,4},{12,8},{16,12},{20,16},{24,20},{28,24},{5,1},{9,5},{13... | collective-permute-start | bytes 393224 | tf_op jit(solution)/shard_map/ppermute | solution.py:17
  2090.4 20.2 collective-permute-start.13
  2097.8 18.4 collective-permute-start.18
  2099.3 21.9 collective-permute-start.19
  2104.8 16.5 collective-permute-start.20
  2106.1 15.2 collective-permute-start.21
  2110.7 10.6 collective-permute-start.22
  2126.7 366.0 %all-reduce.17.cloned.1.call-start = ((), (), s32[]{:S(2)}) async-start(), calls=%async_computation.11 | async-start | bytes 19136512 | tf_op jit(solution)/shard_map/psum | solution.py:357
  (140 other events, 3006.6 us)
Sparse Core Ops, SparseCore 0:
  177.6 53.2 all-reduce.12
  1418.2 178.9 reduce-scatter.2
  1599.8 180.4 reduce-scatter.4
  1958.2 20.7 all-gather.1
  2126.8 53.4 all-reduce.14
  2186.2 306.4 all-reduce.16
where the time goes:
time: 2530 us; the launch traced here: 2520 us
  waiting for transfers between devices  1620 us (64%)
  matrix products  293 us (12%)
  local copies, waits for them, and re-layouts  276 us (11%)
  other arithmetic  163 us (6%)
  starting transfers between devices  105 us (4%)
  blocking collectives  39.9 us (2%)
    all_to_all x2, waiting for transfers between devices, to_owners(): lax.all_to_all(row_block, 'ep', split_axis=0, concat_axis=0, tiled=True)  938 us
    reduce_scatter x2, waiting for transfers between devices, owner_sum(): lax.psum_scatter(values.astype(jnp.bfloat16), 'tp', scatter_dimension=3,...  288 us
    psum x1, waiting for transfers between devices, body(): lax.psum(q_weight_grad.astype(jnp.bfloat16), 'ep').astype(jnp.float32)  269 us
    all_to_all x2, waiting for transfers between devices, from_owners(): lax.all_to_all(row_block, 'ep', split_axis=0, concat_axis=0, tiled=True)  91.4 us
    ppermute x24, starting transfers between devices, shifted(): return lax.ppermute(block, axis, route)  80.1 us
  transfers between devices with their start and end apart: 34, of which 8 were waited for; matrix products, arithmetic and copies ran while one was open for 21% of the time, Pallas kernels for 0%

commit v1 on v0

--- a/solution.py
+++ b/solution.py
@@ -1,6 +1,8 @@
 import jax
 import jax.numpy as jnp
 from jax import lax
+from jax.experimental import pallas as pl
+from jax.experimental.pallas import tpu as pltpu
 from jax.sharding import PartitionSpec as P
 
 SPAN = 4
@@ -52,18 +54,93 @@
     )
 
 
-def to_owners(row_block):
-    return lax.all_to_all(row_block, "ep", split_axis=0, concat_axis=0, tiled=True)
-
-
-def from_owners(row_block):
-    return lax.all_to_all(row_block, "ep", split_axis=0, concat_axis=0, tiled=True)
-
-
-def owner_sum(values):
-    return lax.psum_scatter(
-        values.astype(jnp.bfloat16), "tp", scatter_dimension=3, tiled=True
-    ).astype(jnp.float32)
+NT_DIMS = (((1,), (1,)), ((), ()))
+
+
+def expert_kernel(
+    rows_ref,
+    cotangent_ref,
+    chosen_ref,
+    router_ref,
+    router_t_ref,
+    select_ref,
+    gate_ref,
+    up_ref,
+    down_ref,
+    out_ref,
+    grad_ref,
+    hidden_ref,
+    d_gate_ref,
+    d_up_ref,
+    dlog_ref,
+):
+    f32 = jnp.float32
+    low = jnp.bfloat16
+    rows = rows_ref[...]
+    logits = jnp.dot(rows, router_ref[...], preferred_element_type=f32)
+    logits = jnp.where(chosen_ref[...] > 0.5, logits, MASKED)
+    probs = jnp.exp(logits - jnp.max(logits, axis=-1, keepdims=True))
+    probs = probs / jnp.sum(probs, axis=-1, keepdims=True)
+    select = select_ref[...]
+    probs_high = probs.astype(low)
+    probs_rest = (probs - probs_high.astype(f32)).astype(low)
+    weight = jnp.dot(probs_high, select, preferred_element_type=f32)
+    weight += jnp.dot(probs_rest, select, preferred_element_type=f32)
+    gate = jnp.dot(rows, gate_ref[...], preferred_element_type=f32)
+    up = jnp.dot(rows, up_ref[...], preferred_element_type=f32)
+    d_hidden = (
+        lax.dot_general(cotangent_ref[...], down_ref[...], NT_DIMS, preferred_element_type=f32)
+        * weight
+    )
+    sig = 1.0 / (1.0 + jnp.exp(-gate))
+    silu = gate * sig
+    hidden = silu * up
+    d_up = (d_hidden * silu).astype(low)
+    d_gate = (d_hidden * up * sig * (1.0 + gate * (1.0 - sig))).astype(low)
+    hidden_low = (hidden * weight).astype(low)
+    dots = lax.dot_general(
+        (d_hidden * hidden).astype(low), select, NT_DIMS, preferred_element_type=f32
+    )
+    dlog = (dots - probs * jnp.sum(dots, axis=-1, keepdims=True)).astype(low)
+    hidden_ref[...] = hidden_low
+    d_gate_ref[...] = d_gate
+    d_up_ref[...] = d_up
+    dlog_ref[...] = dlog
+    out_ref[...] = jnp.dot(hidden_low, down_ref[...], preferred_element_type=f32).astype(low)
+    grads = lax.dot_general(d_gate, gate_ref[...], NT_DIMS, preferred_element_type=f32)
+    grads += lax.dot_general(d_up, up_ref[...], NT_DIMS, preferred_element_type=f32)
+    grads += jnp.dot(dlog, router_t_ref[...], preferred_element_type=f32)
+    grad_ref[...] = grads.astype(low)
+
+
+def expert_pass(rows, cotangents, chosen, router, select, gate, up, down):
+    count, model_width = rows.shape
+    experts_all = router.shape[1]
+    width = down.shape[0]
+    tile = 512
+
+    def tiled(columns):
+        return pl.BlockSpec((tile, columns), lambda i: (i, 0))
+
+    def whole(array):
+        return pl.BlockSpec(array.shape, lambda i: (0, 0), pipeline_mode=pl.Buffered(1))
+
+    fixed = (router, router.T, select, gate, up, down)
+    columns = (model_width, model_width, width, width, width, experts_all)
+    return pl.pallas_call(
+        expert_kernel,
+        grid=(count // tile,),
+        in_specs=[tiled(model_width), tiled(model_width), tiled(experts_all)]
+        + [whole(array) for array in fixed],
+        out_specs=[tiled(size) for size in columns],
+        out_shape=[jax.ShapeDtypeStruct((count, size), jnp.bfloat16) for size in columns],
+        compiler_params=pltpu.CompilerParams(vmem_limit_bytes=60 * 1024 * 1024),
+        cost_estimate=pl.CostEstimate(
+            flops=12 * count * model_width * width,
+            bytes_accessed=8 * count * model_width,
+            transcendentals=count * width,
+        ),
+    )(rows, cotangents, chosen, *fixed)
 
 
 def body(
@@ -85,7 +162,6 @@
     out_grad,
 ):
     tokens = block_in.shape[0]
-    model_width = block_in.shape[1]
     head_width = q_gain.shape[0]
     kv_heads = k_weight.shape[1] // head_width
     group_size = q_weight.shape[1] // head_width // kv_heads
@@ -93,7 +169,7 @@
     tp_rank = lax.axis_index("tp")
     ep_count = lax.axis_size("ep")
     ep_rank = lax.axis_index("ep")
-    share_width = model_width // tp_count
+    share_rows = tokens // tp_count
     seq_span = SPAN
     dev_slot = ep_rank % seq_span
     block_pos = (dev_slot + seq_span - 1) % seq_span
@@ -102,12 +178,20 @@
     positions = block_pos * tokens + row_index
     score_scale = head_width ** (-0.5)
 
-    def column_share(full_rows):
-        return lax.dynamic_slice_in_dim(full_rows, tp_rank * share_width, share_width, 1)
-
+    def my_rows(full_rows):
+        return lax.dynamic_slice_in_dim(full_rows, tp_rank * share_rows, share_rows, 0)
+
+    def sum_rows(partial_rows):
+        parts = lax.all_to_all(
+            partial_rows.astype(jnp.bfloat16), "tp", split_axis=0, concat_axis=0, tiled=True
+        )
+        return jnp.sum(
+            parts.reshape(tp_count, share_rows, -1).astype(jnp.float32), axis=0
+        )
+
+    dy_all = lax.all_gather(my_rows(out_grad), ("ep", "tp"), axis=0, tiled=True)
     x_full = block_in.astype(jnp.float32)
-    attn_in, input_norm_back = jax.vjp(rms_scale, x_full, input_norm)
-    attn_low = attn_in.astype(jnp.bfloat16)
+    attn_low = rms_scale(x_full, input_norm).astype(jnp.bfloat16)
     q_lin = jnp.dot(attn_low, q_weight, preferred_element_type=jnp.float32).reshape(
         tokens, kv_heads, group_size, head_width
     )
@@ -175,104 +259,44 @@
         )
     o_low = attn_acc.reshape(tokens, -1).astype(jnp.bfloat16)
     head_part = jnp.dot(o_low, o_weight, preferred_element_type=jnp.float32)
-    x_mid = x_full + lax.psum(head_part.astype(jnp.bfloat16), "tp").astype(jnp.float32)
+    x_mid = my_rows(x_full) + sum_rows(head_part)
     ffn_in, post_norm_back = jax.vjp(rms_scale, x_mid, post_norm)
-    ffn_low = ffn_in.astype(jnp.bfloat16)
-    logits = jnp.dot(ffn_low, router, preferred_element_type=jnp.float32)
+    ffn_all = lax.all_gather(ffn_in.astype(jnp.bfloat16), ("ep", "tp"), axis=0, tiled=True)
     experts_all = router.shape[1]
-    top_count = expert_ids.shape[1]
-    chosen = expert_ids[:, :, None] == jnp.arange(experts_all, dtype=jnp.int32)[None, None, :]
-
-    def route_gates(logit_rows):
-        picked = jnp.sum(jnp.where(chosen, logit_rows[:, None, :], 0.0), axis=-1)
-        return jax.nn.softmax(picked, axis=-1)
-
-    gate_probs, gates_back = jax.vjp(route_gates, logits)
     local_experts = expert_gate.shape[0]
-    capacity = 3 * tokens * top_count // (2 * experts_all)
-    assigned = tokens * top_count
-    flat_ids = expert_ids.reshape(-1)
-    expert_hits = (flat_ids[:, None] == jnp.arange(experts_all, dtype=jnp.int32)[None, :]).astype(
-        jnp.int32
-    )
-    slot_ranks = jnp.sum(expert_hits * (jnp.cumsum(expert_hits, axis=0) - 1), axis=1)
-    slot_index = flat_ids * capacity + slot_ranks
-    owners = (
-        jnp.full((experts_all * capacity,), assigned, jnp.int32)
-        .at[slot_index]
-        .set(jnp.arange(assigned, dtype=jnp.int32))
-    )
-    slot_tokens = owners // top_count
-    slot_gates = jnp.concatenate([gate_probs.reshape(-1), jnp.zeros((1,), jnp.float32)])[owners]
-    padded_rows = jnp.concatenate([ffn_low, jnp.zeros((1, model_width), jnp.bfloat16)], axis=0)
-    send_forward = padded_rows[slot_tokens].reshape(ep_count, local_experts, capacity, -1)
-    arrived = to_owners(send_forward)
-    gate_pre = jnp.einsum(
-        "secd,edf->secf", arrived, expert_gate, preferred_element_type=jnp.float32
-    )
-    up_pre = jnp.einsum("secd,edf->secf", arrived, expert_up, preferred_element_type=jnp.float32)
-    gate_sig = jax.nn.sigmoid(gate_pre)
-    silu_vals = gate_pre * gate_sig
-    hidden_low = (silu_vals * up_pre).astype(jnp.bfloat16)
-    expert_out = jnp.einsum(
-        "secf,efd->secd", hidden_low, expert_down, preferred_element_type=jnp.float32
-    )
-    out_low = owner_sum(expert_out).astype(jnp.bfloat16)
-    returned = from_owners(out_low).reshape(experts_all * capacity, share_width)
-    mixed_rows = returned[slot_index].reshape(tokens, top_count, share_width).astype(jnp.float32)
-    x_share = column_share(x_mid)
-    block_out = (x_share + jnp.sum(gate_probs[:, :, None] * mixed_rows, axis=1)).astype(
-        jnp.bfloat16
-    )
-    grad_full = out_grad.astype(jnp.float32)
-    grad_share = column_share(grad_full)
-    gate_dots = lax.psum(jnp.sum(grad_share[:, None, :] * mixed_rows, axis=-1), "tp")
-    (d_logits,) = gates_back(gate_dots)
-    dlog_low = d_logits.astype(jnp.bfloat16)
-    grad_rows = jnp.concatenate([grad_full, jnp.zeros((1, model_width), jnp.float32)], axis=0)
-    send_backward = (
-        (grad_rows[slot_tokens] * slot_gates[:, None])
-        .astype(jnp.bfloat16)
-        .reshape(ep_count, local_experts, capacity, -1)
-    )
-    arrived_grad = to_owners(send_backward)
-    d_hidden = jnp.einsum(
-        "secd,efd->secf", arrived_grad, expert_down, preferred_element_type=jnp.float32
-    )
+    hidden_width = expert_gate.shape[2]
+    ids_all = lax.all_gather(expert_ids, "ep", axis=0, tiled=True)
+    expert_index = jnp.arange(experts_all, dtype=jnp.int32)
+    chosen = jnp.any(ids_all[:, :, None] == expert_index[None, None, :], axis=1)
+    chosen_low = chosen.astype(jnp.bfloat16)
+    width = local_experts * hidden_width
+    own_expert = ep_rank * local_experts + jnp.arange(width, dtype=jnp.int32) // hidden_width
+    select = (expert_index[:, None] == own_expert[None, :]).astype(jnp.bfloat16)
+    gate_cat = expert_gate.transpose(1, 0, 2).reshape(-1, width)
+    up_cat = expert_up.transpose(1, 0, 2).reshape(-1, width)
+    down_cat = expert_down.reshape(width, -1)
+    expert_out, row_grads, hidden_low, d_gate_low, d_up_low, dlog_low = expert_pass(
+        ffn_all, dy_all, chosen_low, router, select, gate_cat, up_cat, down_cat
+    )
+    d_ffn = lax.psum_scatter(
+        row_grads, ("ep", "tp"), scatter_dimension=0, tiled=True
+    ).astype(jnp.float32)
+    mixed = lax.psum_scatter(
+        expert_out, ("ep", "tp"), scatter_dimension=0, tiled=True
+    ).astype(jnp.float32)
+    block_rows = (x_mid + mixed).astype(jnp.bfloat16)
+    block_out = lax.all_to_all(block_rows, "tp", split_axis=1, concat_axis=0, tiled=True)
     down_grad = jnp.einsum(
-        "secf,secd->efd", hidden_low, arrived_grad, preferred_element_type=jnp.float32
-    )
-    d_gate_low = (d_hidden * up_pre * gate_sig * (1.0 + gate_pre * (1.0 - gate_sig))).astype(
-        jnp.bfloat16
-    )
-    d_up_low = (d_hidden * silu_vals).astype(jnp.bfloat16)
-    gate_grad = jnp.einsum(
-        "secd,secf->edf", arrived, d_gate_low, preferred_element_type=jnp.float32
-    )
-    up_grad = jnp.einsum("secd,secf->edf", arrived, d_up_low, preferred_element_type=jnp.float32)
-    row_grads = jnp.einsum(
-        "secf,edf->secd", d_gate_low, expert_gate, preferred_element_type=jnp.float32
-    )
-    row_grads = row_grads + jnp.einsum(
-        "secf,edf->secd", d_up_low, expert_up, preferred_element_type=jnp.float32
-    )
-    grads_low = owner_sum(row_grads).astype(jnp.bfloat16)
-    returned_grad = from_owners(grads_low).reshape(experts_all * capacity, share_width)
-    d_ffn_share = jnp.sum(
-        returned_grad[slot_index].reshape(tokens, top_count, share_width).astype(jnp.float32),
-        axis=1,
-    )
-    router_share = lax.dynamic_slice_in_dim(router, tp_rank * share_width, share_width, 0)
-    d_ffn_share = d_ffn_share + jnp.einsum(
-        "te,qe->tq", dlog_low, router_share, preferred_element_type=jnp.float32
-    )
-    d_ffn = lax.all_gather(d_ffn_share.astype(jnp.bfloat16), "tp", axis=1, tiled=True).astype(
-        d_ffn_share.dtype
-    )
-    router_grad = jnp.einsum("td,te->de", ffn_low, dlog_low, preferred_element_type=jnp.float32)
+        "tf,td->fd", hidden_low, dy_all, preferred_element_type=jnp.float32
+    ).reshape(expert_down.shape)
+    gate_grad = jnp.einsum("td,tf->df", ffn_all, d_gate_low, preferred_element_type=jnp.float32)
+    up_grad = jnp.einsum("td,tf->df", ffn_all, d_up_low, preferred_element_type=jnp.float32)
+    gate_grad = gate_grad.reshape(-1, local_experts, hidden_width).transpose(1, 0, 2)
+    up_grad = up_grad.reshape(-1, local_experts, hidden_width).transpose(1, 0, 2)
+    router_grad = jnp.einsum("td,te->de", ffn_all, dlog_low, preferred_element_type=jnp.float32)
     d_mid_norm, post_norm_grad = post_norm_back(d_ffn)
-    d_mid = grad_full + d_mid_norm
-    d_mid_low = d_mid.astype(jnp.bfloat16)
+    d_mid = my_rows(out_grad).astype(jnp.float32) + d_mid_norm
+    d_mid_low = lax.all_gather(d_mid.astype(jnp.bfloat16), "tp", axis=0, tiled=True)
     o_weight_grad = jnp.einsum("tj,td->jd", o_low, d_mid_low, preferred_element_type=jnp.float32)
     d_attn_low = (
         jnp.einsum("td,jd->tj", d_mid_low, o_weight, preferred_element_type=jnp.float32)
@@ -336,33 +360,21 @@
     d_attn_in = d_attn_in + jnp.einsum(
         "tj,dj->td", dv_low, v_weight, preferred_element_type=jnp.float32
     )
-    d_attn_in, q_gain_grad, k_gain_grad = (
-        lax.psum(d_attn_in.astype(jnp.bfloat16), "tp").astype(jnp.float32),
-        lax.psum(q_gain_grad.astype(jnp.bfloat16), "tp").astype(jnp.float32),
-        lax.psum(k_gain_grad.astype(jnp.bfloat16), "tp").astype(jnp.float32),
-    )
-    d_in_norm, input_norm_grad = input_norm_back(d_attn_in)
-    input_grad = (d_mid + d_in_norm).astype(jnp.bfloat16)
-    (
-        q_weight_grad,
-        k_weight_grad,
-        v_weight_grad,
-        o_weight_grad,
-        router_grad,
-        input_norm_grad,
-        post_norm_grad,
-        q_gain_grad,
-        k_gain_grad,
-    ) = (
+    d_attn_rows = sum_rows(d_attn_in)
+    x_rows = my_rows(x_full)
+    _, input_norm_rows = jax.vjp(rms_scale, x_rows, input_norm)
+    d_in_norm, input_norm_grad = input_norm_rows(d_attn_rows)
+    input_grad = lax.all_gather(
+        (d_mid + d_in_norm).astype(jnp.bfloat16), "tp", axis=0, tiled=True
+    )
+    (q_weight_grad, k_weight_grad, v_weight_grad, o_weight_grad) = (
         lax.psum(q_weight_grad.astype(jnp.bfloat16), "ep").astype(jnp.float32),
         lax.psum(k_weight_grad.astype(jnp.bfloat16), "ep").astype(jnp.float32),
         lax.psum(v_weight_grad.astype(jnp.bfloat16), "ep").astype(jnp.float32),
         lax.psum(o_weight_grad.astype(jnp.bfloat16), "ep").astype(jnp.float32),
-        lax.psum(router_grad.astype(jnp.bfloat16), "ep").astype(jnp.float32),
-        lax.psum(input_norm_grad.astype(jnp.bfloat16), "ep").astype(jnp.float32),
-        lax.psum(post_norm_grad.astype(jnp.bfloat16), "ep").astype(jnp.float32),
-        lax.psum(q_gain_grad.astype(jnp.bfloat16), "ep").astype(jnp.float32),
-        lax.psum(k_gain_grad.astype(jnp.bfloat16), "ep").astype(jnp.float32),
+    )
+    (router_grad, input_norm_grad, post_norm_grad, q_gain_grad, k_gain_grad) = lax.psum(
+        (router_grad, input_norm_grad, post_norm_grad, q_gain_grad, k_gain_grad), ("ep", "tp")
     )
     return (
         block_out,

time: 2530 us -> 1290 us (0.51)
  waiting for transfers between devices: 1620 us -> 666 us
  local copies, waits for them, and re-layouts: 276 us -> 62.7 us
  matrix products: 293 us -> 173 us
  Pallas kernels: 0 us -> 115 us
  other arithmetic: 163 us -> 79.4 us
  blocking collectives: 39.9 us -> 81.8 us
    all_to_all x4 -> x3, waiting for transfers between devices: 1030 us -> 71.8 us  [the longest x2 71.8 us: sum_rows(): lax.all_to_all(partial_rows.astype(jnp.bfloat16), 'tp', split_axis=0, con...]
    gather x5 -> x0, local copies, waits for them, and re-layouts: 174 us -> none  [the longest x1 49 us: body(): grad_rows[slot_tokens] * slot_gates[:, None]]
    pallas_call x0 -> x1, Pallas kernels: none -> 115 us  [expert_pass(): pl.pallas_call(expert_kernel, grid=(count // tile,), in_specs=[tiled(mode...]
    dot_general x12 -> x4, matrix products: 175 us -> 70.9 us  [the longest x1 20.6 us: body(): jnp.einsum('td,tf->df', ffn_all, d_up_low, preferred_element_type=jnp.flo...]
    reduce_scatter x2, waiting for transfers between devices: 288 us -> 200 us  [the longest x1 181 us: body(): lax.psum_scatter(row_grads, ('ep', 'tp'), scatter_dimension=0, tiled=True)]
    psum x2 -> x1, waiting for transfers between devices: 36.6 us -> 117 us  [body(): lax.psum((router_grad, input_norm_grad, post_norm_grad, q_gain_grad, k_ga...]
    psum x1, waiting for transfers between devices: 269 us -> 191 us  [body(): lax.psum(q_weight_grad.astype(jnp.bfloat16), 'ep').astype(jnp.float32)]
    all_gather x1 -> x4, waiting for transfers between devices: 0.01 us -> 74.5 us  [the longest x1 74.5 us: body(): lax.all_gather(ffn_in.astype(jnp.bfloat16), ('ep', 'tp'), axis=0, tiled=T...]
  transfers between devices with their start and end apart: 34 -> 35, of which waited for: 8 -> 9; matrix products, arithmetic and copies ran while one was open for 21% -> 23% of each run, Pallas kernels for 0% -> 0%
where the time goes in v1:
time: 1290 us
  waiting for transfers between devices  666 us (52%)
  matrix products  173 us (13%)
  Pallas kernels  115 us (9%)
  starting transfers between devices  94.7 us (7%)
  blocking collectives  81.8 us (6%)
  other arithmetic  79.4 us (6%)
  local copies, waits for them, and re-layouts  62.7 us (5%)
  between operations  16.5 us (1%)
    psum x1, waiting for transfers between devices, body(): lax.psum(q_weight_grad.astype(jnp.bfloat16), 'ep').astype(jnp.float32)  191 us
    reduce_scatter x1, waiting for transfers between devices, body(): lax.psum_scatter(row_grads, ('ep', 'tp'), scatter_dimension=0, tiled=True)  181 us
    psum x1, waiting for transfers between devices, body(): lax.psum((router_grad, input_norm_grad, post_norm_grad, q_gain_grad, k_ga...  117 us
    pallas_call x1, Pallas kernels, expert_pass(): pl.pallas_call(expert_kernel, grid=(count // tile,), in_specs=[tiled(mode...  115 us
    ppermute x24, starting transfers between devices, shifted(): return lax.ppermute(block, axis, route)  80.8 us
    all_gather x1, waiting for transfers between devices, body(): lax.all_gather(ffn_in.astype(jnp.bfloat16), ('ep', 'tp'), axis=0, tiled=T...  74.5 us
    all_to_all x2, waiting for transfers between devices, sum_rows(): lax.all_to_all(partial_rows.astype(jnp.bfloat16), 'tp', split_axis=0, con...  71.8 us
    psum x1, blocking collectives, body(): lax.psum((router_grad, input_norm_grad, post_norm_grad, q_gain_grad, k_ga...  49.4 us
  transfers between devices with their start and end apart: 35, of which 9 were waited for; matrix products, arithmetic and copies ran while one was open for 23% of the time, Pallas kernels for 0%

profile of v1, /device:TPU:0, one launch (start us, length us, event | category | flops | bytes accessed | tf_op | source)
XLA Modules:
  0.0 1288.9 jit_solution(1126095220898188928)
XLA Ops:
  16.9 5.5 collective-permute-start
  28.5 8.0 collective-permute-start.4
  56.3 5.5 collective-permute-start.8
  72.6 6.9 collective-permute-start.10
  87.9 6.6 exponential_reduce_fusion
  94.9 13.0 %fusion.16 = (bf16[8,512,512]{1,2,0:T(8,128)(2,1)}, bf16[8,512,512]{1,2,0:T(8,128)(2,1)}, bf16[8,512,512]{1,2,0:T(8,128)(2,1)}, bf16[8,512,512]{1,2,0:T(8,128)(2,1)}) fusion(f32[512,512,8]{1,0,2:T(8,128)} %get-tuple-element.80, f32[8,512]{1,0:T(8,128)S(1)} %add_select_fusion, pred[512,512]{0,1:T(8,128)(4,1)S(1)} %get-tuple-element.75, ...), kind=kLoop, calls=%fused_computation.32 | loop fusion | flops 41943040 | bytes 51396608 | tf_op jit(solution)/shard_map/reshape.86
  132.4 23.2 %all-to-all-done = bf16[4,128,2048]{2,1,0:T(8,128)(2,1)} async-done(((bf16[4,128,2048]{2,1,0:T(8,128)(2,1)}), bf16[4,128,2048]{2,1,0:T(8,128)(2,1)}, u32[]{:S(2)}, u32[]{:S(2)}) %all-to-all-start) | async-done | bytes 2097184 | tf_op jit(solution)/shard_map/all_to_all | solution.py:185
  170.2 32.5 %all_gather.17 = s32[4096,8]{0,1:T(8,128)S(1)} all-gather(s32[512,8]{0,1:T(8,128)S(1)} %copy-done.76), channel_id=1, replica_groups=mesh['ep'=8,'tp'=4] {'ep'}, dimensions={0}, use_global_device_ids=true | all-gather | bytes 147456 | tf_op jit(solution)/shard_map/all_gather | solution.py:268
  206.3 74.5 %all-gather.5.cloned.1.call-done.rows_ref = bf16[4096,2048]{1,0:T(8,128)(2,1)} async-done(((bf16[128,2048]{1,0:T(8,128)(2,1)}), bf16[4096,2048]{1,0:T(8,128)(2,1)}) %all-gather.5.cloned.1.call-update) | async-done | bytes 16777232 | tf_op jit(solution)/shard_map/all_gather | solution.py:264
  280.8 114.8 %shard_map.263 = (bf16[4096,2048]{1,0:T(8,128)(2,1)}, bf16[4096,2048]{1,0:T(8,128)(2,1)}, bf16[4096,768]{1,0:T(8,128)(2,1)}, bf16[4096,768]{1,0:T(8,128)(2,1)}, ...) custom-call(bf16[4096,2048]{1,0:T(8,128)(2,1)} %all-gather.5.cloned.1.call-done.rows_ref, ...), custom_call_target="tpu_custom_call" | custom-call | flops 77309411328 | bytes 67108864 | tf_op jit(solution)/shard_map/pallas_call | solution.py:130
  396.1 180.7 %reduce-scatter.5.cloned.1.call-done = bf16[128,2048]{1,0:T(8,128)(2,1)} async-done(((bf16[4096,2048]{1,0:T(8,128)(2,1)}), bf16[128,2048]{1,0:T(8,128)(2,1)}) %reduce-scatter.5.cloned.1.call-update) | async-done | bytes 524304 | tf_op jit(solution)/shard_map/reduce_scatter | solution.py:281
  582.4 8.1 copy.399
  590.4 8.1 copy.402
  598.5 8.0 copy.405
  606.6 8.1 copy.397
  614.6 5.2 convolution_convert_fusion.5
  626.2 6.0 fusion.23
  645.3 8.4 collective-permute-start.13
  703.1 6.6 collective-permute-start.19
  720.1 5.2 collective-permute-start.23
  726.1 8.1 collective-permute-done.23
  742.3 48.6 %all-to-all-done.2 = bf16[4,128,2048]{2,1,0:T(8,128)(2,1)} async-done(((bf16[4,128,2048]{2,1,0:T(8,128)(2,1)}), bf16[4,128,2048]{2,1,0:T(8,128)(2,1)}, u32[]{:S(2)}, u32[]{:S(2)}) %all-to-all-start.2) | async-done | bytes 2097184 | tf_op jit(solution)/shard_map/all_to_all | solution.py:185
  794.5 19.2 %reduce-scatter.3.cloned.1.call-done = bf16[128,2048]{1,0:T(8,128)(2,1)} async-done(((bf16[4096,2048]{1,0:T(8,128)(2,1)}), bf16[128,2048]{1,0:T(8,128)(2,1)}) %reduce-scatter.3.cloned.1.call-update) | async-done | bytes 524304 | tf_op jit(solution)/shard_map/reduce_scatter | solution.py:284
  816.8 6.4 convolution_convert_fusion
  832.7 9.5 fusion.126
  842.2 20.3 %fusion.127 = f32[2048,768]{0,1:T(8,128)} fusion(bf16[4096,2048]{1,0:T(8,128)(2,1)} %all-gather.5.cloned.1.call-done.rows_ref, bf16[4096,768]{1,0:T(8,128)(2,1)} %get-tuple-element.23), kind=kOutput, calls=%fused_computation.261 | convolution fusion | flops 12884901888 | bytes 29360128 | tf_op jit(solution)/shard_map/td,tf->df/dot_general | solution.py:292
  862.5 20.6 %fusion.128 = f32[2048,768]{0,1:T(8,128)} fusion(bf16[4096,2048]{1,0:T(8,128)(2,1)} %all-gather.5.cloned.1.call-done.rows_ref, bf16[4096,768]{1,0:T(8,128)(2,1)} %get-tuple-element.24), kind=kOutput, calls=%fused_computation.262 | convolution fusion | flops 12884901888 | bytes 29360128 | tf_op jit(solution)/shard_map/td,tf->df/dot_general | solution.py:293
  887.7 20.5 %fusion.129 = f32[768,2048]{1,0:T(8,128)} fusion(bf16[4096,768]{1,0:T(8,128)(2,1)} %get-tuple-element.25, bf16[4096,2048]{1,0:T(8,128)(2,1)} %all-gather.7.cloned.1.call-done.cotangent_ref), kind=kOutput, calls=%fused_computation.263 | convolution fusion | flops 12884901888 | bytes 29360128 | tf_op jit(solution)/shard_map/tf,td->fd/dot_general | solution.py:289
  908.2 49.4 %all-reduce.4 = (f32[2048]{0:T(1024)}, f32[128]{0:T(128)}, f32[128]{0:T(128)}, f32[2048]{0:T(1024)}) all-reduce(f32[2048]{0:T(1024)S(1)} %get-tuple-element.28, f32[128]{0:T(128)S(1)} %copy-done.90, f32[128]{0:T(128)S(1)} %get-tuple-element.32, f32[2048]{0:T(1024)S(1)} %copy-done.75), channel_id=1, replica_groups=mesh['ep'=8,'tp'=4] {'ep','tp'}, use_global_device_ids=true, to_apply=%region_24.25 | all-reduce | flops 4352 | bytes 34816 | tf_op jit(solution)/shard_map/psum | solution.py:376
  957.5 191.5 %all-reduce.11.cloned.1.call-done = (bf16[2048,1024]{1,0:T(8,128)(2,1)}, bf16[2048,128]{1,0:T(8,128)(2,1)}, bf16[2048,128]{1,0:T(8,128)(2,1)}, bf16[1024,2048]{1,0:T(8,128)(2,1)}) async-done(((bf16[2048,1024]{1,0:T(8,128)(2,1)}, bf16[2048,128]{1,0:T(8,128)(2,1)}, bf16[2048,128]{1,0:T(8,128)(2,1)}, bf16[1024,2048]{1,0:T(8,128)(2,1)}), (bf16[2048,1024]{1,0:T(8,128)(2,1)}, bf16[2048,128]{1,0:T(8,128)(2,1)}, ...) | async-done | bytes 9437200 | tf_op jit(solution)/shard_map/psum | solution.py:371
  1149.0 6.8 convert_element_type.403
  1162.3 116.7 %all-reduce.9.cloned.1.call-done = f32[2048,32]{0,1:T(8,128)} async-done(((f32[2048,32]{0,1:T(8,128)}), f32[2048,32]{0,1:T(8,128)}) %all-reduce.9.cloned.1.call-update) | async-done | bytes 262160 | tf_op jit(solution)/shard_map/psum | solution.py:376
  (380 shorter events, 220.1 us)
Async XLA Ops:
  7.2 199.1 %all-gather.7.cloned.1.call-start = ((), (), s32[]{:S(2)}) async-start(), calls=%async_computation.6 | async-start | bytes 17301504 | tf_op jit(solution)/shard_map/all_gather | solution.py:192
  16.9 38.0 %collective-permute-start = (bf16[512,1,128]{2,0,1:T(8,128)(2,1)}, bf16[512,1,128]{2,0,1:T(8,128)(2,1)}, u32[]{:S(2)}, u32[]{:S(2)}) collective-permute-start(bf16[512,1,128]{2,0,1:T(8,128)(2,1)} %pad_maximum_fusion.1), channel_id=1, source_target_pairs={{0,4},{4,8},{8,12},{12,16},{16,20},{20,24},{24,28},{1,5},{5,9},{9,... | collective-permute-start | bytes 393224 | tf_op jit(solution)/shard_map/ppermute | solution.py:19
  22.4 33.8 %collective-permute-start.1 = (bf16[512,1,128]{2,0,1:T(8,128)(2,1)}, bf16[512,1,128]{2,0,1:T(8,128)(2,1)}, u32[]{:S(2)}, u32[]{:S(2)}) collective-permute-start(bf16[512,1,128]{2,0,1:T(8,128)(2,1)} %pad_maximum_fusion.1), channel_id=1, source_target_pairs={{12,0},{16,4},{20,8},{24,12},{28,16},{13,1},{17,5},{21,9},{25,13},... | collective-permute-start | bytes 393224 | tf_op jit(solution)/shard_map/ppermute | solution.py:19
  23.7 40.6 %collective-permute-start.2 = (bf16[512,1,128]{2,0,1:T(8,128)(2,1)}, bf16[512,1,128]{2,0,1:T(8,128)(2,1)}, u32[]{:S(2)}, u32[]{:S(2)}) collective-permute-start(bf16[512,1,128]{2,0,1:T(8,128)(2,1)} %pad_maximum_fusion.1), channel_id=1, source_target_pairs={{0,8},{4,12},{8,16},{12,20},{16,24},{20,28},{1,9},{5,13},{9,17},{1... | collective-permute-start | bytes 393224 | tf_op jit(solution)/shard_map/ppermute | solution.py:19
  27.2 38.4 %collective-permute-start.3 = (bf16[512,1,128]{2,0,1:T(8,128)(2,1)}, bf16[512,1,128]{2,0,1:T(8,128)(2,1)}, u32[]{:S(2)}, u32[]{:S(2)}) collective-permute-start(bf16[512,1,128]{2,0,1:T(8,128)(2,1)} %pad_maximum_fusion.1), channel_id=1, source_target_pairs={{8,0},{12,4},{16,8},{20,12},{24,16},{28,20},{9,1},{13,5},{17,9},{2... | collective-permute-start | bytes 393224 | tf_op jit(solution)/shard_map/ppermute | solution.py:19
  28.5 42.7 %collective-permute-start.4 = (bf16[512,1,128]{2,0,1:T(8,128)(2,1)}, bf16[512,1,128]{2,0,1:T(8,128)(2,1)}, u32[]{:S(2)}, u32[]{:S(2)}) collective-permute-start(bf16[512,1,128]{2,0,1:T(8,128)(2,1)} %pad_maximum_fusion.1), channel_id=1, source_target_pairs={{0,12},{4,16},{8,20},{12,24},{16,28},{1,13},{5,17},{9,21},{13,25},... | collective-permute-start | bytes 393224 | tf_op jit(solution)/shard_map/ppermute | solution.py:19
  54.9 17.6 %collective-permute-start.5 = (bf16[512,1,128]{2,0,1:T(8,128)(2,1)}, bf16[512,1,128]{2,0,1:T(8,128)(2,1)S(1)}, u32[]{:S(2)}, u32[]{:S(2)}) collective-permute-start(bf16[512,1,128]{2,0,1:T(8,128)(2,1)} %pad_maximum_fusion.1), channel_id=1, source_target_pairs={{4,0},{8,4},{12,8},{16,12},{20,16},{24,20},{28,24},{5,1},{9,5},{13... | collective-permute-start | bytes 393224 | tf_op jit(solution)/shard_map/ppermute | solution.py:19
  56.3 51.6 %collective-permute-start.8 = (bf16[512,1,128]{2,0,1:T(8,128)(2,1)S(1)}, bf16[512,1,128]{2,0,1:T(8,128)(2,1)S(1)}, u32[]{:S(2)}, u32[]{:S(2)}) collective-permute-start(bf16[512,1,128]{2,0,1:T(8,128)(2,1)S(1)} %bitcast.483), channel_id=1, source_target_pairs={{0,8},{4,12},{8,16},{12,20},{16,24},{20,28},{1,9},{5,13},{9,17},{1... | collective-permute-start | bytes 393224 | tf_op jit(solution)/shard_map/ppermute | solution.py:19
  64.3 45.5 %collective-permute-start.9 = (bf16[512,1,128]{2,0,1:T(8,128)(2,1)S(1)}, bf16[512,1,128]{2,0,1:T(8,128)(2,1)S(1)}, u32[]{:S(2)}, u32[]{:S(2)}) collective-permute-start(bf16[512,1,128]{2,0,1:T(8,128)(2,1)S(1)} %bitcast.484), channel_id=1, source_target_pairs={{8,0},{12,4},{16,8},{20,12},{24,16},{28,20},{9,1},{13,5},{17,9},{2... | collective-permute-start | bytes 393224 | tf_op jit(solution)/shard_map/ppermute | solution.py:19
  65.6 47.2 %collective-permute-start.6 = (bf16[512,1,128]{2,0,1:T(8,128)(2,1)S(1)}, bf16[512,1,128]{2,0,1:T(8,128)(2,1)}, u32[]{:S(2)}, u32[]{:S(2)}) collective-permute-start(bf16[512,1,128]{2,0,1:T(8,128)(2,1)S(1)} %bitcast.485), channel_id=1, source_target_pairs={{0,4},{4,8},{8,12},{12,16},{16,20},{20,24},{24,28},{1,5},{5,9},{9,... | collective-permute-start | bytes 393224 | tf_op jit(solution)/shard_map/ppermute | solution.py:19
  71.2 41.6 %collective-permute-start.7 = (bf16[512,1,128]{2,0,1:T(8,128)(2,1)S(1)}, bf16[512,1,128]{2,0,1:T(8,128)(2,1)}, u32[]{:S(2)}, u32[]{:S(2)}) collective-permute-start(bf16[512,1,128]{2,0,1:T(8,128)(2,1)S(1)} %bitcast.486), channel_id=1, source_target_pairs={{12,0},{16,4},{20,8},{24,12},{28,16},{13,1},{17,5},{21,9},{25,13},... | collective-permute-start | bytes 393224 | tf_op jit(solution)/shard_map/ppermute | solution.py:19
  72.6 43.3 %collective-permute-start.10 = (bf16[512,1,128]{2,0,1:T(8,128)(2,1)S(1)}, bf16[512,1,128]{2,0,1:T(8,128)(2,1)S(1)}, u32[]{:S(2)}, u32[]{:S(2)}) collective-permute-start(bf16[512,1,128]{2,0,1:T(8,128)(2,1)S(1)} %bitcast.487), channel_id=1, source_target_pairs={{0,12},{4,16},{8,20},{12,24},{16,28},{1,13},{5,17},{9,21},{13,25},... | collective-permute-start | bytes 393224 | tf_op jit(solution)/shard_map/ppermute | solution.py:19
  125.1 30.5 %all-to-all-start = ((bf16[4,128,2048]{2,1,0:T(8,128)(2,1)}), bf16[4,128,2048]{2,1,0:T(8,128)(2,1)}, u32[]{:S(2)}, u32[]{:S(2)}) async-start(bf16[4,128,2048]{2,1,0:T(8,128)(2,1)} %bitcast.475), calls=%async_computation | async-start | bytes 4194304 | tf_op jit(solution)/shard_map/all_to_all | solution.py:185
  129.9 151.0 %all-gather.5.cloned.1.call-start = ((), (), s32[]{:S(2)}) async-start(), calls=%async_computation.5 | async-start | bytes 17301504 | tf_op jit(solution)/shard_map/all_gather | solution.py:264
  160.7 416.1 %reduce-scatter.5.cloned.1.call-start = ((), (), s32[]{:S(2)}) async-start(), calls=%async_computation.8 | async-start | bytes 17301504 | tf_op jit(solution)/shard_map/reduce_scatter | solution.py:281
  395.7 218.9 %all-gather.9.cloned.1.call-start = ((), (), s32[]{:S(2)}) async-start(), calls=%async_computation.9 | async-start | bytes 2621440 | tf_op jit(solution)/shard_map/all_gather | solution.py:299
  581.8 231.9 %reduce-scatter.3.cloned.1.call-start = ((), (), s32[]{:S(2)}) async-start(), calls=%async_computation.7 | async-start | bytes 17301504 | tf_op jit(solution)/shard_map/reduce_scatter | solution.py:284
  634.2 60.9 %collective-permute-start.16 = (bf16[512,1,128]{2,0,1:T(8,128)(2,1)}, bf16[512,1,128]{2,0,1:T(8,128)(2,1)S(1)}, u32[]{:S(2)}, u32[]{:S(2)}) collective-permute-start(bf16[512,1,128]{2,0,1:T(8,128)(2,1)} %get-tuple-element.65), channel_id=1, source_target_pairs={{12,0},{16,4},{20,8},{24,12},{28,16},{13,1},{17,5},{21,9},{25,13},... | collective-permute-start | bytes 393224 | tf_op jit(solution)/shard_map/ppermute | solution.py:19
  635.5 66.2 %collective-permute-start.17 = (bf16[512,1,128]{2,0,1:T(8,128)(2,1)}, bf16[512,1,128]{2,0,1:T(8,128)(2,1)S(1)}, u32[]{:S(2)}, u32[]{:S(2)}) collective-permute-start(bf16[512,1,128]{2,0,1:T(8,128)(2,1)} %get-tuple-element.66), channel_id=1, source_target_pairs={{0,4},{4,8},{8,12},{12,16},{16,20},{20,24},{24,28},{1,5},{5,9},{9,... | collective-permute-start | bytes 393224 | tf_op jit(solution)/shard_map/ppermute | solution.py:19
  644.0 59.2 %collective-permute-start.12 = (bf16[512,1,128]{2,0,1:T(8,128)(2,1)}, bf16[512,1,128]{2,0,1:T(8,128)(2,1)S(1)}, u32[]{:S(2)}, u32[]{:S(2)}) collective-permute-start(bf16[512,1,128]{2,0,1:T(8,128)(2,1)} %get-tuple-element.61), channel_id=1, source_target_pairs={{4,0},{8,4},{12,8},{16,12},{20,16},{24,20},{28,24},{5,1},{9,5},{13... | collective-permute-start | bytes 393224 | tf_op jit(solution)/shard_map/ppermute | solution.py:19
  645.3 64.5 %collective-permute-start.13 = (bf16[512,1,128]{2,0,1:T(8,128)(2,1)}, bf16[512,1,128]{2,0,1:T(8,128)(2,1)S(1)}, u32[]{:S(2)}, u32[]{:S(2)}) collective-permute-start(bf16[512,1,128]{2,0,1:T(8,128)(2,1)} %get-tuple-element.62), channel_id=1, source_target_pairs={{0,12},{4,16},{8,20},{12,24},{16,28},{1,13},{5,17},{9,21},{13,25},... | collective-permute-start | bytes 393224 | tf_op jit(solution)/shard_map/ppermute | solution.py:19
  662.4 48.6 %collective-permute-start.14 = (bf16[512,1,128]{2,0,1:T(8,128)(2,1)}, bf16[512,1,128]{2,0,1:T(8,128)(2,1)S(1)}, u32[]{:S(2)}, u32[]{:S(2)}) collective-permute-start(bf16[512,1,128]{2,0,1:T(8,128)(2,1)} %get-tuple-element.63), channel_id=1, source_target_pairs={{8,0},{12,4},{16,8},{20,12},{24,16},{28,20},{9,1},{13,5},{17,9},{2... | collective-permute-start | bytes 393224 | tf_op jit(solution)/shard_map/ppermute | solution.py:19
  695.1 20.5 %collective-permute-start.15 = (bf16[512,1,128]{2,0,1:T(8,128)(2,1)S(1)}, bf16[512,1,128]{2,0,1:T(8,128)(2,1)S(1)}, u32[]{:S(2)}, u32[]{:S(2)}) collective-permute-start(bf16[512,1,128]{2,0,1:T(8,128)(2,1)S(1)} %copy-done.94), channel_id=1, source_target_pairs={{0,8},{4,12},{8,16},{12,20},{16,24},{20,28},{1,9},{5,13},{9,17},{1... | collective-permute-start | bytes 393224 | tf_op jit(solution)/shard_map/ppermute | solution.py:19
  701.7 18.4 %collective-permute-start.18 = (bf16[512,1,128]{2,0,1:T(8,128)(2,1)S(1)}, bf16[512,1,128]{2,0,1:T(8,128)(2,1)S(1)}, u32[]{:S(2)}, u32[]{:S(2)}) collective-permute-start(bf16[512,1,128]{2,0,1:T(8,128)(2,1)S(1)} %get-tuple-element.55), channel_id=1, source_target_pairs={{4,0},{8,4},{12,8},{16,12},{20,16},{24,20},{28,24},{5,1},{9,5},{13... | collective-permute-start | bytes 393224 | tf_op jit(solution)/shard_map/ppermute | solution.py:19
  703.1 22.9 %collective-permute-start.19 = (bf16[512,1,128]{2,0,1:T(8,128)(2,1)S(1)}, bf16[512,1,128]{2,0,1:T(8,128)(2,1)S(1)}, u32[]{:S(2)}, u32[]{:S(2)}) collective-permute-start(bf16[512,1,128]{2,0,1:T(8,128)(2,1)S(1)} %get-tuple-element.56), channel_id=1, source_target_pairs={{0,12},{4,16},{8,20},{12,24},{16,28},{1,13},{5,17},{9,21},{13,25},... | collective-permute-start | bytes 393224 | tf_op jit(solution)/shard_map/ppermute | solution.py:19
  709.8 16.3 %collective-permute-start.20 = (bf16[512,1,128]{2,0,1:T(8,128)(2,1)S(1)}, bf16[512,1,128]{2,0,1:T(8,128)(2,1)S(1)}, u32[]{:S(2)}, u32[]{:S(2)}) collective-permute-start(bf16[512,1,128]{2,0,1:T(8,128)(2,1)S(1)} %get-tuple-element.57), channel_id=1, source_target_pairs={{8,0},{12,4},{16,8},{20,12},{24,16},{28,20},{9,1},{13,5},{17,9},{2... | collective-permute-start | bytes 393224 | tf_op jit(solution)/shard_map/ppermute | solution.py:19
  711.1 15.0 %collective-permute-start.21 = (bf16[512,1,128]{2,0,1:T(8,128)(2,1)S(1)}, bf16[512,1,128]{2,0,1:T(8,128)(2,1)S(1)}, u32[]{:S(2)}, u32[]{:S(2)}) collective-permute-start(bf16[512,1,128]{2,0,1:T(8,128)(2,1)S(1)} %get-tuple-element.58), channel_id=1, source_target_pairs={{0,8},{4,12},{8,16},{12,20},{16,24},{20,28},{1,9},{5,13},{9,17},{1... | collective-permute-start | bytes 393224 | tf_op jit(solution)/shard_map/ppermute | solution.py:19
  737.6 53.3 %all-to-all-start.2 = ((bf16[4,128,2048]{2,1,0:T(8,128)(2,1)}), bf16[4,128,2048]{2,1,0:T(8,128)(2,1)}, u32[]{:S(2)}, u32[]{:S(2)}) async-start(bf16[4,128,2048]{2,1,0:T(8,128)(2,1)} %bitcast.467), calls=%async_computation.4 | async-start | bytes 4194304 | tf_op jit(solution)/shard_map/all_to_all | solution.py:185
  742.2 215.3 %all-gather.11.cloned.1.call-start = ((), (), s32[]{:S(2)}) async-start(), calls=%async_computation.10 | async-start | bytes 2621440 | tf_op jit(solution)/shard_map/all_gather | solution.py:367
  816.7 332.3 %all-reduce.11.cloned.1.call-start = ((), (), s32[]{:S(2)}) async-start(), calls=%async_computation.12 | async-start | bytes 18874368 | tf_op jit(solution)/shard_map/psum | solution.py:371
  831.5 447.6 %all-reduce.9.cloned.1.call-start = ((), (), s32[]{:S(2)}) async-start(), calls=%async_computation.11 | async-start | bytes 524288 | tf_op jit(solution)/shard_map/psum | solution.py:376
  883.9 73.6 %all-to-all-start.1 = ((bf16[128,4,512]{2,0,1:T(8,128)(2,1)}), bf16[128,4,512]{2,0,1:T(8,128)(2,1)S(1)}, u32[]{:S(2)}, u32[]{:S(2)}) async-start(bf16[128,4,512]{2,0,1:T(8,128)(2,1)} %bitcast.449), calls=%async_computation.2 | async-start | bytes 1048576 | tf_op jit(solution)/shard_map/all_to_all | solution.py:288
  (107 other events, 1501.0 us)
Sparse Core Ops, SparseCore 0:
  11.5 134.3 all-gather.6
  160.9 119.9 all-gather.4
  395.8 181.0 reduce-scatter.4
  581.9 24.2 all-gather.8
  608.3 205.3 reduce-scatter.2
  816.8 25.2 all-gather.10
  847.8 301.1 all-reduce.10
  1155.1 123.8 all-reduce.8

commit v2 on v1

v2 whole, which is shorter than its diff:
```python
import jax
import jax.numpy as jnp
from jax import lax
from jax.experimental import pallas as pl
from jax.experimental.pallas import tpu as pltpu
from jax.sharding import PartitionSpec as P

SPAN = 4
EPSILON = 1e-06
THETA = 1000000.0
MASKED = -1e30
LOG2E = 1.4426950408889634
NT_DIMS = (((1,), (1,)), ((), ()))
TN_DIMS = (((0,), (0,)), ((), ()))
VMEM_LIMIT = 60 * 1024 * 1024
TILE = 256
CHUNKS = 4
F32 = jnp.float32
LOW = jnp.bfloat16


def rms_scale(values, scales):
    return values * lax.rsqrt(jnp.mean(values * values, axis=-1, keepdims=True) + EPSILON) * scales


def swap(block, axis, mask):
    devices = range(lax.axis_size(axis))
    return lax.ppermute(block, axis, [(i, i ^ mask) for i in devices])


def turn(block, step):
    count = lax.axis_size("ep")
    return lax.ppermute(block, "ep", [(i, (i + 2 * step) % count) for i in range(count)])


def add_low(kept, received):
    return (kept.astype(F32) + received.astype(F32)).astype(LOW)


def tie(*values):
    return lax.optimization_barrier(values)


def paired(block, axis, mask):
    return jnp.concatenate([block, swap(block, axis, mask)], axis=0)


def spread_start(slots):
    half = slots[0].shape[0] // 2
    first = jnp.concatenate([rows[:half] for rows in slots], axis=0)
    second = jnp.concatenate([rows[half:] for rows in slots], axis=0)
    return paired(first, "tp", 2), paired(second, "ep", 1)


def spread_next(first, second):
    return jnp.concatenate([paired(first, "ep", 1), paired(second, "tp", 2)], axis=0)


def halves(block):
    size = block.shape[0] // 2
    return block[:size], block[size:]


def fold(block, axis, mask):
    kept, sent = halves(block)
    return add_low(kept, swap(sent, axis, mask))


def fold_inner(block, axis, mask):
    parts = block.reshape(2, 2, -1, block.shape[1])
    kept = add_low(parts[:, 0], swap(parts[:, 1], axis, mask))
    return kept.reshape(-1, block.shape[1])


def collect_start(kept, sent):
    return halves(add_low(kept, swap(sent, "tp", 1)))


def collect_next(first, second):
    return fold(first, "ep", 1), fold(second, "tp", 2)


def collect_last(first, second):
    return fold(first, "tp", 2), fold(second, "ep", 1)


def slot_rows(first, second, count):
    parts = [part.reshape(count, -1, part.shape[1]) for part in (first, second)]
    return jnp.concatenate(parts, axis=1)


def pick(array, index, axis=0):
    return lax.dynamic_index_in_dim(array, index, axis, keepdims=False)


def ep_masks():
    return [1 << n for n in range(lax.axis_size("ep").bit_length() - 1)]


def halve_sum(block, mask):
    bit = lax.axis_index("ep") // mask % 2
    parts = block.reshape(2, -1, block.shape[1])
    return add_low(pick(parts, bit), swap(pick(parts, 1 - bit), "ep", mask))


def double(block, mask):
    bit = lax.axis_index("ep") // mask % 2
    other = swap(block, "ep", mask)
    low = jnp.where(bit == 0, block, other)
    high = jnp.where(bit == 0, other, block)
    return jnp.concatenate([low, high], axis=0)


def sum_all(values):
    for axis in ("tp", "ep"):
        mask = 1
        while mask < lax.axis_size(axis):
            values = values + swap(values, axis, mask)
            mask *= 2
    return values


def expert_kernel(
    own_ref,
    other_ref,
    cotangent_own_ref,
    cotangent_other_ref,
    router_ref,
    router_t_ref,
    select_ref,
    gate_ref,
    up_ref,
    down_ref,
    *refs,
):
    grad_keep_ref, grad_send_ref, out_keep_ref, out_send_ref = refs[-10:-6]
    rows_ref, cotangents_ref, hidden_ref, d_gate_ref, d_up_ref, dlog_ref = refs[-6:]
    is_own = pl.program_id(0) < pl.num_programs(0) // 2
    rows = jnp.where(is_own, own_ref[...], other_ref[...])
    model_width = rows.shape[1]
    cotangents = jnp.where(is_own, cotangent_own_ref[...], cotangent_other_ref[...])
    cotangents = cotangents.reshape(rows.shape[0], -1)
    chosen = cotangents[:, model_width : model_width + router_ref.shape[1]].astype(F32)
    logits = jnp.dot(rows, router_ref[...], preferred_element_type=F32)
    logits = jnp.where(chosen > 0.5, logits, MASKED)
    probs = jnp.exp(logits - jnp.max(logits, axis=-1, keepdims=True))
    probs = probs / jnp.sum(probs, axis=-1, keepdims=True)
    select = select_ref[...]
    probs_high = probs.astype(LOW)
    probs_rest = (probs - probs_high.astype(F32)).astype(LOW)
    weight = jnp.dot(probs_high, select, preferred_element_type=F32)
    weight += jnp.dot(probs_rest, select, preferred_element_type=F32)
    gate = jnp.dot(rows, gate_ref[...], preferred_element_type=F32)
    up = jnp.dot(rows, up_ref[...], preferred_element_type=F32)
    d_hidden = (
        lax.dot_general(
            cotangents[:, :model_width], down_ref[...], NT_DIMS, preferred_element_type=F32
        )
        * weight
    )
    sig = 1.0 / (1.0 + jnp.exp(-gate))
    silu = gate * sig
    hidden = silu * up
    d_up = (d_hidden * silu).astype(LOW)
    d_gate = (d_hidden * up * sig * (1.0 + gate * (1.0 - sig))).astype(LOW)
    hidden_low = (hidden * weight).astype(LOW)
    dots = lax.dot_general(
        (d_hidden * hidden).astype(LOW), select, NT_DIMS, preferred_element_type=F32
    )
    dlog = (dots - probs * jnp.sum(dots, axis=-1, keepdims=True)).astype(LOW)

    def store(ref, values):
        ref[...] = values.reshape(ref.shape)

    def store_either(keep_ref, send_ref, values):
        @pl.when(is_own)
        def _():
            store(keep_ref, values)

        @pl.when(jnp.logical_not(is_own))
        def _():
            store(send_ref, values)

    store(rows_ref, rows)
    store(cotangents_ref, cotangents[:, :model_width])
    store(hidden_ref, hidden_low)
    store(d_gate_ref, d_gate)
    store(d_up_ref, d_up)
    store(dlog_ref, dlog)
    outs = jnp.dot(hidden_low, down_ref[...], preferred_element_type=F32).astype(LOW)
    store_either(out_keep_ref, out_send_ref, outs)
    grads = lax.dot_general(d_gate, gate_ref[...], NT_DIMS, preferred_element_type=F32)
    grads += lax.dot_general(d_up, up_ref[...], NT_DIMS, preferred_element_type=F32)
    grads += jnp.dot(dlog, router_t_ref[...], preferred_element_type=F32)
    store_either(grad_keep_ref, grad_send_ref, grads.astype(LOW))


def expert_pass(own, other, cotangents, at, chunk, slots_all, fixed, kept):
    count, model_width = own.shape
    groups, _, unit, wide = cotangents[0].shape
    slots = slots_all // CHUNKS
    half = count // TILE
    width = fixed[-1].shape[0]
    experts_all = fixed[0].shape[1]
    block = TILE // (slots * unit)

    def first(i):
        return jnp.minimum(i, half - 1)

    def second(i):
        return jnp.maximum(i - half, 0)

    def every(i):
        return i

    def rows_spec(index):
        return pl.BlockSpec((TILE, model_width), lambda i: (index(i), 0))

    def placed(columns, index, where):
        return pl.BlockSpec((block, slots, unit, columns), lambda i: (index(i), where, 0, 0))

    def whole(array):
        return pl.BlockSpec(array.shape, lambda i: (0, 0), pipeline_mode=pl.Buffered(1))

    columns = (model_width, model_width, width, width, width, experts_all)
    in_specs = [
        rows_spec(first),
        rows_spec(second),
        placed(wide, first, at),
        placed(wide, second, at),
    ] + [whole(array) for array in fixed]
    aliases = {len(in_specs) + n: 2 + n for n in range(len(kept))}
    part = jax.ShapeDtypeStruct((count, model_width), LOW)
    place = jax.ShapeDtypeStruct((groups, slots_all, unit, model_width), LOW)
    return pl.pallas_call(
        expert_kernel,
        grid=(2 * half,),
        in_specs=in_specs + [pl.BlockSpec(memory_space=pl.ANY)] * len(kept),
        out_specs=[
            rows_spec(first),
            rows_spec(second),
            placed(model_width, first, chunk),
            placed(model_width, second, chunk),
        ]
        + [placed(size, every, chunk) for size in columns],
        out_shape=[part, part, place, place]
        + [jax.ShapeDtypeStruct((2 * groups, slots_all, unit, size), LOW) for size in columns],
        input_output_aliases=aliases,
        compiler_params=pltpu.CompilerParams(vmem_limit_bytes=VMEM_LIMIT),
        cost_estimate=pl.CostEstimate(
            flops=24 * count * model_width * width,
            bytes_accessed=20 * count * model_width,
            transcendentals=2 * count * width,
        ),
        name="expert_pass",
    )(own, other, *cotangents, *fixed, *kept)


def turned_halves(values):
    return pltpu.roll(values, values.shape[1] // 2, 1)


def head_rows(lin, gain, cos, sin):
    scale = lax.rsqrt(jnp.mean(lin * lin, axis=-1, keepdims=True) + EPSILON)
    hat = lin * scale
    normed = hat * gain
    return scale, hat, normed * cos + turned_halves(normed) * sin


def allowed_keys(place_ref, block, keys, queries):
    key_pos = place_ref[2 + block] + lax.broadcasted_iota(jnp.int32, (keys, 1), 0)
    key_pos = jnp.where(key_pos < place_ref[1], -1, key_pos)
    query_pos = place_ref[0] + lax.broadcasted_iota(jnp.int32, (1, queries), 1)
    return key_pos <= query_pos


def attend_kernel(
    place_ref, q_ref, gain_ref, cos_ref, sin_ref, k_ref, v_t_ref, o_ref, norm_ref
):
    queries, head_width = q_ref.shape
    _, _, q_rot = head_rows(q_ref[...], gain_ref[...], cos_ref[...], sin_ref[...])
    q_low = q_rot.astype(LOW)
    factor = head_width ** (-0.5) * LOG2E
    total = jnp.zeros((1, queries), F32)
    acc = jnp.zeros((head_width, queries), F32)
    for block in range(SPAN):
        span = pl.ds(block * queries, queries)
        scores = lax.dot_general(k_ref[span, :], q_low, NT_DIMS, preferred_element_type=F32)
        probs = jnp.where(
            allowed_keys(place_ref, block, queries, queries), jnp.exp2(scores * factor), 0.0
        )
        total += jnp.sum(probs, axis=0, keepdims=True)
        acc += jnp.dot(v_t_ref[:, span], probs.astype(LOW), preferred_element_type=F32)
    o_ref[...] = (acc / total).T.astype(LOW)
    norm_ref[0] = 1.0 / total


def attend(place, q_lin, gain, cos, sin, k_all, v_t):
    tokens, columns = q_lin.shape
    head_width = gain.shape[1]
    heads = columns // head_width
    row = pl.BlockSpec((tokens, head_width), lambda h, p: (0, h))

    def whole(array):
        return pl.BlockSpec(array.shape, lambda h, p: (0, 0))

    return pl.pallas_call(
        attend_kernel,
        grid_spec=pltpu.PrefetchScalarGridSpec(
            num_scalar_prefetch=1,
            grid=(heads,),
            in_specs=[row] + [whole(x) for x in (gain, cos, sin, k_all, v_t)],
            out_specs=[row, pl.BlockSpec((1, 1, tokens), lambda h, p: (h, 0, 0))],
        ),
        out_shape=[
            jax.ShapeDtypeStruct((tokens, columns), LOW),
            jax.ShapeDtypeStruct((heads, 1, tokens), F32),
        ],
        compiler_params=pltpu.CompilerParams(vmem_limit_bytes=VMEM_LIMIT),
        cost_estimate=pl.CostEstimate(
            flops=16 * SPAN * tokens * tokens * columns // 8 * 2,
            bytes_accessed=8 * tokens * columns,
            transcendentals=SPAN * tokens * tokens * heads,
        ),
        name="attend",
    )(place, q_lin, gain, cos, sin, k_all, v_t)


def attend_back_kernel(
    place_ref,
    q_ref,
    d_ref,
    gain_ref,
    cos_ref,
    sin_ref,
    k_ref,
    k_t_ref,
    v_ref,
    norm_ref,
    dq_ref,
    dk_ref,
    dv_ref,
    dgain_ref,
):
    queries, head_width = q_ref.shape
    gain = gain_ref[...]
    scale, hat, q_rot = head_rows(q_ref[...], gain, cos_ref[...], sin_ref[...])
    q_low = q_rot.astype(LOW)
    d_low = d_ref[...]
    shrink = head_width ** (-0.5)
    factor = shrink * LOG2E
    inverse = norm_ref[0]
    delta = jnp.zeros((1, queries), F32)
    kept = []

    @pl.when(pl.program_id(0) == 0)
    def _():
        dk_ref[...] = jnp.zeros_like(dk_ref)
        dv_ref[...] = jnp.zeros_like(dv_ref)
        dgain_ref[...] = jnp.zeros_like(dgain_ref)

    for block in range(SPAN):
        span = pl.ds(block * queries, queries)
        scores = lax.dot_general(k_ref[span, :], q_low, NT_DIMS, preferred_element_type=F32)
        probs = jnp.where(
            allowed_keys(place_ref, block, queries, queries),
            jnp.exp2(scores * factor) * inverse,
            0.0,
        )
        d_probs = lax.dot_general(v_ref[span, :], d_low, NT_DIMS, preferred_element_type=F32)
        delta += jnp.sum(probs * d_probs, axis=0, keepdims=True)
        dv_ref[span, :] += jnp.dot(probs.astype(LOW), d_low, preferred_element_type=F32)
        kept.append((probs, d_probs))
    acc = jnp.zeros((head_width, queries), F32)
    for block in range(SPAN):
        span = pl.ds(block * queries, queries)
        probs, d_probs = kept[block]
        d_scores = (probs * (d_probs - delta)).astype(LOW)
        dk_ref[span, :] += jnp.dot(d_scores, q_low, preferred_element_type=F32) * shrink
        acc += jnp.dot(k_t_ref[:, span], d_scores, preferred_element_type=F32)
    d_rot = acc.T * shrink
    d_normed = d_rot * cos_ref[...] + turned_halves(d_rot * sin_ref[...])
    dgain_ref[...] += jnp.sum(d_normed * hat, axis=0, keepdims=True)
    scaled = d_normed * gain
    d_lin = scale * (scaled - hat * jnp.mean(scaled * hat, axis=-1, keepdims=True))
    dq_ref[...] = d_lin.astype(LOW)


def attend_back(place, q_lin, d_attn, gain, cos, sin, k_all, v_all, inverse):
    tokens, columns = q_lin.shape
    head_width = gain.shape[1]
    heads = columns // head_width
    keys = k_all.shape[0]
    row = pl.BlockSpec((tokens, head_width), lambda h, p: (0, h))
    k_t = k_all.T

    def whole(shape):
        return pl.BlockSpec(shape, lambda h, p: (0, 0))

    fixed = (gain, cos, sin, k_all, k_t, v_all)
    return pl.pallas_call(
        attend_back_kernel,
        grid_spec=pltpu.PrefetchScalarGridSpec(
            num_scalar_prefetch=1,
            grid=(heads,),
            in_specs=[row, row]
            + [whole(x.shape) for x in fixed]
            + [pl.BlockSpec((1, 1, tokens), lambda h, p: (h, 0, 0))],
            out_specs=[
                row,
                whole((keys, head_width)),
                whole((keys, head_width)),
                whole((1, head_width)),
            ],
        ),
        out_shape=[
            jax.ShapeDtypeStruct((tokens, columns), LOW),
            jax.ShapeDtypeStruct((keys, head_width), F32),
            jax.ShapeDtypeStruct((keys, head_width), F32),
            jax.ShapeDtypeStruct((1, head_width), F32),
        ],
        compiler_params=pltpu.CompilerParams(vmem_limit_bytes=VMEM_LIMIT),
        cost_estimate=pl.CostEstimate(
            flops=20 * keys * tokens * columns,
            bytes_accessed=8 * tokens * columns,
            transcendentals=keys * tokens * heads,
        ),
        name="attend_back",
    )(place, q_lin, d_attn, *fixed, inverse)


def body(
    block_in,
    input_norm,
    q_weight,
    k_weight,
    v_weight,
    q_gain,
    k_gain,
    o_weight,
    post_norm,
    router,
    expert_gate,
    expert_up,
    expert_down,
    expert_ids,
    prefix_len,
    out_grad,
):
    tokens, model_width = block_in.shape
    head_width = q_gain.shape[0]
    tp_count = lax.axis_size("tp")
    tp_rank = lax.axis_index("tp")
    ep_count = lax.axis_size("ep")
    ep_rank = lax.axis_index("ep")
    share_rows = tokens // tp_count
    dev_slot = ep_rank % SPAN
    prefix = lax.dynamic_index_in_dim(prefix_len, ep_rank // SPAN, keepdims=False)
    core_bit = tp_rank % 2
    x_bit = tp_rank // 2
    row_index = jnp.arange(tokens, dtype=jnp.int32)
    slots_all = ep_count // 2

    def block_place(slot):
        return (slot + SPAN - 1) % SPAN * tokens

    def my_rows(full_rows):
        return lax.dynamic_slice_in_dim(full_rows, tp_rank * share_rows, share_rows, 0)

    def sum_rows(partial_rows):
        parts = partial_rows.reshape(2, 2, share_rows, -1)

        sent = swap(pick(parts, 1 - core_bit, 1).astype(LOW), "tp", 1)
        parts = pick(parts, core_bit, 1) + sent.astype(F32)
        sent = swap(pick(parts, 1 - x_bit, 0).astype(LOW), "tp", 2)
        return pick(parts, x_bit, 0) + sent.astype(F32)

    def join_rows(rows):
        other = swap(rows, "tp", 2)
        pair = jnp.stack([jnp.where(x_bit == 0, rows, other), jnp.where(x_bit == 0, other, rows)])
        other = swap(pair, "tp", 1)
        low = jnp.where(core_bit == 0, pair, other)
        high = jnp.where(core_bit == 0, other, pair)
        return jnp.stack([low, high], axis=1).reshape(tokens, -1)

    experts_all = router.shape[1]
    local_experts = expert_gate.shape[0]
    hidden_width = expert_gate.shape[2]
    expert_index = jnp.arange(experts_all, dtype=jnp.int32)
    width = local_experts * hidden_width

    chosen = jnp.any(my_rows(expert_ids)[:, :, None] == expert_index[None, None, :], axis=1)
    chosen = jnp.pad(chosen.astype(LOW), ((0, 0), (0, -experts_all % 128)))
    wide_rows = jnp.concatenate([my_rows(out_grad), chosen], axis=1)
    per_chunk = slots_all // CHUNKS
    order = [c * per_chunk + at for c in (0, 1, 3, 2) for at in range(per_chunk)]
    unit = share_rows // 2

    def fetch(rows, positions):
        return [
            rows if order[p] == 0 else turn(rows, slots_all - order[p])
            for c in positions
            for p in range(c * per_chunk, (c + 1) * per_chunk)
        ]

    wide_first = spread_start(fetch(wide_rows, (0,)))
    large = slots_all > CHUNKS
    near_groups = ((1,), (2,)) if large else ((1, 2),)
    wide_near = [fetch(wide_rows, group) for group in near_groups]

    x_full = block_in.astype(F32)
    attn_low = rms_scale(x_full, input_norm).astype(LOW)
    k_lin = jnp.dot(attn_low, k_weight, preferred_element_type=F32)
    v_low = jnp.dot(attn_low, v_weight, preferred_element_type=F32).astype(LOW)
    half_width = head_width // 2
    exponents = jnp.arange(half_width, dtype=F32) * (-2.0 / head_width)
    positions = block_place(dev_slot) + row_index
    angles = positions.astype(F32)[:, None] * (THETA**exponents)[None, :]
    cos_half, sin_half = jnp.cos(angles), jnp.sin(angles)
    cos = jnp.concatenate([cos_half, cos_half], axis=1)
    sin = jnp.concatenate([-sin_half, sin_half], axis=1)

    def key_path(lin_rows, scales):
        normed = rms_scale(lin_rows, scales)
        lead, tail = normed[:, :half_width], normed[:, half_width:]
        return normed * cos + jnp.concatenate([tail, lead], axis=1) * sin

    k_rot, k_back = jax.vjp(key_path, k_lin, k_gain)
    pair = jnp.concatenate([k_rot.astype(LOW), v_low], axis=1)
    pair, *wide_first = tie(pair, *wide_first)
    pairs = [pair] + [swap(pair, "ep", d) for d in range(1, SPAN)]
    wide_first = spread_next(*wide_first)
    q_lin = jnp.dot(attn_low, q_weight, preferred_element_type=F32)
    width_own = local_experts * hidden_width
    gate_cat = expert_gate.transpose(1, 0, 2).reshape(-1, width_own)
    up_cat = expert_up.transpose(1, 0, 2).reshape(-1, width_own)
    gate_cat, up_cat, q_lin, wide_first, wide_rows, pairs, wide_near = tie(
        gate_cat, up_cat, q_lin, wide_first, wide_rows, pairs, wide_near
    )
    wide_far = fetch(wide_rows, (3,))
    wide_near = [spread_start(group) for group in wide_near]
    wide_first_other = swap(wide_first, "tp", 1)
    k_all = jnp.concatenate([p[:, :head_width] for p in pairs], axis=0)
    v_all = jnp.concatenate([p[:, head_width:] for p in pairs], axis=0)
    place = jnp.stack(
        [block_place(dev_slot), prefix] + [block_place(dev_slot ^ d) for d in range(SPAN)]
    ).astype(jnp.int32)
    gain_row = q_gain.reshape(1, -1)
    o_low, inverse = attend(place, q_lin, gain_row, cos, sin, k_all, v_all.T)
    o_low, wide_first_other, wide_near = tie(o_low, wide_first_other, wide_near)
    wide_near = [spread_next(*group) for group in wide_near]
    head_part = jnp.dot(o_low, o_weight, preferred_element_type=F32)
    x_mid = my_rows(x_full) + sum_rows(head_part)
    ffn_in, post_norm_back = jax.vjp(rms_scale, x_mid, post_norm)
    ffn_low = ffn_in.astype(LOW)
    ffn_low, *wide_far = tie(ffn_low, *wide_far)

    own_expert = ep_rank * local_experts + jnp.arange(width, dtype=jnp.int32) // hidden_width
    select = (expert_index[:, None] == own_expert[None, :]).astype(LOW)
    down_cat = expert_down.reshape(width, -1)
    fixed = (router, router.T, select, gate_cat, up_cat, down_cat)
    started = {c: spread_start(fetch(ffn_low, (c,))) for c in range(3)}
    owned = {c: spread_next(*started[c]) for c in range(2)}
    others = {0: swap(owned[0], "tp", 1)}
    ffn_last = fetch(ffn_low, (3,))

    def shaped(*arrays):
        return [x.reshape(8, -1, unit, x.shape[1]) for x in arrays]

    def land(total, chunk, first, second):
        rows = slot_rows(first, second, per_chunk)
        for at in range(per_chunk):
            h = order[chunk * per_chunk + at]
            total = total + (rows[at] if h == 0 else turn(rows[at], h)).astype(F32)
        return total

    kept = []
    folded = {}
    for chunk in range(CHUNKS):
        moving = []
        if chunk + 1 < CHUNKS:
            moving.append(("other", chunk + 1, [owned[chunk + 1]]))
        if chunk + 2 < CHUNKS:
            moving.append(("own", chunk + 2, list(started[chunk + 2])))
        if chunk + 3 < CHUNKS:
            moving.append(("start", chunk + 3, ffn_last))
        if chunk == 0:
            for n, group in enumerate(wide_near):
                moving.append(("other", f"near{n}", [group]))
            moving.append(("start", "far", wide_far))
        if chunk == 1:
            moving.append(("own", "far", list(started["far"])))
        if chunk == 2:
            moving.append(("other", "far", [owned["far"]]))
        for stage in range(3):
            if chunk - 1 - stage >= 0:
                moving.append((stage, chunk - 1 - stage, list(folded[chunk - 1 - stage])))
        flat = [x for entry in moving for x in entry[2]]
        rows_own, rows_other, *flat = tie(owned[chunk], others[chunk], *flat)
        results = []
        for name, c, values in moving:
            taken, flat = flat[: len(values)], flat[len(values) :]
            if name == "other":
                results.append([swap(taken[0], "tp", 1)])
            elif name == "own":
                results.append([spread_next(*taken)])
            elif name == "start":
                results.append(list(spread_start(taken)))
            else:
                results.append(list((collect_start, collect_next, collect_last)[name](*taken)))
        wide = (
            (wide_first, wide_first_other),
            (wide_near[0], others.get("near0")),
            (wide_near[-1], others.get("near1" if large else "near0")),
            (owned.get("far"), others.get("far")),
        )[chunk]
        outs = expert_pass(
            rows_own,
            rows_other,
            shaped(*wide),
            1 if chunk == 2 and not large else 0,
            chunk,
            slots_all,
            fixed,
            kept,
        )
        flat = [x for values in results for x in values]
        grad_keep, grad_send, *flat = tie(outs[0], outs[1], *flat)
        kept = outs[2:]
        for (name, c, _), values in zip(moving, results):
            taken, flat = flat[: len(values)], flat[len(values) :]
            if name == "other":
                others[c] = taken[0]
            elif name == "own":
                owned[c] = taken[0]
            elif name == "start":
                started[c] = taken
            else:
                folded[c] = taken
        folded[chunk] = [grad_keep, grad_send]
    d_ffn = land(jnp.zeros_like(x_mid), 0, *folded[0])
    d_ffn = land(d_ffn, 1, *collect_last(*folded[1]))
    d_ffn = land(d_ffn, 2, *collect_last(*collect_next(*folded[2])))
    d_ffn = land(d_ffn, 3, *collect_last(*collect_next(*collect_start(*folded[3]))))
    out_keep, out_send, rows_all, cotangent_rows, hidden_low, d_gate_low, d_up_low, dlog_low = [
        x.reshape(-1, x.shape[-1]) for x in kept
    ]
    def over_rows(left, right):
        return jnp.einsum("ta,tb->ab", left, right, preferred_element_type=F32)

    def split_experts(wide_grad):
        return wide_grad.reshape(-1, local_experts, hidden_width).transpose(1, 0, 2)

    d_ffn, out_keep, out_send = tie(d_ffn, out_keep, out_send)
    out_first, out_second = collect_start(out_keep, out_send)
    if large:
        out_first, out_second, rows_all, d_gate_low, d_up_low, hidden_low = tie(
            out_first, out_second, rows_all, d_gate_low, d_up_low, hidden_low
        )
        router_grad_t = over_rows(dlog_low, rows_all)
        down_grad = over_rows(hidden_low, cotangent_rows).reshape(expert_down.shape)
        gate_grad = split_experts(over_rows(rows_all, d_gate_low))
        up_grad = split_experts(over_rows(rows_all, d_up_low))
        d_ffn, router_grad_t, down_grad, gate_grad, up_grad = tie(
            d_ffn, router_grad_t, down_grad, gate_grad, up_grad
        )
    d_mid_norm, post_norm_grad = post_norm_back(d_ffn)
    d_mid = my_rows(out_grad).astype(F32) + d_mid_norm
    d_mid_low = join_rows(d_mid.astype(LOW))
    o_sum = jnp.einsum("tj,td->jd", o_low, d_mid_low, preferred_element_type=F32).astype(LOW)
    d_attn_low = jnp.einsum(
        "td,jd->tj", d_mid_low, o_weight, preferred_element_type=F32
    ).astype(LOW)
    d_attn_low, o_sum, out_first, out_second = tie(d_attn_low, o_sum, out_first, out_second)
    masks = ep_masks()
    o_sum = halve_sum(o_sum, masks[0])
    out_second = fold(out_second, "tp", 2)
    dq_low, dk_all, dv_all, q_gain_grad = attend_back(
        place, q_lin, d_attn_low, gain_row, cos, sin, k_all, v_all, inverse
    )
    dq_low, dk_all, dv_all, o_sum, out_first, out_second = tie(
        dq_low, dk_all, dv_all, o_sum, out_first, out_second
    )
    out_first = fold_inner(out_first, "tp", 2)
    for mask in masks[1:]:
        o_sum = halve_sum(o_sum, mask)
    split = dq_low.shape[1] // 2
    first_sum = jnp.einsum(
        "td,tj->dj", attn_low, dq_low[:, :split], preferred_element_type=F32
    ).astype(LOW)
    first_sum = halve_sum(first_sum, masks[0])
    pair_grad = jnp.concatenate([dk_all, dv_all], axis=1)
    total = pair_grad[:tokens]
    for d in range(1, SPAN):
        part = pair_grad[d * tokens : (d + 1) * tokens].astype(LOW)
        total = total + swap(part, "ep", d).astype(F32)
    dk_lin, k_gain_grad = k_back(total[:, :head_width])
    dk_low = dk_lin.astype(LOW)
    dv_low = total[:, head_width:].astype(LOW)
    second_sum = jnp.einsum(
        "td,tj->dj",
        attn_low,
        jnp.concatenate([dq_low[:, split:], dk_low, dv_low], axis=1),
        preferred_element_type=F32,
    ).astype(LOW)
    d_attn_in = jnp.einsum("tj,dj->td", dq_low, q_weight, preferred_element_type=F32)
    d_attn_in = d_attn_in + jnp.einsum("tj,dj->td", dk_low, k_weight, preferred_element_type=F32)
    d_attn_in = d_attn_in + jnp.einsum("tj,dj->td", dv_low, v_weight, preferred_element_type=F32)

    first_sum, second_sum, o_sum, d_attn_in, out_first, dlog_low, hidden_low = tie(
        first_sum, second_sum, o_sum, d_attn_in, out_first, dlog_low, hidden_low
    )
    second_sum = halve_sum(second_sum, masks[0])
    for mask in masks[1:]:
        first_sum = halve_sum(first_sum, mask)
    for mask in masks[:0:-1]:
        o_sum = double(o_sum, mask)
    d_attn_rows = sum_rows(d_attn_in)
    _, input_norm_back = jax.vjp(rms_scale, my_rows(x_full), input_norm)
    d_in_norm, input_norm_grad = input_norm_back(d_attn_rows)
    input_rows = (d_mid + d_in_norm).astype(LOW)
    if not large:
        router_grad_t = over_rows(dlog_low, rows_all)
        down_grad = over_rows(hidden_low, cotangent_rows).reshape(expert_down.shape)
    gains = jnp.concatenate([q_gain_grad.reshape(-1), k_gain_grad])
    small = jnp.concatenate(
        [
            router_grad_t,
            post_norm_grad[None],
            input_norm_grad[None],
            jnp.pad(gains, (0, model_width - gains.shape[0]))[None],
        ],
        axis=0,
    )
    first_sum, second_sum, o_sum, small, input_rows, d_gate_low, d_up_low = tie(
        first_sum, second_sum, o_sum, small, input_rows, d_gate_low, d_up_low
    )
    o_sum = double(o_sum, masks[0])
    for mask in masks[1:]:
        second_sum = halve_sum(second_sum, mask)
    for mask in masks[:0:-1]:
        first_sum = double(first_sum, mask)
    if not large:
        gate_grad = split_experts(over_rows(rows_all, d_gate_low))
    input_grad = join_rows(input_rows)
    first_sum, second_sum, o_sum, small, d_up_low, out_first, out_second = tie(
        first_sum, second_sum, o_sum, small, d_up_low, out_first, out_second
    )
    first_sum = double(first_sum, masks[0])
    for mask in masks[:0:-1]:
        second_sum = double(second_sum, mask)
    out_first, out_second = fold(out_first, "ep", 1), fold(out_second, "ep", 1)
    if not large:
        up_grad = split_experts(over_rows(rows_all, d_up_low))
    first_sum, second_sum, small, out_first, out_second = tie(
        first_sum, second_sum, small, out_first, out_second
    )
    second_sum = double(second_sum, masks[0])
    small = sum_all(small)
    out_slots = slot_rows(out_first, out_second, slots_all)
    mixed = out_slots[0].astype(F32)
    for p in range(1, slots_all):
        mixed = mixed + turn(out_slots[p], order[p]).astype(F32)
    block_rows = (x_mid + mixed).astype(LOW)
    block_out = lax.all_to_all(block_rows, "tp", split_axis=1, concat_axis=0, tiled=True)
    o_weight_grad = o_sum.astype(F32)
    q_weight_grad = jnp.concatenate([first_sum, second_sum[:, :split]], axis=1).astype(F32)
    k_weight_grad = second_sum[:, split : split + head_width].astype(F32)
    v_weight_grad = second_sum[:, split + head_width :].astype(F32)
    router_grad = small[:experts_all].T
    post_norm_grad, input_norm_grad, gains = small[experts_all : experts_all + 3]
    return (
        block_out,
        input_grad,
        input_norm_grad,
        q_weight_grad,
        k_weight_grad,
        v_weight_grad,
        gains[:head_width],
        gains[head_width : 2 * head_width],
        o_weight_grad,
        post_norm_grad,
        router_grad,
        gate_grad,
        up_grad,
        down_grad,
    )


def solution(mesh):
    in_specs = (
        P("ep", None),
        P(),
        P(None, "tp"),
        P(None, "tp"),
        P(None, "tp"),
        P(),
        P(),
        P("tp", None),
        P(),
        P(),
        P("ep", None, "tp"),
        P("ep", None, "tp"),
        P("ep", "tp", None),
        P("ep", None),
        P(),
        P("ep", None),
    )
    out_specs = (
        P("ep", "tp"),
        P("ep", None),
        P(),
        P(None, "tp"),
        P(None, "tp"),
        P(None, "tp"),
        P(),
        P(),
        P("tp", None),
        P(),
        P(),
        P("ep", None, "tp"),
        P("ep", None, "tp"),
        P("ep", "tp", None),
    )
    return jax.shard_map(body, mesh=mesh, in_specs=in_specs, out_specs=out_specs, check_vma=False)
```

time: 1290 us -> 1020 us (0.79)
  waiting for transfers between devices: 666 us -> 364 us
  Pallas kernels: 115 us -> 205 us
  matrix products: 173 us -> 83.7 us
  blocking collectives: 81.8 us -> 0 us
  other arithmetic: 79.4 us -> 127 us
  local copies, waits for them, and re-layouts: 62.7 us -> 101 us
  starting transfers between devices: 94.7 us -> 124 us
  between operations: 16.5 us -> 3.14 us
    ppermute x24 -> x109, waiting for transfers between devices: 10.7 us -> 364 us  [the longest x97 299 us: swap(): return lax.ppermute(block, axis, [(i, i ^ mask) for i in devices])]
    psum x2 -> x0, waiting for transfers between devices: 308 us -> none  [the longest x1 191 us: body(): lax.psum(q_weight_grad.astype(jnp.bfloat16), 'ep').astype(jnp.float32)]
    reduce_scatter x2 -> x0, waiting for transfers between devices: 200 us -> none  [the longest x1 181 us: body(): lax.psum_scatter(row_grads, ('ep', 'tp'), scatter_dimension=0, tiled=True)]
    pallas_call x1 -> x6, Pallas kernels: 115 us -> 205 us  [the longest x4 151 us: expert_pass(): pl.pallas_call(expert_kernel, grid=(2 * half,), in_specs=in_specs + [pl.B...]
    dot_general x40 -> x15, matrix products: 173 us -> 83.7 us  [the longest x4 60.6 us: over_rows(): return jnp.einsum('ta,tb->ab', left, right, preferred_element_type=F32)]
    all_gather x4 -> x0, waiting for transfers between devices: 74.5 us -> none  [the longest x1 74.5 us: body(): lax.all_gather(ffn_in.astype(jnp.bfloat16), ('ep', 'tp'), axis=0, tiled=T...]
    all_to_all x2 -> x0, waiting for transfers between devices: 71.8 us -> none  [sum_rows(): lax.all_to_all(partial_rows.astype(jnp.bfloat16), 'tp', split_axis=0, con...]
    psum x1 -> x0, blocking collectives: 49.4 us -> none  [body(): lax.psum((router_grad, input_norm_grad, post_norm_grad, q_gain_grad, k_ga...]
  transfers between devices with their start and end apart: 35 -> 110, of which waited for: 9 -> 45; matrix products, arithmetic and copies ran while one was open for 23% -> 24% of each run, Pallas kernels for 0% -> 20%
where the time goes in v2:
time: 1020 us; the launch traced here: 1010 us
  waiting for transfers between devices  364 us (36%)
  Pallas kernels  205 us (20%)
  other arithmetic  127 us (12%)
  starting transfers between devices  124 us (12%)
  local copies, waits for them, and re-layouts  101 us (10%)
  matrix products  83.7 us (8%)
    ppermute x97, waiting for transfers between devices, swap(): return lax.ppermute(block, axis, [(i, i ^ mask) for i in devices])  299 us
    pallas_call x4, Pallas kernels, expert_pass(): pl.pallas_call(expert_kernel, grid=(2 * half,), in_specs=in_specs + [pl.B...  151 us
    ppermute x97, starting transfers between devices, swap(): return lax.ppermute(block, axis, [(i, i ^ mask) for i in devices])  85.1 us
    ppermute x12, waiting for transfers between devices, turn(): lax.ppermute(block, 'ep', [(i, (i + 2 * step) % count) for i in range(cou...  64.3 us
    dot_general x4, matrix products, over_rows(): return jnp.einsum('ta,tb->ab', left, right, preferred_element_type=F32)  60.6 us
    convert_element_type x27, other arithmetic, add_low(): return (kept.astype(F32) + received.astype(F32)).astype(LOW)  39.8 us
    pallas_call x1, Pallas kernels, attend_back(): pl.pallas_call(attend_back_kernel, grid_spec=pltpu.PrefetchScalarGridSpec...  35.4 us
    ppermute x12, starting transfers between devices, turn(): lax.ppermute(block, 'ep', [(i, (i + 2 * step) % count) for i in range(cou...  34.9 us
  transfers between devices with their start and end apart: 110, of which 45 were waited for; matrix products, arithmetic and copies ran while one was open for 24% of the time, Pallas kernels for 20%

profile of v2, /device:TPU:0, one launch (start us, length us, event | category | flops | bytes accessed | tf_op | source)
XLA Modules:
  0.0 1007.9 jit_solution(3617241511238588599)
XLA Ops:
  59.5 18.1 %attend.1 = (bf16[512,1024]{1,0:T(8,128)(2,1)}, f32[8,1,512]{2,1,0:T(1,128)}) custom-call(s32[6]{0:T(128)} %stack.57.place_ref, f32[512,1024]{1,0:T(8,128)} %fusion.69.q_ref, f32[1,128]{1,0:T(1,128)} %bitcast.319, f32[512,128]{1,0:T(8,128)} %get-tuple-element.448.cos_ref, f32[512,128]{1,0:T(8,128)} %get-tuple-element.364.sin_ref, ...), custom_call_target="tpu_custom_call" | custom-call | flops 4294967296 | bytes 4194304 | tf_op jit(solution)/shard_map/attend/pallas_call | solution.py:307
  101.1 19.4 %collective-permute-done.29 = bf16[256,2176]{1,0:T(8,128)(2,1)S(1)} collective-permute-done((bf16[256,2176]{1,0:T(8,128)(2,1)}, bf16[256,2176]{1,0:T(8,128)(2,1)S(1)}, u32[]{:S(2)}, u32[]{:S(2)}) %collective-permute-start.29) | collective-permute-done | bytes 1114144 | tf_op jit(solution)/shard_map/ppermute | solution.py:28
  122.6 9.5 collective-permute-done.13
  145.4 10.4 %collective-permute-done.25 = bf16[128,2048]{1,0:T(8,128)(2,1)S(1)} collective-permute-done((bf16[128,2048]{1,0:T(8,128)(2,1)S(1)}, bf16[128,2048]{1,0:T(8,128)(2,1)S(1)}, u32[]{:S(2)}, u32[]{:S(2)}) %collective-permute-start.25) | collective-permute-done | bytes 524320 | tf_op jit(solution)/shard_map/ppermute | solution.py:33
  168.1 9.3 collective-permute-done.16
  180.8 11.0 %collective-permute-done.17 = bf16[128,2048]{1,0:T(8,128)(2,1)S(1)} collective-permute-done((bf16[128,2048]{1,0:T(8,128)(2,1)S(1)}, bf16[128,2048]{1,0:T(8,128)(2,1)S(1)}, u32[]{:S(2)}, u32[]{:S(2)}) %collective-permute-start.17) | collective-permute-done | bytes 524320 | tf_op jit(solution)/shard_map/ppermute | solution.py:28
  212.4 37.6 %expert_pass.4 = (bf16[512,2048]{1,0:T(8,128)(2,1)}, bf16[512,2048]{1,0:T(8,128)(2,1)}, bf16[8,4,64,2048]{3,2,1,0:T(8,128)(2,1)}, bf16[8,4,64,2048]{3,2,1,0:T(8,...) custom-call(bf16[512,2048]{1,0:T(8,128)(2,1)} %copy-done.57, ...), custom_call_target="tpu_custom_call" | custom-call | flops 19327352832 | bytes 20971520 | tf_op jit(solution)/shard_map/expert_pass/pallas_call | solution.py:235
  277.8 10.8 %collective-permute-done.40 = bf16[128,2048]{1,0:T(8,128)(2,1)S(1)} collective-permute-done((bf16[128,2048]{1,0:T(8,128)(2,1)S(1)}, bf16[128,2048]{1,0:T(8,128)(2,1)S(1)}, u32[]{:S(2)}, u32[]{:S(2)}) %collective-permute-start.40) | collective-permute-done | bytes 524320 | tf_op jit(solution)/shard_map/ppermute | solution.py:28
  289.3 37.9 %expert_pass.5 = (bf16[512,2048]{1,0:T(8,128)(2,1)}, bf16[512,2048]{1,0:T(8,128)(2,1)}, bf16[8,4,64,2048]{3,2,1,0:T(8,128)(2,1)}, bf16[8,4,64,2048]{3,2,1,0:T(8,...) custom-call(bf16[512,2048]{1,0:T(8,128)(2,1)} %constant_dynamic-upda, ...), custom_call_target="tpu_custom_call", output_to_operand_aliasing={{2}: (10, {}), {3}: (11, {}), {4}: (12, {}), {5}: (13, {}),... | custom-call | flops 19327352832 | bytes 20971520 | tf_op jit(solution)/shard_map/expert_pass/pallas_call | solution.py:235
  339.8 38.1 %expert_pass.6 = (bf16[512,2048]{1,0:T(8,128)(2,1)}, bf16[512,2048]{1,0:T(8,128)(2,1)}, bf16[8,4,64,2048]{3,2,1,0:T(8,128)(2,1)}, bf16[8,4,64,2048]{3,2,1,0:T(8,...) custom-call(bf16[512,2048]{1,0:T(8,128)(2,1)} %pad_maximum_fusion.3., ...), custom_call_target="tpu_custom_call", output_to_operand_aliasing={{2}: (10, {}), {3}: (11, {}), {4}: (12, {}), {5}: (13, {}),... | custom-call | flops 19327352832 | bytes 20971520 | tf_op jit(solution)/shard_map/expert_pass/pallas_call | solution.py:235
  390.3 37.8 %expert_pass.7 = (bf16[512,2048]{1,0:T(8,128)(2,1)}, bf16[512,2048]{1,0:T(8,128)(2,1)}, bf16[8,4,64,2048]{3,2,1,0:T(8,128)(2,1)}, bf16[8,4,64,2048]{3,2,1,0:T(8,...) custom-call(bf16[512,2048]{1,0:T(8,128)(2,1)} %pad_maximum_fusion.4., ...), custom_call_target="tpu_custom_call", output_to_operand_aliasing={{2}: (10, {}), {3}: (11, {}), {4}: (12, {}), {5}: (13, {}),... | custom-call | flops 19327352832 | bytes 20971520 | tf_op jit(solution)/shard_map/expert_pass/pallas_call | solution.py:235
  447.0 8.6 collective-permute-start.57
  484.7 10.5 %collective-permute-start.68 = (bf16[128,2048]{1,0:T(8,128)(2,1)S(1)}, bf16[128,2048]{1,0:T(8,128)(2,1)S(1)}, u32[]{:S(2)}, u32[]{:S(2)}) collective-permute-start(bf16[128,2048]{1,0:T(8,128)(2,1)S(1)} %maximum_bitcast_fusion.3), channel_id=1, source_target_pairs={{0,16},{4,20},{8,24},{12,28},{16,0},{20,4},{24,8},{28,12},{1,17},{... | collective-permute-start | bytes 1572872 | tf_op jit(solution)/shard_map/ppermute | solution.py:33
  497.0 23.7 %collective-permute-done.68 = bf16[128,2048]{1,0:T(8,128)(2,1)S(1)} collective-permute-done((bf16[128,2048]{1,0:T(8,128)(2,1)S(1)}, bf16[128,2048]{1,0:T(8,128)(2,1)S(1)}, u32[]{:S(2)}, u32[]{:S(2)}) %collective-permute-start.68) | collective-permute-done | bytes 524320 | tf_op jit(solution)/shard_map/ppermute | solution.py:33
  523.7 13.7 %collective-permute-done.69 = bf16[128,2048]{1,0:T(8,128)(2,1)} collective-permute-done((bf16[128,2048]{1,0:T(8,128)(2,1)S(1)}, bf16[128,2048]{1,0:T(8,128)(2,1)}, u32[]{:S(2)}, u32[]{:S(2)}) %collective-permute-start.69) | collective-permute-done | bytes 524320 | tf_op jit(solution)/shard_map/ppermute | solution.py:28
  567.5 35.4 %attend_back.1 = (bf16[512,1024]{1,0:T(8,128)(2,1)}, f32[2048,128]{1,0:T(8,128)}, f32[2048,128]{1,0:T(8,128)}, f32[1,128]{1,0:T(1,128)}) custom-call(s32[6]{0:T(128)} %stack.57.place_ref, f32[512,1024]{1,0:T(8,128)} %fusion.69.q_ref, bf16[512,1024]{1,0:T(8,128)(2,1)} %convolution_convert_fusion.3.d_ref, f32[1,128]{1,0:T(1,128)} %bitcast.320, ...), custom_call_target="tpu_custom_call" | custom-call | flops 21474836480 | bytes 4194304 | tf_op jit(solution)/shard_map/attend_back/pallas_call | solution.py:401
  602.9 9.6 collective-permute-done.73
  647.1 16.6 %collective-permute-done.78 = bf16[256,2048]{1,0:T(8,128)(2,1)S(1)} collective-permute-done((bf16[256,2048]{1,0:T(8,128)(2,1)S(1)}, bf16[256,2048]{1,0:T(8,128)(2,1)S(1)}, u32[]{:S(2)}, u32[]{:S(2)}) %collective-permute-start.78) | collective-permute-done | bytes 1048608 | tf_op jit(solution)/shard_map/ppermute | solution.py:28
  668.2 20.2 %collective-permute-done.79 = bf16[128,2048]{1,0:T(8,128)(2,1)S(1)} collective-permute-done((bf16[128,2048]{1,0:T(8,128)(2,1)S(1)}, bf16[128,2048]{1,0:T(8,128)(2,1)S(1)}, u32[]{:S(2)}, u32[]{:S(2)}) %collective-permute-start.79) | collective-permute-done | bytes 524320 | tf_op jit(solution)/shard_map/ppermute | solution.py:28
  696.6 18.6 %collective-permute-done.84 = bf16[128,2048]{1,0:T(8,128)(2,1)S(1)} collective-permute-done((bf16[128,2048]{1,0:T(8,128)(2,1)S(1)}, bf16[128,2048]{1,0:T(8,128)(2,1)S(1)}, u32[]{:S(2)}, u32[]{:S(2)}) %collective-permute-start.84) | collective-permute-done | bytes 524320 | tf_op jit(solution)/shard_map/ppermute | solution.py:28
  726.0 19.0 %collective-permute-done.82 = bf16[256,512]{1,0:T(8,128)(2,1)S(1)} collective-permute-done((bf16[256,512]{1,0:T(8,128)(2,1)S(1)}, bf16[256,512]{1,0:T(8,128)(2,1)S(1)}, u32[]{:S(2)}, u32[]{:S(2)}) %collective-permute-start.82) | collective-permute-done | bytes 262176 | tf_op jit(solution)/shard_map/ppermute | solution.py:28
  759.8 20.6 %collective-permute-done.88 = bf16[256,512]{1,0:T(8,128)(2,1)S(1)} collective-permute-done((bf16[256,512]{1,0:T(8,128)(2,1)S(1)}, bf16[256,512]{1,0:T(8,128)(2,1)S(1)}, u32[]{:S(2)}, u32[]{:S(2)}) %collective-permute-start.88) | collective-permute-done | bytes 262176 | tf_op jit(solution)/shard_map/ppermute | solution.py:28
  785.1 8.6 copy.163
  797.6 15.7 %collective-permute-done.91 = bf16[256,768]{1,0:T(8,128)(2,1)S(1)} collective-permute-done((bf16[256,768]{1,0:T(8,128)(2,1)S(1)}, bf16[256,768]{1,0:T(8,128)(2,1)S(1)}, u32[]{:S(2)}, u32[]{:S(2)}) %collective-permute-start.91) | collective-permute-done | bytes 393248 | tf_op jit(solution)/shard_map/ppermute | solution.py:28
  821.9 18.6 %fusion.96 = f32[4,192,2048]{2,1,0:T(8,128)} fusion(bf16[4,192,4096]{2,1,0:T(8,128)(2,1)S(1)} %bitcast.282, bf16[4096,2048,1]{1,0,2:T(8,128)(2,1)} %bitcast.251), kind=kOutput, calls=%fused_computation.309 | convolution fusion | flops 12884901888 | bytes 29360128 | tf_op jit(solution)/shard_map/ta,tb->ab/dot_general | solution.py:649
  840.5 8.7 copy.161
  855.4 13.3 %collective-permute-done.93 = bf16[1024,512]{1,0:T(8,128)(2,1)} collective-permute-done((bf16[1024,512]{1,0:T(8,128)(2,1)S(1)}, bf16[1024,512]{1,0:T(8,128)(2,1)}, u32[]{:S(2)}, u32[]{:S(2)}) %collective-permute-start.93) | collective-permute-done | bytes 1048608 | tf_op jit(solution)/shard_map/ppermute | solution.py:28
  871.9 18.2 %collective-permute-done.96 = bf16[256,2048]{1,0:T(8,128)(2,1)S(1)} collective-permute-done((bf16[256,2048]{1,0:T(8,128)(2,1)S(1)}, bf16[256,2048]{1,0:T(8,128)(2,1)S(1)}, u32[]{:S(2)}, u32[]{:S(2)}) %collective-permute-start.96) | collective-permute-done | bytes 1048608 | tf_op jit(solution)/shard_map/ppermute | solution.py:28
  895.6 18.6 %convolution_bitcast_fusion.1 = f32[4,2048,192]{1,2,0:T(8,128)} fusion(bf16[4096,2048,1]{1,0,2:T(8,128)(2,1)} %bitcast.246, bf16[4,192,4096]{2,1,0:T(8,128)(2,1)S(1)} %bitcast.279), kind=kOutput, calls=%fused_computation.16 | convolution fusion | flops 12884901888 | bytes 29360128 | tf_op jit(solution)/shard_map/ta,tb->ab/dot_general | solution.py:649
  934.1 17.1 %collective-permute-done.100 = bf16[128,2048]{1,0:T(8,128)(2,1)} collective-permute-done((bf16[128,2048]{1,0:T(8,128)(2,1)}, bf16[128,2048]{1,0:T(8,128)(2,1)}, u32[]{:S(2)}, u32[]{:S(2)}) %collective-permute-start.100) | collective-permute-done | bytes 524320 | tf_op jit(solution)/shard_map/ppermute | solution.py:33
  960.9 9.7 collective-permute-start.107
  970.6 20.3 %convolution_bitcast_fusion = f32[4,2048,192]{1,2,0:T(8,128)} fusion(bf16[4096,2048,1]{1,0,2:T(8,128)(2,1)} %bitcast.247, bf16[4,192,4096]{2,1,0:T(8,128)(2,1)} %bitcast.283), kind=kOutput, calls=%fused_computation.15 | convolution fusion | flops 12884901888 | bytes 29360128 | tf_op jit(solution)/shard_map/ta,tb->ab/dot_general | solution.py:649
  (606 shorter events, 419.8 us)
Async XLA Ops:
  3.6 43.9 %collective-permute-start.7 = (bf16[128,2176]{1,0:T(8,128)(2,1)}, bf16[128,2176]{1,0:T(8,128)(2,1)}, u32[]{:S(2)}, u32[]{:S(2)}) collective-permute-start(bf16[128,2176]{1,0:T(8,128)(2,1)} %pad_maximum_fusion.16), channel_id=1, source_target_pairs={{0,24},{4,28},{8,0},{12,4},{16,8},{20,12},{24,16},{28,20},{1,25},{... | collective-permute-start | bytes 1671176 | tf_op jit(solution)/shard_map/ppermute | solution.py:33
  91.7 43.2 %collective-permute-start.14 = (bf16[128,2176]{1,0:T(8,128)(2,1)}, bf16[128,2176]{1,0:T(8,128)(2,1)S(1)}, u32[]{:S(2)}, u32[]{:S(2)}) collective-permute-start(bf16[128,2176]{1,0:T(8,128)(2,1)} %pad_maximum_fusion.16), channel_id=1, source_target_pairs={{0,16},{4,20},{8,24},{12,28},{16,0},{20,4},{24,8},{28,12},{1,17},{... | collective-permute-start | bytes 1671176 | tf_op jit(solution)/shard_map/ppermute | solution.py:33
  94.4 43.6 %collective-permute-start.30 = (bf16[256,2176]{1,0:T(8,128)(2,1)}, bf16[256,2176]{1,0:T(8,128)(2,1)S(1)}, u32[]{:S(2)}, u32[]{:S(2)}) collective-permute-start(bf16[256,2176]{1,0:T(8,128)(2,1)} %pad_maximum_fusion.11), channel_id=1, source_target_pairs={{0,2},{1,3},{2,0},{3,1},{4,6},{5,7},{6,4},{7,5},{8,10},{9,11},{10,... | collective-permute-start | bytes 3342344 | tf_op jit(solution)/shard_map/ppermute | solution.py:28
  142.9 52.1 %collective-permute-start.28 = (bf16[128,2048]{1,0:T(8,128)(2,1)S(1)}, bf16[128,2048]{1,0:T(8,128)(2,1)S(1)}, u32[]{:S(2)}, u32[]{:S(2)}) collective-permute-start(bf16[128,2048]{1,0:T(8,128)(2,1)S(1)} %multiply_convert_fusion.1), channel_id=1, source_target_pairs={{0,16},{4,20},{8,24},{12,28},{16,0},{20,4},{24,8},{28,12},{1,17},{... | collective-permute-start | bytes 1572872 | tf_op jit(solution)/shard_map/ppermute | solution.py:33
  197.1 76.5 %collective-permute-start.36 = (bf16[1024,2176]{1,0:T(8,128)(2,1)}, bf16[1024,2176]{1,0:T(8,128)(2,1)}, u32[]{:S(2)}, u32[]{:S(2)}) collective-permute-start(bf16[1024,2176]{1,0:T(8,128)(2,1)} %constant_dynamic-update-slice_fusion.12), channel_id=1, source_target_pairs={{0,1},{1,0},{2,3},{3,2},{4,5},{5,4},{6,7},{7,6},{8,9},{9,8},{10,11... | collective-permute-start | bytes 13369352 | tf_op jit(solution)/shard_map/ppermute | solution.py:28
  208.4 46.2 %collective-permute-start.38 = (bf16[64,2176]{1,0:T(8,128)(2,1)S(1)}, bf16[64,2176]{1,0:T(8,128)(2,1)S(1)}, u32[]{:S(2)}, u32[]{:S(2)}) collective-permute-start(bf16[64,2176]{1,0:T(8,128)(2,1)S(1)} %get-tuple-element.410), channel_id=1, source_target_pairs={{0,4},{4,0},{8,12},{12,8},{16,20},{20,16},{24,28},{28,24},{1,5},{5... | collective-permute-start | bytes 835592 | tf_op jit(solution)/shard_map/ppermute | solution.py:28
  211.6 41.4 %collective-permute-start.34 = (bf16[64,2048]{1,0:T(8,128)(2,1)S(1)}, bf16[64,2048]{1,0:T(8,128)(2,1)}, u32[]{:S(2)}, u32[]{:S(2)}) collective-permute-start(bf16[64,2048]{1,0:T(8,128)(2,1)S(1)} %get-tuple-element.425), channel_id=1, source_target_pairs={{0,2},{1,3},{2,0},{3,1},{4,6},{5,7},{6,4},{7,5},{8,10},{9,11},{10,... | collective-permute-start | bytes 786440 | tf_op jit(solution)/shard_map/ppermute | solution.py:28
  212.3 61.3 %collective-permute-start.31 = (bf16[512,2048]{1,0:T(8,128)(2,1)}, bf16[512,2048]{1,0:T(8,128)(2,1)}, u32[]{:S(2)}, u32[]{:S(2)}) collective-permute-start(bf16[512,2048]{1,0:T(8,128)(2,1)} %constant_dynamic-update-slice_fusion.own_ref), channel_id=1, source_target_pairs={{0,1},{1,0},{2,3},{3,2},{4,5},{5,4},{6,7},{7,6},{8,9},{9,8},{10,11... | collective-permute-start | bytes 6291464 | tf_op jit(solution)/shard_map/ppermute | solution.py:28
  274.6 58.3 %collective-permute-start.44 = (bf16[512,2048]{1,0:T(8,128)(2,1)}, bf16[512,2048]{1,0:T(8,128)(2,1)}, u32[]{:S(2)}, u32[]{:S(2)}) collective-permute-start(bf16[512,2048]{1,0:T(8,128)(2,1)} %get-tuple-element.242), channel_id=1, source_target_pairs={{0,1},{1,0},{2,3},{3,2},{4,5},{5,4},{6,7},{7,6},{8,9},{9,8},{10,11... | collective-permute-start | bytes 6291464 | tf_op jit(solution)/shard_map/ppermute | solution.py:28
  274.6 55.4 %collective-permute-start.42 = (bf16[128,2176]{1,0:T(8,128)(2,1)S(1)}, bf16[128,2176]{1,0:T(8,128)(2,1)}, u32[]{:S(2)}, u32[]{:S(2)}) collective-permute-start(bf16[128,2176]{1,0:T(8,128)(2,1)S(1)} %pad_maximum_fusion.22), channel_id=1, source_target_pairs={{0,4},{4,0},{8,12},{12,8},{16,20},{20,16},{24,28},{28,24},{1,5},{5... | collective-permute-start | bytes 1671176 | tf_op jit(solution)/shard_map/ppermute | solution.py:28
  275.7 54.3 %collective-permute-start.43 = (bf16[128,2176]{1,0:T(8,128)(2,1)S(1)}, bf16[128,2176]{1,0:T(8,128)(2,1)}, u32[]{:S(2)}, u32[]{:S(2)}) collective-permute-start(bf16[128,2176]{1,0:T(8,128)(2,1)S(1)} %pad_maximum_fusion.23), channel_id=1, source_target_pairs={{0,2},{1,3},{2,0},{3,1},{4,6},{5,7},{6,4},{7,5},{8,10},{9,11},{10,... | collective-permute-start | bytes 1671176 | tf_op jit(solution)/shard_map/ppermute | solution.py:28
  277.0 50.2 %collective-permute-start.41 = (bf16[128,2048]{1,0:T(8,128)(2,1)S(1)}, bf16[128,2048]{1,0:T(8,128)(2,1)}, u32[]{:S(2)}, u32[]{:S(2)}) collective-permute-start(bf16[128,2048]{1,0:T(8,128)(2,1)S(1)} %pad_maximum_fusion.35), channel_id=1, source_target_pairs={{0,2},{1,3},{2,0},{3,1},{4,6},{5,7},{6,4},{7,5},{8,10},{9,11},{10,... | collective-permute-start | bytes 1572872 | tf_op jit(solution)/shard_map/ppermute | solution.py:28
  288.5 47.0 %collective-permute-start.39 = (bf16[512,2048]{1,0:T(8,128)(2,1)}, bf16[512,2048]{1,0:T(8,128)(2,1)}, u32[]{:S(2)}, u32[]{:S(2)}) collective-permute-start(bf16[512,2048]{1,0:T(8,128)(2,1)} %pad_maximum_fusion.3.own_ref), channel_id=1, source_target_pairs={{0,1},{1,0},{2,3},{3,2},{4,5},{5,4},{6,7},{7,6},{8,9},{9,8},{10,11... | collective-permute-start | bytes 6291464 | tf_op jit(solution)/shard_map/ppermute | solution.py:28
  336.5 41.4 %collective-permute-start.49 = (bf16[128,2048]{1,0:T(8,128)(2,1)S(1)}, bf16[128,2048]{1,0:T(8,128)(2,1)S(1)}, u32[]{:S(2)}, u32[]{:S(2)}) collective-permute-start(bf16[128,2048]{1,0:T(8,128)(2,1)S(1)} %slice.331), channel_id=1, source_target_pairs={{0,2},{1,3},{2,0},{3,1},{4,6},{5,7},{6,4},{7,5},{8,10},{9,11},{10,... | collective-permute-start | bytes 1572872 | tf_op jit(solution)/shard_map/ppermute | solution.py:28
  339.3 41.1 %collective-permute-start.47 = (bf16[512,2048]{1,0:T(8,128)(2,1)}, bf16[512,2048]{1,0:T(8,128)(2,1)}, u32[]{:S(2)}, u32[]{:S(2)}) collective-permute-start(bf16[512,2048]{1,0:T(8,128)(2,1)} %get-tuple-element.265), channel_id=1, source_target_pairs={{0,1},{1,0},{2,3},{3,2},{4,5},{5,4},{6,7},{7,6},{8,9},{9,8},{10,11... | collective-permute-start | bytes 6291464 | tf_op jit(solution)/shard_map/ppermute | solution.py:28
  339.3 43.7 %collective-permute-start.46 = (bf16[512,2176]{1,0:T(8,128)(2,1)}, bf16[512,2176]{1,0:T(8,128)(2,1)}, u32[]{:S(2)}, u32[]{:S(2)}) collective-permute-start(bf16[512,2176]{1,0:T(8,128)(2,1)} %pad_maximum_fusion.2), channel_id=1, source_target_pairs={{0,1},{1,0},{2,3},{3,2},{4,5},{5,4},{6,7},{7,6},{8,9},{9,8},{10,11... | collective-permute-start | bytes 6684680 | tf_op jit(solution)/shard_map/ppermute | solution.py:28
  339.8 43.2 %collective-permute-start.45 = (bf16[512,2048]{1,0:T(8,128)(2,1)}, bf16[512,2048]{1,0:T(8,128)(2,1)}, u32[]{:S(2)}, u32[]{:S(2)}) collective-permute-start(bf16[512,2048]{1,0:T(8,128)(2,1)} %pad_maximum_fusion.4.own_ref), channel_id=1, source_target_pairs={{0,1},{1,0},{2,3},{3,2},{4,5},{5,4},{6,7},{7,6},{8,9},{9,8},{10,11... | collective-permute-start | bytes 6291464 | tf_op jit(solution)/shard_map/ppermute | solution.py:28
  383.8 44.3 %collective-permute-start.54 = (bf16[64,2048]{1,0:T(8,128)(2,1)}, bf16[64,2048]{1,0:T(8,128)(2,1)}, u32[]{:S(2)}, u32[]{:S(2)}) collective-permute-start(bf16[64,2048]{1,0:T(8,128)(2,1)} %slice.341), channel_id=1, source_target_pairs={{0,4},{4,0},{8,12},{12,8},{16,20},{20,16},{24,28},{28,24},{1,5},{5... | collective-permute-start | bytes 786440 | tf_op jit(solution)/shard_map/ppermute | solution.py:28
  386.0 43.1 %collective-permute-start.53 = (bf16[64,2048]{1,0:T(8,128)(2,1)}, bf16[64,2048]{1,0:T(8,128)(2,1)S(1)}, u32[]{:S(2)}, u32[]{:S(2)}) collective-permute-start(bf16[64,2048]{1,0:T(8,128)(2,1)} %slice.339), channel_id=1, source_target_pairs={{0,2},{1,3},{2,0},{3,1},{4,6},{5,7},{6,4},{7,5},{8,10},{9,11},{10,... | collective-permute-start | bytes 786440 | tf_op jit(solution)/shard_map/ppermute | solution.py:28
  387.6 41.6 %collective-permute-start.52 = (bf16[128,2048]{1,0:T(8,128)(2,1)}, bf16[128,2048]{1,0:T(8,128)(2,1)}, u32[]{:S(2)}, u32[]{:S(2)}) collective-permute-start(bf16[128,2048]{1,0:T(8,128)(2,1)} %slice.337), channel_id=1, source_target_pairs={{0,2},{1,3},{2,0},{3,1},{4,6},{5,7},{6,4},{7,5},{8,10},{9,11},{10,... | collective-permute-start | bytes 1572872 | tf_op jit(solution)/shard_map/ppermute | solution.py:28
  389.7 41.0 %collective-permute-start.51 = (bf16[128,2048]{1,0:T(8,128)(2,1)}, bf16[128,2048]{1,0:T(8,128)(2,1)}, u32[]{:S(2)}, u32[]{:S(2)}) collective-permute-start(bf16[128,2048]{1,0:T(8,128)(2,1)} %slice.335), channel_id=1, source_target_pairs={{0,4},{4,0},{8,12},{12,8},{16,20},{20,16},{24,28},{28,24},{1,5},{5... | collective-permute-start | bytes 1572872 | tf_op jit(solution)/shard_map/ppermute | solution.py:28
  390.3 41.6 %collective-permute-start.50 = (bf16[512,2048]{1,0:T(8,128)(2,1)}, bf16[512,2048]{1,0:T(8,128)(2,1)}, u32[]{:S(2)}, u32[]{:S(2)}) collective-permute-start(bf16[512,2048]{1,0:T(8,128)(2,1)} %get-tuple-element.289), channel_id=1, source_target_pairs={{0,1},{1,0},{2,3},{3,2},{4,5},{5,4},{6,7},{7,6},{8,9},{9,8},{10,11... | collective-permute-start | bytes 6291464 | tf_op jit(solution)/shard_map/ppermute | solution.py:28
  447.0 48.2 %collective-permute-start.57 = (bf16[128,2048]{1,0:T(8,128)(2,1)S(1)}, bf16[128,2048]{1,0:T(8,128)(2,1)S(1)}, u32[]{:S(2)}, u32[]{:S(2)}) collective-permute-start(bf16[128,2048]{1,0:T(8,128)(2,1)S(1)} %maximum_bitcast_fusion.1), channel_id=1, source_target_pairs={{0,8},{4,12},{8,16},{12,20},{16,24},{20,28},{24,0},{28,4},{1,9},{5... | collective-permute-start | bytes 1572872 | tf_op jit(solution)/shard_map/ppermute | solution.py:33
  564.5 48.0 %collective-permute-start.73 = (bf16[512,2048]{1,0:T(8,128)(2,1)}, bf16[512,2048]{1,0:T(8,128)(2,1)}, u32[]{:S(2)}, u32[]{:S(2)}) collective-permute-start(bf16[512,2048]{1,0:T(8,128)(2,1)} %slice.365), channel_id=1, source_target_pairs={{0,2},{1,3},{2,0},{3,1},{4,6},{5,7},{6,4},{7,5},{8,10},{9,11},{10,... | collective-permute-start | bytes 6291464 | tf_op jit(solution)/shard_map/ppermute | solution.py:28
  566.6 50.3 %collective-permute-start.72 = (bf16[512,2048]{1,0:T(8,128)(2,1)}, bf16[512,2048]{1,0:T(8,128)(2,1)}, u32[]{:S(2)}, u32[]{:S(2)}) collective-permute-start(bf16[512,2048]{1,0:T(8,128)(2,1)} %dynamic-slice_bitcast_fusion), channel_id=1, source_target_pairs={{0,4},{4,0},{8,12},{12,8},{16,20},{20,16},{24,28},{28,24},{1,5},{5... | collective-permute-start | bytes 6291464 | tf_op jit(solution)/shard_map/ppermute | solution.py:28
  626.2 62.3 %collective-permute-start.80 = (bf16[2,256,2048]{2,1,0:T(8,128)(2,1)}, bf16[2,256,2048]{2,1,0:T(8,128)(2,1)}, u32[]{:S(2)}, u32[]{:S(2)}) collective-permute-start(bf16[2,256,2048]{2,1,0:T(8,128)(2,1)} %slice_bitcast_fusion), channel_id=1, source_target_pairs={{0,2},{1,3},{2,0},{3,1},{4,6},{5,7},{6,4},{7,5},{8,10},{9,11},{10,... | collective-permute-start | bytes 6291464 | tf_op jit(solution)/shard_map/ppermute | solution.py:28
  693.9 60.9 %collective-permute-start.83 = (bf16[1024,768]{1,0:T(8,128)(2,1)}, bf16[1024,768]{1,0:T(8,128)(2,1)}, u32[]{:S(2)}, u32[]{:S(2)}) collective-permute-start(bf16[1024,768]{1,0:T(8,128)(2,1)} %dynamic-slice_bitcast_fusion.1), channel_id=1, source_target_pairs={{0,4},{4,0},{8,12},{12,8},{16,20},{20,16},{24,28},{28,24},{1,5},{5... | collective-permute-start | bytes 4718600 | tf_op jit(solution)/shard_map/ppermute | solution.py:28
  756.6 56.7 %collective-permute-start.92 = (bf16[512,2048]{1,0:T(8,128)(2,1)}, bf16[512,2048]{1,0:T(8,128)(2,1)}, u32[]{:S(2)}, u32[]{:S(2)}) collective-permute-start(bf16[512,2048]{1,0:T(8,128)(2,1)} %pad_maximum_fusion.6), channel_id=1, source_target_pairs={{0,4},{4,0},{8,12},{12,8},{16,20},{20,16},{24,28},{28,24},{1,5},{5... | collective-permute-start | bytes 6291464 | tf_op jit(solution)/shard_map/ppermute | solution.py:28
  819.9 50.2 %collective-permute-start.97 = (bf16[256,2048]{1,0:T(8,128)(2,1)}, bf16[256,2048]{1,0:T(8,128)(2,1)}, u32[]{:S(2)}, u32[]{:S(2)}) collective-permute-start(bf16[256,2048]{1,0:T(8,128)(2,1)} %slice.379), channel_id=1, source_target_pairs={{0,4},{4,0},{8,12},{12,8},{16,20},{20,16},{24,28},{28,24},{1,5},{5... | collective-permute-start | bytes 3145736 | tf_op jit(solution)/shard_map/ppermute | solution.py:28
  820.4 48.3 %collective-permute-start.93 = (bf16[1024,512]{1,0:T(8,128)(2,1)S(1)}, bf16[1024,512]{1,0:T(8,128)(2,1)}, u32[]{:S(2)}, u32[]{:S(2)}) collective-permute-start(bf16[1024,512]{1,0:T(8,128)(2,1)S(1)} %pad_maximum_fusion.14), channel_id=1, source_target_pairs={{0,4},{4,0},{8,12},{12,8},{16,20},{20,16},{24,28},{28,24},{1,5},{5... | collective-permute-start | bytes 3145736 | tf_op jit(solution)/shard_map/ppermute | solution.py:28
  849.2 44.6 %collective-permute-start.101 = (bf16[128,2048]{1,0:T(8,128)(2,1)S(1)}, bf16[128,2048]{1,0:T(8,128)(2,1)S(1)}, u32[]{:S(2)}, u32[]{:S(2)}) collective-permute-start(bf16[128,2048]{1,0:T(8,128)(2,1)S(1)} %copy-done.33), channel_id=1, source_target_pairs={{0,2},{1,3},{2,0},{3,1},{4,6},{5,7},{6,4},{7,5},{8,10},{9,11},{10,... | collective-permute-start | bytes 1572872 | tf_op jit(solution)/shard_map/ppermute | solution.py:28
  931.5 65.8 %collective-permute-start.108 = (bf16[1024,768]{1,0:T(8,128)(2,1)}, bf16[1024,768]{1,0:T(8,128)(2,1)}, u32[]{:S(2)}, u32[]{:S(2)}) collective-permute-start(bf16[1024,768]{1,0:T(8,128)(2,1)} %pad_maximum_fusion.9), channel_id=1, source_target_pairs={{0,4},{4,0},{8,12},{12,8},{16,20},{20,16},{24,28},{28,24},{1,5},{5... | collective-permute-start | bytes 4718600 | tf_op jit(solution)/shard_map/ppermute | solution.py:28
  (166 other events, 2449.5 us)

commit v3 on v2

--- a/solution.py
+++ b/solution.py
@@ -1,3 +1,5 @@
+import functools
+
 import jax
 import jax.numpy as jnp
 from jax import lax
@@ -37,51 +39,76 @@
     return (kept.astype(F32) + received.astype(F32)).astype(LOW)
 
 
-def tie(*values):
-    return lax.optimization_barrier(values)
-
-
-def paired(block, axis, mask):
-    return jnp.concatenate([block, swap(block, axis, mask)], axis=0)
+def halves(block):
+    size = block.shape[0] // 2
+    return block[:size], block[size:]
 
 
 def spread_start(slots):
     half = slots[0].shape[0] // 2
     first = jnp.concatenate([rows[:half] for rows in slots], axis=0)
     second = jnp.concatenate([rows[half:] for rows in slots], axis=0)
-    return paired(first, "tp", 2), paired(second, "ep", 1)
-
-
-def spread_next(first, second):
-    return jnp.concatenate([paired(first, "ep", 1), paired(second, "tp", 2)], axis=0)
-
-
-def halves(block):
-    size = block.shape[0] // 2
-    return block[:size], block[size:]
-
-
-def fold(block, axis, mask):
+    sends = [(first, "tp", 2), (second, "ep", 1)]
+    return sends, lambda a, b: (jnp.concatenate([first, a]), jnp.concatenate([second, b]))
+
+
+def spread_next(pair):
+    first, second = pair
+    sends = [(first, "ep", 1), (second, "tp", 2)]
+    return sends, lambda a, b: jnp.concatenate([first, a, second, b])
+
+
+def spread_last(own):
+    return [(own, "tp", 1)], lambda a: a
+
+
+def collect_start(kept, sent):
+    return [(sent, "tp", 1)], lambda a: halves(add_low(kept, a))
+
+
+def collect_both(pair, first_link, second_link):
+    (first, first_sent), (second, second_sent) = halves(pair[0]), halves(pair[1])
+    sends = [(first_sent, *first_link), (second_sent, *second_link)]
+    return sends, lambda a, b: (add_low(first, a), add_low(second, b))
+
+
+def collect_next(pair):
+    return collect_both(pair, ("ep", 1), ("tp", 2))
+
+
+def collect_last(pair):
+    return collect_both(pair, ("tp", 2), ("ep", 1))
+
+
+def fold_one(block, axis, mask):
     kept, sent = halves(block)
-    return add_low(kept, swap(sent, axis, mask))
+    return [(sent, axis, mask)], lambda a: add_low(kept, a)
 
 
 def fold_inner(block, axis, mask):
     parts = block.reshape(2, 2, -1, block.shape[1])
-    kept = add_low(parts[:, 0], swap(parts[:, 1], axis, mask))
-    return kept.reshape(-1, block.shape[1])
-
-
-def collect_start(kept, sent):
-    return halves(add_low(kept, swap(sent, "tp", 1)))
-
-
-def collect_next(first, second):
-    return fold(first, "ep", 1), fold(second, "tp", 2)
-
-
-def collect_last(first, second):
-    return fold(first, "tp", 2), fold(second, "ep", 1)
+    kept, sent = parts[:, 0], parts[:, 1]
+    return [(sent, axis, mask)], lambda a: add_low(kept, a).reshape(-1, block.shape[1])
+
+
+def tie(*values):
+    return lax.optimization_barrier(values)
+
+
+def now(stage):
+    return stage[1](*[swap(x, axis, mask) for x, axis, mask in stage[0]])
+
+
+def step(stages, compute=None, values=()):
+    sends = [[send[0] for send in stage[0]] for stage in stages]
+    sends, values = lax.optimization_barrier((sends, values))
+    received = [
+        [swap(x, axis, mask) for x, (_, axis, mask) in zip(blocks, stage[0])]
+        for blocks, stage in zip(sends, stages)
+    ]
+    result = compute(*values) if compute is not None else values
+    received, result = lax.optimization_barrier((received, result))
+    return [stage[1](*blocks) for stage, blocks in zip(stages, received)], result
 
 
 def slot_rows(first, second, count):
@@ -100,24 +127,35 @@
 def halve_sum(block, mask):
     bit = lax.axis_index("ep") // mask % 2
     parts = block.reshape(2, -1, block.shape[1])
-    return add_low(pick(parts, bit), swap(pick(parts, 1 - bit), "ep", mask))
+    kept, sent = pick(parts, bit), pick(parts, 1 - bit)
+    return [(sent, "ep", mask)], lambda a: add_low(kept, a)
 
 
 def double(block, mask):
     bit = lax.axis_index("ep") // mask % 2
-    other = swap(block, "ep", mask)
-    low = jnp.where(bit == 0, block, other)
-    high = jnp.where(bit == 0, other, block)
-    return jnp.concatenate([low, high], axis=0)
-
-
-def sum_all(values):
-    for axis in ("tp", "ep"):
-        mask = 1
-        while mask < lax.axis_size(axis):
-            values = values + swap(values, axis, mask)
-            mask *= 2
+
+    def join(other):
+        low = jnp.where(bit == 0, block, other)
+        high = jnp.where(bit == 0, other, block)
+        return jnp.concatenate([low, high], axis=0)
+
+    return [(block, "ep", mask)], join
+
+
+def sum_axis(values, axis):
+    mask = 1
+    while mask < lax.axis_size(axis):
+        values = values + swap(values, axis, mask)
+        mask *= 2
     return values
+
+
+def sum_tp(values):
+    return sum_axis(values, "tp")
+
+
+def sum_over_ep(values):
+    return sum_axis(values, "ep")
 
 
 def expert_kernel(
@@ -229,21 +267,23 @@
         placed(wide, first, at),
         placed(wide, second, at),
     ] + [whole(array) for array in fixed]
-    aliases = {len(in_specs) + n: 2 + n for n in range(len(kept))}
+    loose = 4 if slots_all > CHUNKS else 2
+    aliases = {len(in_specs) + n: loose + n for n in range(len(kept))}
     part = jax.ShapeDtypeStruct((count, model_width), LOW)
     place = jax.ShapeDtypeStruct((groups, slots_all, unit, model_width), LOW)
     return pl.pallas_call(
         expert_kernel,
         grid=(2 * half,),
         in_specs=in_specs + [pl.BlockSpec(memory_space=pl.ANY)] * len(kept),
-        out_specs=[
-            rows_spec(first),
-            rows_spec(second),
-            placed(model_width, first, chunk),
-            placed(model_width, second, chunk),
-        ]
+        out_specs=[rows_spec(first), rows_spec(second)]
+        + (
+            [rows_spec(first), rows_spec(second)]
+            if loose == 4
+            else [placed(model_width, first, chunk), placed(model_width, second, chunk)]
+        )
         + [placed(size, every, chunk) for size in columns],
-        out_shape=[part, part, place, place]
+        out_shape=[part, part]
+        + ([part, part] if loose == 4 else [place, place])
         + [jax.ShapeDtypeStruct((2 * groups, slots_all, unit, size), LOW) for size in columns],
         input_output_aliases=aliases,
         compiler_params=pltpu.CompilerParams(vmem_limit_bytes=VMEM_LIMIT),
@@ -503,10 +543,10 @@
             for p in range(c * per_chunk, (c + 1) * per_chunk)
         ]
 
-    wide_first = spread_start(fetch(wide_rows, (0,)))
     large = slots_all > CHUNKS
-    near_groups = ((1,), (2,)) if large else ((1, 2),)
-    wide_near = [fetch(wide_rows, group) for group in near_groups]
+    groups = ((0,), (1,), (2,), (3,)) if large else ((0,), (1, 2), (3,))
+    wide_first = now(spread_start(fetch(wide_rows, groups[0])))
+    wide_near = [fetch(wide_rows, group) for group in groups[1:-1]]
 
     x_full = block_in.astype(F32)
     attn_low = rms_scale(x_full, input_norm).astype(LOW)
@@ -527,19 +567,18 @@
 
     k_rot, k_back = jax.vjp(key_path, k_lin, k_gain)
     pair = jnp.concatenate([k_rot.astype(LOW), v_low], axis=1)
-    pair, *wide_first = tie(pair, *wide_first)
+    pair, wide_first = tie(pair, wide_first)
     pairs = [pair] + [swap(pair, "ep", d) for d in range(1, SPAN)]
-    wide_first = spread_next(*wide_first)
+    wide_first = now(spread_next(wide_first))
     q_lin = jnp.dot(attn_low, q_weight, preferred_element_type=F32)
-    width_own = local_experts * hidden_width
-    gate_cat = expert_gate.transpose(1, 0, 2).reshape(-1, width_own)
-    up_cat = expert_up.transpose(1, 0, 2).reshape(-1, width_own)
+    gate_cat = expert_gate.transpose(1, 0, 2).reshape(-1, width)
+    up_cat = expert_up.transpose(1, 0, 2).reshape(-1, width)
     gate_cat, up_cat, q_lin, wide_first, wide_rows, pairs, wide_near = tie(
         gate_cat, up_cat, q_lin, wide_first, wide_rows, pairs, wide_near
     )
-    wide_far = fetch(wide_rows, (3,))
-    wide_near = [spread_start(group) for group in wide_near]
-    wide_first_other = swap(wide_first, "tp", 1)
+    wide_far = fetch(wide_rows, groups[-1])
+    wide_near = [now(spread_start(group)) for group in wide_near]
+    wide_first_other = now(spread_last(wide_first))
     k_all = jnp.concatenate([p[:, :head_width] for p in pairs], axis=0)
     v_all = jnp.concatenate([p[:, head_width:] for p in pairs], axis=0)
     place = jnp.stack(
@@ -548,147 +587,147 @@
     gain_row = q_gain.reshape(1, -1)
     o_low, inverse = attend(place, q_lin, gain_row, cos, sin, k_all, v_all.T)
     o_low, wide_first_other, wide_near = tie(o_low, wide_first_other, wide_near)
-    wide_near = [spread_next(*group) for group in wide_near]
+    wide_near = [now(spread_next(group)) for group in wide_near]
     head_part = jnp.dot(o_low, o_weight, preferred_element_type=F32)
     x_mid = my_rows(x_full) + sum_rows(head_part)
     ffn_in, post_norm_back = jax.vjp(rms_scale, x_mid, post_norm)
     ffn_low = ffn_in.astype(LOW)
-    ffn_low, *wide_far = tie(ffn_low, *wide_far)
+    ffn_low, wide_far = tie(ffn_low, wide_far)
 
     own_expert = ep_rank * local_experts + jnp.arange(width, dtype=jnp.int32) // hidden_width
     select = (expert_index[:, None] == own_expert[None, :]).astype(LOW)
     down_cat = expert_down.reshape(width, -1)
     fixed = (router, router.T, select, gate_cat, up_cat, down_cat)
-    started = {c: spread_start(fetch(ffn_low, (c,))) for c in range(3)}
-    owned = {c: spread_next(*started[c]) for c in range(2)}
-    others = {0: swap(owned[0], "tp", 1)}
+    started = {c: now(spread_start(fetch(ffn_low, (c,)))) for c in range(3)}
+    owned = {c: now(spread_next(started[c])) for c in range(2)}
+    others = {0: now(spread_last(owned[0])), "wide0": wide_first_other}
+    owned["wide0"] = wide_first
+    for n, group in enumerate(wide_near):
+        owned[f"wide{n + 1}"] = group
     ffn_last = fetch(ffn_low, (3,))
 
     def shaped(*arrays):
         return [x.reshape(8, -1, unit, x.shape[1]) for x in arrays]
 
-    def land(total, chunk, first, second):
-        rows = slot_rows(first, second, per_chunk)
+    def apply_experts(at, chunk, own, other, wide_own, wide_other, *kept):
+        wide = shaped(wide_own, wide_other)
+        return expert_pass(own, other, wide, at, chunk, slots_all, fixed, kept)
+
+    def land(total, chunk, pair):
+        rows = slot_rows(*pair, per_chunk)
         for at in range(per_chunk):
             h = order[chunk * per_chunk + at]
             total = total + (rows[at] if h == 0 else turn(rows[at], h)).astype(F32)
         return total
 
     kept = []
-    folded = {}
+    back, forth = {}, {}
     for chunk in range(CHUNKS):
-        moving = []
+        names, stages = [], []
+
+        def add(store, key, stage):
+            names.append((store, key))
+            stages.append(stage)
+
         if chunk + 1 < CHUNKS:
-            moving.append(("other", chunk + 1, [owned[chunk + 1]]))
+            add(others, chunk + 1, spread_last(owned[chunk + 1]))
         if chunk + 2 < CHUNKS:
-            moving.append(("own", chunk + 2, list(started[chunk + 2])))
-        if chunk + 3 < CHUNKS:
-            moving.append(("start", chunk + 3, ffn_last))
+            add(owned, chunk + 2, spread_next(started[chunk + 2]))
         if chunk == 0:
-            for n, group in enumerate(wide_near):
-                moving.append(("other", f"near{n}", [group]))
-            moving.append(("start", "far", wide_far))
-        if chunk == 1:
-            moving.append(("own", "far", list(started["far"])))
-        if chunk == 2:
-            moving.append(("other", "far", [owned["far"]]))
-        for stage in range(3):
-            if chunk - 1 - stage >= 0:
-                moving.append((stage, chunk - 1 - stage, list(folded[chunk - 1 - stage])))
-        flat = [x for entry in moving for x in entry[2]]
-        rows_own, rows_other, *flat = tie(owned[chunk], others[chunk], *flat)
-        results = []
-        for name, c, values in moving:
-            taken, flat = flat[: len(values)], flat[len(values) :]
-            if name == "other":
-                results.append([swap(taken[0], "tp", 1)])
-            elif name == "own":
-                results.append([spread_next(*taken)])
-            elif name == "start":
-                results.append(list(spread_start(taken)))
-            else:
-                results.append(list((collect_start, collect_next, collect_last)[name](*taken)))
-        wide = (
-            (wide_first, wide_first_other),
-            (wide_near[0], others.get("near0")),
-            (wide_near[-1], others.get("near1" if large else "near0")),
-            (owned.get("far"), others.get("far")),
-        )[chunk]
-        outs = expert_pass(
-            rows_own,
-            rows_other,
-            shaped(*wide),
-            1 if chunk == 2 and not large else 0,
-            chunk,
-            slots_all,
-            fixed,
-            kept,
+            add(started, 3, spread_start(ffn_last))
+            add(started, "far", spread_start(wide_far))
+        for n, group in enumerate(groups):
+            if group == (3,) and chunk == 1:
+                add(owned, f"wide{n}", spread_next(started["far"]))
+            if chunk == group[0] - 1:
+                add(others, f"wide{n}", spread_last(owned[f"wide{n}"]))
+        for store in (back, forth) if large else (back,):
+            if chunk >= 1:
+                add(store, chunk - 1, collect_start(*store[chunk - 1]))
+            if chunk >= 2:
+                add(store, chunk - 2, collect_next(store[chunk - 2]))
+            if chunk >= 3:
+                add(store, chunk - 3, collect_last(store[chunk - 3]))
+        n, group = next((n, group) for n, group in enumerate(groups) if chunk in group)
+        wide = owned[f"wide{n}"], others[f"wide{n}"]
+        at = chunk - group[0]
+        results, outs = step(
+            stages,
+            functools.partial(apply_experts, at, chunk),
+            (owned[chunk], others[chunk], *wide, *kept),
         )
-        flat = [x for values in results for x in values]
-        grad_keep, grad_send, *flat = tie(outs[0], outs[1], *flat)
-        kept = outs[2:]
-        for (name, c, _), values in zip(moving, results):
-            taken, flat = flat[: len(values)], flat[len(values) :]
-            if name == "other":
-                others[c] = taken[0]
-            elif name == "own":
-                owned[c] = taken[0]
-            elif name == "start":
-                started[c] = taken
-            else:
-                folded[c] = taken
-        folded[chunk] = [grad_keep, grad_send]
-    d_ffn = land(jnp.zeros_like(x_mid), 0, *folded[0])
-    d_ffn = land(d_ffn, 1, *collect_last(*folded[1]))
-    d_ffn = land(d_ffn, 2, *collect_last(*collect_next(*folded[2])))
-    d_ffn = land(d_ffn, 3, *collect_last(*collect_next(*collect_start(*folded[3]))))
-    out_keep, out_send, rows_all, cotangent_rows, hidden_low, d_gate_low, d_up_low, dlog_low = [
-        x.reshape(-1, x.shape[-1]) for x in kept
+        for (store, key), value in zip(names, results):
+            store[key] = value
+        back[chunk] = outs[:2]
+        forth[chunk] = outs[2:4]
+        kept = outs[4:] if large else outs[2:]
+    rows_all, cotangent_rows, hidden_low, d_gate_low, d_up_low, dlog_low = [
+        x.reshape(-1, x.shape[-1]) for x in kept[-6:]
     ]
+    if large:
+        forth[3] = now(collect_start(*forth[3]))
+        forth[2], forth[3] = [now(collect_next(forth[c])) for c in (2, 3)]
+        for c in (1, 2, 3):
+            forth[c] = now(collect_last(forth[c]))
+        out_pair = [jnp.concatenate([forth[c][n] for c in range(CHUNKS)]) for n in range(2)]
+        out_pair, rows_all, back = tie(out_pair, rows_all, back)
+    else:
+        out_keep, out_send = [x.reshape(-1, model_width) for x in kept[:2]]
+
     def over_rows(left, right):
         return jnp.einsum("ta,tb->ab", left, right, preferred_element_type=F32)
 
     def split_experts(wide_grad):
         return wide_grad.reshape(-1, local_experts, hidden_width).transpose(1, 0, 2)
 
-    d_ffn, out_keep, out_send = tie(d_ffn, out_keep, out_send)
-    out_first, out_second = collect_start(out_keep, out_send)
-    if large:
-        out_first, out_second, rows_all, d_gate_low, d_up_low, hidden_low = tie(
-            out_first, out_second, rows_all, d_gate_low, d_up_low, hidden_low
-        )
-        router_grad_t = over_rows(dlog_low, rows_all)
-        down_grad = over_rows(hidden_low, cotangent_rows).reshape(expert_down.shape)
-        gate_grad = split_experts(over_rows(rows_all, d_gate_low))
-        up_grad = split_experts(over_rows(rows_all, d_up_low))
-        d_ffn, router_grad_t, down_grad, gate_grad, up_grad = tie(
-            d_ffn, router_grad_t, down_grad, gate_grad, up_grad
-        )
+    d_ffn = land(jnp.zeros_like(x_mid), 0, back[0])
+    (back[1], back[2], back[3]), down_grad = step(
+        [collect_last(back[1]), collect_next(back[2]), collect_start(*back[3])],
+        over_rows,
+        (hidden_low, cotangent_rows),
+    )
+    down_grad = down_grad.reshape(expert_down.shape)
+    d_ffn = land(d_ffn, 1, back[1])
+    (back[2], back[3]), gate_grad = step(
+        [collect_last(back[2]), collect_next(back[3])], over_rows, (rows_all, d_gate_low)
+    )
+    d_ffn = land(d_ffn, 2, back[2])
+    (back[3],), router_grad_t = step([collect_last(back[3])], over_rows, (dlog_low, rows_all))
+    d_ffn = land(d_ffn, 3, back[3])
+
     d_mid_norm, post_norm_grad = post_norm_back(d_ffn)
     d_mid = my_rows(out_grad).astype(F32) + d_mid_norm
-    d_mid_low = join_rows(d_mid.astype(LOW))
+    if large:
+        d_mid_low = join_rows(d_mid.astype(LOW))
+    else:
+        (out_pair,), d_mid_low = step(
+            [collect_start(out_keep, out_send)], join_rows, (d_mid.astype(LOW),)
+        )
     o_sum = jnp.einsum("tj,td->jd", o_low, d_mid_low, preferred_element_type=F32).astype(LOW)
     d_attn_low = jnp.einsum(
         "td,jd->tj", d_mid_low, o_weight, preferred_element_type=F32
     ).astype(LOW)
+    masks = ep_masks()
+    out_first, out_second = out_pair
     d_attn_low, o_sum, out_first, out_second = tie(d_attn_low, o_sum, out_first, out_second)
-    masks = ep_masks()
-    o_sum = halve_sum(o_sum, masks[0])
-    out_second = fold(out_second, "tp", 2)
+    o_sum = now(halve_sum(o_sum, masks[0]))
+    if not large:
+        out_second = now(fold_one(out_second, "tp", 2))
     dq_low, dk_all, dv_all, q_gain_grad = attend_back(
         place, q_lin, d_attn_low, gain_row, cos, sin, k_all, v_all, inverse
     )
     dq_low, dk_all, dv_all, o_sum, out_first, out_second = tie(
         dq_low, dk_all, dv_all, o_sum, out_first, out_second
     )
-    out_first = fold_inner(out_first, "tp", 2)
+    if not large:
+        out_first = now(fold_inner(out_first, "tp", 2))
     for mask in masks[1:]:
-        o_sum = halve_sum(o_sum, mask)
+        o_sum = now(halve_sum(o_sum, mask))
     split = dq_low.shape[1] // 2
     first_sum = jnp.einsum(
         "td,tj->dj", attn_low, dq_low[:, :split], preferred_element_type=F32
     ).astype(LOW)
-    first_sum = halve_sum(first_sum, masks[0])
+    first_sum = now(halve_sum(first_sum, masks[0]))
     pair_grad = jnp.concatenate([dk_all, dv_all], axis=1)
     total = pair_grad[:tokens]
     for d in range(1, SPAN):
@@ -707,21 +746,15 @@
     d_attn_in = d_attn_in + jnp.einsum("tj,dj->td", dk_low, k_weight, preferred_element_type=F32)
     d_attn_in = d_attn_in + jnp.einsum("tj,dj->td", dv_low, v_weight, preferred_element_type=F32)
 
-    first_sum, second_sum, o_sum, d_attn_in, out_first, dlog_low, hidden_low = tie(
-        first_sum, second_sum, o_sum, d_attn_in, out_first, dlog_low, hidden_low
-    )
-    second_sum = halve_sum(second_sum, masks[0])
+    second_sum = now(halve_sum(second_sum, masks[0]))
     for mask in masks[1:]:
-        first_sum = halve_sum(first_sum, mask)
+        first_sum = now(halve_sum(first_sum, mask))
     for mask in masks[:0:-1]:
-        o_sum = double(o_sum, mask)
+        o_sum = now(double(o_sum, mask))
     d_attn_rows = sum_rows(d_attn_in)
     _, input_norm_back = jax.vjp(rms_scale, my_rows(x_full), input_norm)
     d_in_norm, input_norm_grad = input_norm_back(d_attn_rows)
     input_rows = (d_mid + d_in_norm).astype(LOW)
-    if not large:
-        router_grad_t = over_rows(dlog_low, rows_all)
-        down_grad = over_rows(hidden_low, cotangent_rows).reshape(expert_down.shape)
     gains = jnp.concatenate([q_gain_grad.reshape(-1), k_gain_grad])
     small = jnp.concatenate(
         [
@@ -732,31 +765,32 @@
         ],
         axis=0,
     )
-    first_sum, second_sum, o_sum, small, input_rows, d_gate_low, d_up_low = tie(
-        first_sum, second_sum, o_sum, small, input_rows, d_gate_low, d_up_low
-    )
-    o_sum = double(o_sum, masks[0])
+    first_sum, second_sum, o_sum, small, input_rows, out_first, out_second, gate_grad = tie(
+        first_sum, second_sum, o_sum, small, input_rows, out_first, out_second, gate_grad
+    )
+    o_sum = now(double(o_sum, masks[0]))
     for mask in masks[1:]:
-        second_sum = halve_sum(second_sum, mask)
+        second_sum = now(halve_sum(second_sum, mask))
     for mask in masks[:0:-1]:
-        first_sum = double(first_sum, mask)
+        first_sum = now(double(first_sum, mask))
+    up_grad = over_rows(rows_all, d_up_low)
+    small = sum_tp(small)
+    input_grad = join_rows(input_rows)
+    first_sum, second_sum, o_sum, small, up_grad, out_first, out_second = tie(
+        first_sum, second_sum, o_sum, small, up_grad, out_first, out_second
+    )
+    first_sum = now(double(first_sum, masks[0]))
+    for mask in masks[:0:-1]:
+        second_sum = now(double(second_sum, mask))
     if not large:
-        gate_grad = split_experts(over_rows(rows_all, d_gate_low))
-    input_grad = join_rows(input_rows)
-    first_sum, second_sum, o_sum, small, d_up_low, out_first, out_second = tie(
-        first_sum, second_sum, o_sum, small, d_up_low, out_first, out_second
-    )
-    first_sum = double(first_sum, masks[0])
-    for mask in masks[:0:-1]:
-        second_sum = double(second_sum, mask)
-    out_first, out_second = fold(out_first, "ep", 1), fold(out_second, "ep", 1)
-    if not large:
-        up_grad = split_experts(over_rows(rows_all, d_up_low))
-    first_sum, second_sum, small, out_first, out_second = tie(
-        first_sum, second_sum, small, out_first, out_second
-    )
-    second_sum = double(second_sum, masks[0])
-    small = sum_all(small)
+        out_first = now(fold_one(out_first, "ep", 1))
+        out_second = now(fold_one(out_second, "ep", 1))
+    first_sum, second_sum, small, out_first, out_second, gate_grad, up_grad = tie(
+        first_sum, second_sum, small, out_first, out_second, gate_grad, up_grad
+    )
+    second_sum = now(double(second_sum, masks[0]))
+    small = sum_over_ep(small)
+    gate_grad, up_grad = split_experts(gate_grad), split_experts(up_grad)
     out_slots = slot_rows(out_first, out_second, slots_all)
     mixed = out_slots[0].astype(F32)
     for p in range(1, slots_all):

time: 1020 us -> 1010 us (level)
    dot_general x3 -> x0, local copies, waits for them, and re-layouts: 25.9 us -> none  [over_rows(): return jnp.einsum('ta,tb->ab', left, right, preferred_element_type=F32)]
    ppermute x12, starting transfers between devices: 34.9 us -> 18.4 us  [turn(): lax.ppermute(block, 'ep', [(i, (i + 2 * step) % count) for i in range(cou...]
    unnamed x190 -> x240, local copies, waits for them, and re-layouts: 27.5 us -> 42.2 us
    ppermute x97, starting transfers between devices: 85.1 us -> 98.7 us  [swap(): return lax.ppermute(block, axis, [(i, i ^ mask) for i in devices])]
    optimization_barrier x2 -> x4, local copies, waits for them, and re-layouts: 9.58 us -> 22.9 us  [tie(): return lax.optimization_barrier(values)]
    concatenate x27 -> x24, other arithmetic: 31.7 us -> 24.8 us  [the longest x7 8.77 us: spread_start(): jnp.concatenate([second, b])]
    convert_element_type x27 -> x22, other arithmetic: 39.8 us -> 38.8 us  [add_low(): return (kept.astype(F32) + received.astype(F32)).astype(LOW)]
  transfers between devices with their start and end apart: 110 -> 110, of which waited for: 45 -> 40; matrix products, arithmetic and copies ran while one was open for 24% -> 20% of each run, Pallas kernels for 20% -> 21%
where the time goes in v3:
time: 1010 us; the launch traced here: 992 us
  waiting for transfers between devices  356 us (35%)
  Pallas kernels  205 us (20%)
  starting transfers between devices  121 us (12%)
  other arithmetic  119 us (12%)
  local copies, waits for them, and re-layouts  105 us (10%)
  matrix products  83.5 us (8%)
    ppermute x97, waiting for transfers between devices, swap(): return lax.ppermute(block, axis, [(i, i ^ mask) for i in devices])  290 us
    pallas_call x4, Pallas kernels, expert_pass(): pl.pallas_call(expert_kernel, grid=(2 * half,), in_specs=in_specs + [pl.B...  151 us
    ppermute x97, starting transfers between devices, swap(): return lax.ppermute(block, axis, [(i, i ^ mask) for i in devices])  98.7 us
    dot_general x4, matrix products, over_rows(): return jnp.einsum('ta,tb->ab', left, right, preferred_element_type=F32)  60.5 us
    ppermute x12, waiting for transfers between devices, turn(): lax.ppermute(block, 'ep', [(i, (i + 2 * step) % count) for i in range(cou...  59.5 us
    unnamed x240, local copies, waits for them, and re-layouts  42.2 us
    convert_element_type x22, other arithmetic, add_low(): return (kept.astype(F32) + received.astype(F32)).astype(LOW)  38.8 us
    pallas_call x1, Pallas kernels, attend_back(): pl.pallas_call(attend_back_kernel, grid_spec=pltpu.PrefetchScalarGridSpec...  35 us
  transfers between devices with their start and end apart: 110, of which 40 were waited for; matrix products, arithmetic and copies ran while one was open for 20% of the time, Pallas kernels for 21%

profile of v3, /device:TPU:0, one launch (start us, length us, event | category | flops | bytes accessed | tf_op | source)
XLA Modules:
  0.0 992.2 jit_solution(3916369598829849277)
XLA Ops:
  30.2 7.5 collective-permute-done.2
  59.6 18.3 %attend.1 = (bf16[512,1024]{1,0:T(8,128)(2,1)}, f32[8,1,512]{2,1,0:T(1,128)}) custom-call(s32[6]{0:T(128)} %stack.57.place_ref, f32[512,1024]{1,0:T(8,128)} %fusion.72.q_ref, f32[1,128]{1,0:T(1,128)} %bitcast.314, f32[512,128]{1,0:T(8,128)} %get-tuple-element.640.cos_ref, f32[512,128]{1,0:T(8,128)} %get-tuple-element.547.sin_ref, ...), custom_call_target="tpu_custom_call" | custom-call | flops 4294967296 | bytes 4194304 | tf_op jit(solution)/shard_map/attend/pallas_call | solution.py:347
  101.0 19.4 %collective-permute-done.24 = bf16[256,2176]{1,0:T(8,128)(2,1)S(1)} collective-permute-done((bf16[256,2176]{1,0:T(8,128)(2,1)}, bf16[256,2176]{1,0:T(8,128)(2,1)S(1)}, u32[]{:S(2)}, u32[]{:S(2)}) %collective-permute-start.24) | collective-permute-done | bytes 1114144 | tf_op jit(solution)/shard_map/ppermute | solution.py:30
  123.7 8.2 collective-permute-done.13
  152.6 7.4 collective-permute-done.16
  162.1 20.3 %collective-permute-done.15 = bf16[128,2048]{1,0:T(8,128)(2,1)S(1)} collective-permute-done((bf16[128,2048]{1,0:T(8,128)(2,1)S(1)}, bf16[128,2048]{1,0:T(8,128)(2,1)S(1)}, u32[]{:S(2)}, u32[]{:S(2)}) %collective-permute-start.15) | collective-permute-done | bytes 524320 | tf_op jit(solution)/shard_map/ppermute | solution.py:35
  196.2 9.2 collective-permute-done.18
  229.3 37.7 %expert_pass.4 = (bf16[512,2048]{1,0:T(8,128)(2,1)}, bf16[512,2048]{1,0:T(8,128)(2,1)}, bf16[8,4,64,2048]{3,2,1,0:T(8,128)(2,1)}, bf16[8,4,64,2048]{3,2,1,0:T(8,...) custom-call(bf16[512,2048]{1,0:T(8,128)(2,1)} %copy-done.78, ...), custom_call_target="tpu_custom_call" | custom-call | flops 19327352832 | bytes 20971520 | tf_op jit(solution)/shard_map/expert_pass/pallas_call | solution.py:274
  280.2 37.8 %expert_pass.5 = (bf16[512,2048]{1,0:T(8,128)(2,1)}, bf16[512,2048]{1,0:T(8,128)(2,1)}, bf16[8,4,64,2048]{3,2,1,0:T(8,128)(2,1)}, bf16[8,4,64,2048]{3,2,1,0:T(8,...) custom-call(bf16[512,2048]{1,0:T(8,128)(2,1)} %constant_dynamic-upda, ...), custom_call_target="tpu_custom_call", output_to_operand_aliasing={{2}: (10, {}), {3}: (11, {}), {4}: (12, {}), {5}: (13, {}),... | custom-call | flops 19327352832 | bytes 20971520 | tf_op jit(solution)/shard_map/expert_pass/pallas_call | solution.py:274
  322.6 8.7 collective-permute-done.41
  349.9 37.8 %expert_pass.6 = (bf16[512,2048]{1,0:T(8,128)(2,1)}, bf16[512,2048]{1,0:T(8,128)(2,1)}, bf16[8,4,64,2048]{3,2,1,0:T(8,128)(2,1)}, bf16[8,4,64,2048]{3,2,1,0:T(8,...) custom-call(bf16[512,2048]{1,0:T(8,128)(2,1)} %copy-done.28, ...), custom_call_target="tpu_custom_call", output_to_operand_aliasing={{2}: (10, {}), {3}: (11, {}), {4}: (12, {}), {5}: (13, {}),... | custom-call | flops 19327352832 | bytes 20971520 | tf_op jit(solution)/shard_map/expert_pass/pallas_call | solution.py:274
  400.8 38.0 %expert_pass.7 = (bf16[512,2048]{1,0:T(8,128)(2,1)}, bf16[512,2048]{1,0:T(8,128)(2,1)}, bf16[8,4,64,2048]{3,2,1,0:T(8,128)(2,1)}, bf16[8,4,64,2048]{3,2,1,0:T(8,...) custom-call(bf16[512,2048]{1,0:T(8,128)(2,1)} %constant_dynamic-upda, ...), custom_call_target="tpu_custom_call", output_to_operand_aliasing={{2}: (10, {}), {3}: (11, {}), {4}: (12, {}), {5}: (13, {}),... | custom-call | flops 19327352832 | bytes 20971520 | tf_op jit(solution)/shard_map/expert_pass/pallas_call | solution.py:274
  451.9 19.2 %fusion.95 = f32[768,2048]{1,0:T(8,128)} fusion(bf16[4096,768]{1,0:T(8,128)(2,1)S(1)} %bitcast.256, bf16[4096,2048]{1,0:T(8,128)(2,1)} %bitcast.253), kind=kOutput, calls=%fused_computation.321 | convolution fusion | flops 12884901888 | bytes 29360128 | tf_op jit(solution)/shard_map/ta,tb->ab/dot_general | solution.py:678
  487.5 16.5 %fusion.96 = f32[2048,768]{1,0:T(8,128)} fusion(bf16[4096,2048]{1,0:T(8,128)(2,1)S(1)} %bitcast.251, bf16[4096,768]{1,0:T(8,128)(2,1)S(1)} %bitcast.259), kind=kOutput, calls=%fused_computation.322 | convolution fusion | flops 12884901888 | bytes 29360128 | tf_op jit(solution)/shard_map/ta,tb->ab/dot_general | solution.py:678
  522.4 18.1 %collective-permute-done.68 = bf16[128,2048]{1,0:T(8,128)(2,1)S(1)} collective-permute-done((bf16[128,2048]{1,0:T(8,128)(2,1)S(1)}, bf16[128,2048]{1,0:T(8,128)(2,1)S(1)}, u32[]{:S(2)}, u32[]{:S(2)}) %collective-permute-start.68) | collective-permute-done | bytes 524320 | tf_op jit(solution)/shard_map/ppermute | solution.py:35
  545.2 12.8 %collective-permute-done.70 = bf16[128,2048]{1,0:T(8,128)(2,1)} collective-permute-done((bf16[128,2048]{1,0:T(8,128)(2,1)S(1)}, bf16[128,2048]{1,0:T(8,128)(2,1)}, u32[]{:S(2)}, u32[]{:S(2)}) %collective-permute-start.70) | collective-permute-done | bytes 524320 | tf_op jit(solution)/shard_map/ppermute | solution.py:30
  573.9 6.6 fusion
  589.5 35.0 %attend_back.1 = (bf16[512,1024]{1,0:T(8,128)(2,1)}, f32[2048,128]{1,0:T(8,128)}, f32[2048,128]{1,0:T(8,128)}, f32[1,128]{1,0:T(1,128)}) custom-call(s32[6]{0:T(128)} %stack.57.place_ref, f32[512,1024]{1,0:T(8,128)} %fusion.72.q_ref, bf16[512,1024]{1,0:T(8,128)(2,1)} %convolution_convert_fusion.3.d_ref, f32[1,128]{1,0:T(1,128)} %bitcast.315, ...), custom_call_target="tpu_custom_call" | custom-call | flops 21474836480 | bytes 4194304 | tf_op jit(solution)/shard_map/attend_back/pallas_call | solution.py:441
  624.5 9.3 collective-permute-done.73
  670.9 14.0 %collective-permute-done.81 = bf16[256,2048]{1,0:T(8,128)(2,1)S(1)} collective-permute-done((bf16[256,2048]{1,0:T(8,128)(2,1)S(1)}, bf16[256,2048]{1,0:T(8,128)(2,1)S(1)}, u32[]{:S(2)}, u32[]{:S(2)}) %collective-permute-start.81) | collective-permute-done | bytes 1048608 | tf_op jit(solution)/shard_map/ppermute | solution.py:30
  692.3 18.4 %collective-permute-done.82 = bf16[128,2048]{1,0:T(8,128)(2,1)S(1)} collective-permute-done((bf16[128,2048]{1,0:T(8,128)(2,1)S(1)}, bf16[128,2048]{1,0:T(8,128)(2,1)S(1)}, u32[]{:S(2)}, u32[]{:S(2)}) %collective-permute-start.82) | collective-permute-done | bytes 524320 | tf_op jit(solution)/shard_map/ppermute | solution.py:30
  714.7 32.4 %collective-permute-done.76 = bf16[256,512]{1,0:T(8,128)(2,1)S(1)} collective-permute-done((bf16[256,512]{1,0:T(8,128)(2,1)S(1)}, bf16[256,512]{1,0:T(8,128)(2,1)S(1)}, u32[]{:S(2)}, u32[]{:S(2)}) %collective-permute-start.76) | collective-permute-done | bytes 262176 | tf_op jit(solution)/shard_map/ppermute | solution.py:30
  754.4 18.6 %collective-permute-done.84 = bf16[256,2048]{1,0:T(8,128)(2,1)S(1)} collective-permute-done((bf16[256,2048]{1,0:T(8,128)(2,1)S(1)}, bf16[256,2048]{1,0:T(8,128)(2,1)S(1)}, u32[]{:S(2)}, u32[]{:S(2)}) %collective-permute-start.84) | collective-permute-done | bytes 1048608 | tf_op jit(solution)/shard_map/ppermute | solution.py:30
  780.2 8.7 collective-permute-done.88
  791.7 21.0 %convolution_bitcast_fusion = f32[2048,768]{1,0:T(8,128)} fusion(bf16[16,4,64,2048]{3,2,1,0:T(8,128)(2,1)} %get-tuple-element.471, bf16[16,4,64,768]{3,2,1,0:T(8,128)(2,1)} %get-tuple-element.516), kind=kOutput, calls=%fused_computation.16 | convolution fusion | flops 12884901888 | bytes 29360128 | tf_op jit(solution)/shard_map/ta,tb->ab/dot_general | solution.py:678
  818.1 16.2 %collective-permute-done.91 = bf16[256,768]{1,0:T(8,128)(2,1)S(1)} collective-permute-done((bf16[256,768]{1,0:T(8,128)(2,1)S(1)}, bf16[256,768]{1,0:T(8,128)(2,1)S(1)}, u32[]{:S(2)}, u32[]{:S(2)}) %collective-permute-start.91) | collective-permute-done | bytes 393248 | tf_op jit(solution)/shard_map/ppermute | solution.py:30
  840.7 16.3 %collective-permute-done.96 = bf16[256,768]{1,0:T(8,128)(2,1)S(1)} collective-permute-done((bf16[256,768]{1,0:T(8,128)(2,1)S(1)}, bf16[256,768]{1,0:T(8,128)(2,1)S(1)}, u32[]{:S(2)}, u32[]{:S(2)}) %collective-permute-start.96) | collective-permute-done | bytes 393248 | tf_op jit(solution)/shard_map/ppermute | solution.py:30
  863.2 22.1 %collective-permute-done.98 = bf16[256,2048]{1,0:T(8,128)(2,1)S(1)} collective-permute-done((bf16[256,2048]{1,0:T(8,128)(2,1)S(1)}, bf16[256,2048]{1,0:T(8,128)(2,1)S(1)}, u32[]{:S(2)}, u32[]{:S(2)}) %collective-permute-start.98) | collective-permute-done | bytes 1048608 | tf_op jit(solution)/shard_map/ppermute | solution.py:30
  885.7 21.1 %collective-permute-done.95 = bf16[1024,512]{1,0:T(8,128)(2,1)S(1)} collective-permute-done((bf16[1024,512]{1,0:T(8,128)(2,1)S(1)}, bf16[1024,512]{1,0:T(8,128)(2,1)S(1)}, u32[]{:S(2)}, u32[]{:S(2)}) %collective-permute-start.95) | collective-permute-done | bytes 1048608 | tf_op jit(solution)/shard_map/ppermute | solution.py:30
  939.7 13.2 %collective-permute-done.106 = f32[35,2048]{1,0:T(8,128)} collective-permute-done((f32[35,2048]{1,0:T(8,128)S(1)}, f32[35,2048]{1,0:T(8,128)}, u32[]{:S(2)}, u32[]{:S(2)}) %collective-permute-start.106) | collective-permute-done | bytes 286752 | tf_op jit(solution)/shard_map/ppermute | solution.py:30
  958.7 7.9 collective-permute-done.102
  974.6 6.9 all-to-all-done
  (642 shorter events, 404.5 us)
Async XLA Ops:
  3.6 43.9 %collective-permute-start.7 = (bf16[128,2176]{1,0:T(8,128)(2,1)}, bf16[128,2176]{1,0:T(8,128)(2,1)}, u32[]{:S(2)}, u32[]{:S(2)}) collective-permute-start(bf16[128,2176]{1,0:T(8,128)(2,1)} %pad_maximum_fusion.13), channel_id=1, source_target_pairs={{0,24},{4,28},{8,0},{12,4},{16,8},{20,12},{24,16},{28,20},{1,25},{... | collective-permute-start | bytes 1671176 | tf_op jit(solution)/shard_map/ppermute | solution.py:35
  91.7 42.5 %collective-permute-start.14 = (bf16[128,2176]{1,0:T(8,128)(2,1)}, bf16[128,2176]{1,0:T(8,128)(2,1)S(1)}, u32[]{:S(2)}, u32[]{:S(2)}) collective-permute-start(bf16[128,2176]{1,0:T(8,128)(2,1)} %pad_maximum_fusion.13), channel_id=1, source_target_pairs={{0,16},{4,20},{8,24},{12,28},{16,0},{20,4},{24,8},{28,12},{1,17},{... | collective-permute-start | bytes 1671176 | tf_op jit(solution)/shard_map/ppermute | solution.py:35
  138.2 44.3 %collective-permute-start.15 = (bf16[128,2048]{1,0:T(8,128)(2,1)S(1)}, bf16[128,2048]{1,0:T(8,128)(2,1)S(1)}, u32[]{:S(2)}, u32[]{:S(2)}) collective-permute-start(bf16[128,2048]{1,0:T(8,128)(2,1)S(1)} %multiply_convert_fusion.1), channel_id=1, source_target_pairs={{0,16},{4,20},{8,24},{12,28},{16,0},{20,4},{24,8},{28,12},{1,17},{... | collective-permute-start | bytes 1572872 | tf_op jit(solution)/shard_map/ppermute | solution.py:35
  151.1 43.4 %collective-permute-start.23 = (bf16[64,2048]{1,0:T(8,128)(2,1)S(1)}, bf16[64,2048]{1,0:T(8,128)(2,1)S(1)}, u32[]{:S(2)}, u32[]{:S(2)}) collective-permute-start(bf16[64,2048]{1,0:T(8,128)(2,1)S(1)} %get-tuple-element.615), channel_id=1, source_target_pairs={{0,4},{4,0},{8,12},{12,8},{16,20},{20,16},{24,28},{28,24},{1,5},{5... | collective-permute-start | bytes 786440 | tf_op jit(solution)/shard_map/ppermute | solution.py:30
  210.0 57.1 %collective-permute-start.38 = (bf16[1024,2176]{1,0:T(8,128)(2,1)}, bf16[1024,2176]{1,0:T(8,128)(2,1)}, u32[]{:S(2)}, u32[]{:S(2)}) collective-permute-start(bf16[1024,2176]{1,0:T(8,128)(2,1)} %constant_dynamic-update-slice_fusion.6), channel_id=1, source_target_pairs={{0,1},{1,0},{2,3},{3,2},{4,5},{5,4},{6,7},{7,6},{8,9},{9,8},{10,11... | collective-permute-start | bytes 13369352 | tf_op jit(solution)/shard_map/ppermute | solution.py:30
  210.0 57.1 %collective-permute-start.31 = (bf16[512,2048]{1,0:T(8,128)(2,1)}, bf16[512,2048]{1,0:T(8,128)(2,1)}, u32[]{:S(2)}, u32[]{:S(2)}) collective-permute-start(bf16[512,2048]{1,0:T(8,128)(2,1)} %constant_dynamic-update-slice_fusion.own_ref), channel_id=1, source_target_pairs={{0,1},{1,0},{2,3},{3,2},{4,5},{5,4},{6,7},{7,6},{8,9},{9,8},{10,11... | collective-permute-start | bytes 6291464 | tf_op jit(solution)/shard_map/ppermute | solution.py:30
  226.0 41.0 %collective-permute-start.32 = (bf16[128,2048]{1,0:T(8,128)(2,1)}, bf16[128,2048]{1,0:T(8,128)(2,1)}, u32[]{:S(2)}, u32[]{:S(2)}) collective-permute-start(bf16[128,2048]{1,0:T(8,128)(2,1)} %pad_maximum_fusion.27), channel_id=1, source_target_pairs={{0,4},{4,0},{8,12},{12,8},{16,20},{20,16},{24,28},{28,24},{1,5},{5... | collective-permute-start | bytes 1572872 | tf_op jit(solution)/shard_map/ppermute | solution.py:30
  276.7 54.6 %collective-permute-start.39 = (bf16[512,2048]{1,0:T(8,128)(2,1)S(1)}, bf16[512,2048]{1,0:T(8,128)(2,1)}, u32[]{:S(2)}, u32[]{:S(2)}) collective-permute-start(bf16[512,2048]{1,0:T(8,128)(2,1)S(1)} %constant_dynamic-update-slice_fusion.16.own_ref), channel_id=1, source_target_pairs={{0,1},{1,0},{2,3},{3,2},{4,5},{5,4},{6,7},{7,6},{8,9},{9,8},{10,11... | collective-permute-start | bytes 6291464 | tf_op jit(solution)/shard_map/ppermute | solution.py:30
  276.8 54.5 %collective-permute-start.44 = (bf16[512,2048]{1,0:T(8,128)(2,1)}, bf16[512,2048]{1,0:T(8,128)(2,1)}, u32[]{:S(2)}, u32[]{:S(2)}) collective-permute-start(bf16[512,2048]{1,0:T(8,128)(2,1)} %get-tuple-element.340), channel_id=1, source_target_pairs={{0,1},{1,0},{2,3},{3,2},{4,5},{5,4},{6,7},{7,6},{8,9},{9,8},{10,11... | collective-permute-start | bytes 6291464 | tf_op jit(solution)/shard_map/ppermute | solution.py:30
  277.3 54.0 %collective-permute-start.42 = (bf16[128,2176]{1,0:T(8,128)(2,1)}, bf16[128,2176]{1,0:T(8,128)(2,1)}, u32[]{:S(2)}, u32[]{:S(2)}) collective-permute-start(bf16[128,2176]{1,0:T(8,128)(2,1)} %pad_maximum_fusion.19), channel_id=1, source_target_pairs={{0,4},{4,0},{8,12},{12,8},{16,20},{20,16},{24,28},{28,24},{1,5},{5... | collective-permute-start | bytes 1671176 | tf_op jit(solution)/shard_map/ppermute | solution.py:30
  278.7 52.6 %collective-permute-start.43 = (bf16[128,2176]{1,0:T(8,128)(2,1)}, bf16[128,2176]{1,0:T(8,128)(2,1)S(1)}, u32[]{:S(2)}, u32[]{:S(2)}) collective-permute-start(bf16[128,2176]{1,0:T(8,128)(2,1)} %pad_maximum_fusion.20), channel_id=1, source_target_pairs={{0,2},{1,3},{2,0},{3,1},{4,6},{5,7},{6,4},{7,5},{8,10},{9,11},{10,... | collective-permute-start | bytes 1671176 | tf_op jit(solution)/shard_map/ppermute | solution.py:30
  346.8 41.0 %collective-permute-start.46 = (bf16[512,2176]{1,0:T(8,128)(2,1)}, bf16[512,2176]{1,0:T(8,128)(2,1)}, u32[]{:S(2)}, u32[]{:S(2)}) collective-permute-start(bf16[512,2176]{1,0:T(8,128)(2,1)} %constant_dynamic-update-slice_fusion.28), channel_id=1, source_target_pairs={{0,1},{1,0},{2,3},{3,2},{4,5},{5,4},{6,7},{7,6},{8,9},{9,8},{10,11... | collective-permute-start | bytes 6684680 | tf_op jit(solution)/shard_map/ppermute | solution.py:30
  346.8 41.0 %collective-permute-start.45 = (bf16[512,2048]{1,0:T(8,128)(2,1)}, bf16[512,2048]{1,0:T(8,128)(2,1)}, u32[]{:S(2)}, u32[]{:S(2)}) collective-permute-start(bf16[512,2048]{1,0:T(8,128)(2,1)} %constant_dynamic-update-slice_fusion.22.own_ref), channel_id=1, source_target_pairs={{0,1},{1,0},{2,3},{3,2},{4,5},{5,4},{6,7},{7,6},{8,9},{9,8},{10,11... | collective-permute-start | bytes 6291464 | tf_op jit(solution)/shard_map/ppermute | solution.py:30
  347.3 40.5 %collective-permute-start.47 = (bf16[512,2048]{1,0:T(8,128)(2,1)}, bf16[512,2048]{1,0:T(8,128)(2,1)}, u32[]{:S(2)}, u32[]{:S(2)}) collective-permute-start(bf16[512,2048]{1,0:T(8,128)(2,1)} %get-tuple-element.381), channel_id=1, source_target_pairs={{0,1},{1,0},{2,3},{3,2},{4,5},{5,4},{6,7},{7,6},{8,9},{9,8},{10,11... | collective-permute-start | bytes 6291464 | tf_op jit(solution)/shard_map/ppermute | solution.py:30
  396.8 42.1 %collective-permute-start.50 = (bf16[512,2048]{1,0:T(8,128)(2,1)}, bf16[512,2048]{1,0:T(8,128)(2,1)}, u32[]{:S(2)}, u32[]{:S(2)}) collective-permute-start(bf16[512,2048]{1,0:T(8,128)(2,1)} %get-tuple-element.421), channel_id=1, source_target_pairs={{0,1},{1,0},{2,3},{3,2},{4,5},{5,4},{6,7},{7,6},{8,9},{9,8},{10,11... | collective-permute-start | bytes 6291464 | tf_op jit(solution)/shard_map/ppermute | solution.py:30
  396.8 42.1 %collective-permute-start.51 = (bf16[128,2048]{1,0:T(8,128)(2,1)}, bf16[128,2048]{1,0:T(8,128)(2,1)S(1)}, u32[]{:S(2)}, u32[]{:S(2)}) collective-permute-start(bf16[128,2048]{1,0:T(8,128)(2,1)} %get-tuple-element.422), channel_id=1, source_target_pairs={{0,4},{4,0},{8,12},{12,8},{16,20},{20,16},{24,28},{28,24},{1,5},{5... | collective-permute-start | bytes 1572872 | tf_op jit(solution)/shard_map/ppermute | solution.py:30
  397.4 41.5 %collective-permute-start.52 = (bf16[128,2048]{1,0:T(8,128)(2,1)}, bf16[128,2048]{1,0:T(8,128)(2,1)}, u32[]{:S(2)}, u32[]{:S(2)}) collective-permute-start(bf16[128,2048]{1,0:T(8,128)(2,1)} %get-tuple-element.423), channel_id=1, source_target_pairs={{0,2},{1,3},{2,0},{3,1},{4,6},{5,7},{6,4},{7,5},{8,10},{9,11},{10,... | collective-permute-start | bytes 1572872 | tf_op jit(solution)/shard_map/ppermute | solution.py:30
  398.2 40.6 %collective-permute-start.53 = (bf16[64,2048]{1,0:T(8,128)(2,1)}, bf16[64,2048]{1,0:T(8,128)(2,1)S(1)}, u32[]{:S(2)}, u32[]{:S(2)}) collective-permute-start(bf16[64,2048]{1,0:T(8,128)(2,1)} %slice.403), channel_id=1, source_target_pairs={{0,2},{1,3},{2,0},{3,1},{4,6},{5,7},{6,4},{7,5},{8,10},{9,11},{10,... | collective-permute-start | bytes 786440 | tf_op jit(solution)/shard_map/ppermute | solution.py:30
  474.4 45.5 %collective-permute-start.60 = (bf16[128,2048]{1,0:T(8,128)(2,1)}, bf16[128,2048]{1,0:T(8,128)(2,1)}, u32[]{:S(2)}, u32[]{:S(2)}) collective-permute-start(bf16[128,2048]{1,0:T(8,128)(2,1)} %maximum_bitcast_fusion.1), channel_id=1, source_target_pairs={{0,8},{4,12},{8,16},{12,20},{16,24},{20,28},{24,0},{28,4},{1,9},{5... | collective-permute-start | bytes 1572872 | tf_op jit(solution)/shard_map/ppermute | solution.py:35
  585.8 48.0 %collective-permute-start.73 = (bf16[512,2048]{1,0:T(8,128)(2,1)}, bf16[512,2048]{1,0:T(8,128)(2,1)}, u32[]{:S(2)}, u32[]{:S(2)}) collective-permute-start(bf16[512,2048]{1,0:T(8,128)(2,1)} %slice.359), channel_id=1, source_target_pairs={{0,2},{1,3},{2,0},{3,1},{4,6},{5,7},{6,4},{7,5},{8,10},{9,11},{10,... | collective-permute-start | bytes 6291464 | tf_op jit(solution)/shard_map/ppermute | solution.py:30
  588.9 49.4 %collective-permute-start.72 = (bf16[512,2048]{1,0:T(8,128)(2,1)}, bf16[512,2048]{1,0:T(8,128)(2,1)}, u32[]{:S(2)}, u32[]{:S(2)}) collective-permute-start(bf16[512,2048]{1,0:T(8,128)(2,1)} %dynamic-slice_bitcast_fusion), channel_id=1, source_target_pairs={{0,4},{4,0},{8,12},{12,8},{16,20},{20,16},{24,28},{28,24},{1,5},{5... | collective-permute-start | bytes 6291464 | tf_op jit(solution)/shard_map/ppermute | solution.py:30
  646.3 106.0 %collective-permute-start.87 = (bf16[2,256,2048]{2,1,0:T(8,128)(2,1)S(1)}, bf16[2,256,2048]{2,1,0:T(8,128)(2,1)S(1)}, u32[]{:S(2)}, u32[]{:S(2)}) collective-permute-start(bf16[2,256,2048]{2,1,0:T(8,128)(2,1)S(1)} %slice_bitcast_fusion), channel_id=1, source_target_pairs={{0,2},{1,3},{2,0},{3,1},{4,6},{5,7},{6,4},{7,5},{8,10},{9,11},{10,... | collective-permute-start | bytes 6291464 | tf_op jit(solution)/shard_map/ppermute | solution.py:30
  670.2 77.7 %collective-permute-start.80 = (bf16[1024,768]{1,0:T(8,128)(2,1)S(1)}, bf16[1024,768]{1,0:T(8,128)(2,1)S(1)}, u32[]{:S(2)}, u32[]{:S(2)}) collective-permute-start(bf16[1024,768]{1,0:T(8,128)(2,1)S(1)} %dynamic-slice_bitcast_fusion.1), channel_id=1, source_target_pairs={{0,4},{4,0},{8,12},{12,8},{16,20},{20,16},{24,28},{28,24},{1,5},{5... | collective-permute-start | bytes 4718600 | tf_op jit(solution)/shard_map/ppermute | solution.py:30
  777.0 57.5 %collective-permute-start.92 = (bf16[512,2048]{1,0:T(8,128)(2,1)}, bf16[512,2048]{1,0:T(8,128)(2,1)S(1)}, u32[]{:S(2)}, u32[]{:S(2)}) collective-permute-start(bf16[512,2048]{1,0:T(8,128)(2,1)} %pad_maximum_fusion.3), channel_id=1, source_target_pairs={{0,4},{4,0},{8,12},{12,8},{16,20},{20,16},{24,28},{28,24},{1,5},{5... | collective-permute-start | bytes 6291464 | tf_op jit(solution)/shard_map/ppermute | solution.py:30
  838.4 46.9 %collective-permute-start.98 = (bf16[256,2048]{1,0:T(8,128)(2,1)S(1)}, bf16[256,2048]{1,0:T(8,128)(2,1)S(1)}, u32[]{:S(2)}, u32[]{:S(2)}) collective-permute-start(bf16[256,2048]{1,0:T(8,128)(2,1)S(1)} %slice.371), channel_id=1, source_target_pairs={{0,4},{4,0},{8,12},{12,8},{16,20},{20,16},{24,28},{28,24},{1,5},{5... | collective-permute-start | bytes 3145736 | tf_op jit(solution)/shard_map/ppermute | solution.py:30
  839.9 79.0 %collective-permute-start.104 = (bf16[2,128,2048]{2,1,0:T(8,128)(2,1)S(1)}, bf16[2,128,2048]{2,1,0:T(8,128)(2,1)S(1)}, u32[]{:S(2)}, u32[]{:S(2)}) collective-permute-start(bf16[2,128,2048]{2,1,0:T(8,128)(2,1)S(1)} %pad_maximum_fusion.12), channel_id=1, source_target_pairs={{0,1},{1,0},{2,3},{3,2},{4,5},{5,4},{6,7},{7,6},{8,9},{9,8},{10,11... | collective-permute-start | bytes 3145736 | tf_op jit(solution)/shard_map/ppermute | solution.py:30
  840.0 66.9 %collective-permute-start.95 = (bf16[1024,512]{1,0:T(8,128)(2,1)S(1)}, bf16[1024,512]{1,0:T(8,128)(2,1)S(1)}, u32[]{:S(2)}, u32[]{:S(2)}) collective-permute-start(bf16[1024,512]{1,0:T(8,128)(2,1)S(1)} %pad_maximum_fusion.11), channel_id=1, source_target_pairs={{0,4},{4,0},{8,12},{12,8},{16,20},{20,16},{24,28},{28,24},{1,5},{5... | collective-permute-start | bytes 3145736 | tf_op jit(solution)/shard_map/ppermute | solution.py:30
  857.2 51.3 %collective-permute-start.97 = (bf16[512,768]{1,0:T(8,128)(2,1)S(1)}, bf16[512,768]{1,0:T(8,128)(2,1)S(1)}, u32[]{:S(2)}, u32[]{:S(2)}) collective-permute-start(bf16[512,768]{1,0:T(8,128)(2,1)S(1)} %pad_maximum_fusion.14), channel_id=1, source_target_pairs={{0,8},{4,12},{8,0},{12,4},{16,24},{20,28},{24,16},{28,20},{1,9},{5... | collective-permute-start | bytes 2359304 | tf_op jit(solution)/shard_map/ppermute | solution.py:30
  912.6 46.1 %collective-permute-start.100 = (bf16[128,2048]{1,0:T(8,128)(2,1)}, bf16[128,2048]{1,0:T(8,128)(2,1)}, u32[]{:S(2)}, u32[]{:S(2)}) collective-permute-start(bf16[128,2048]{1,0:T(8,128)(2,1)} %get-tuple-element.559), channel_id=1, source_target_pairs={{0,8},{4,12},{8,16},{12,20},{16,24},{20,28},{24,0},{28,4},{1,9},{5... | collective-permute-start | bytes 1572872 | tf_op jit(solution)/shard_map/ppermute | solution.py:35
  912.6 46.1 %collective-permute-start.101 = (bf16[128,2048]{1,0:T(8,128)(2,1)}, bf16[128,2048]{1,0:T(8,128)(2,1)}, u32[]{:S(2)}, u32[]{:S(2)}) collective-permute-start(bf16[128,2048]{1,0:T(8,128)(2,1)} %get-tuple-element.561), channel_id=1, source_target_pairs={{0,24},{4,28},{8,0},{12,4},{16,8},{20,12},{24,16},{28,20},{1,25},{... | collective-permute-start | bytes 1572872 | tf_op jit(solution)/shard_map/ppermute | solution.py:35
  916.4 50.1 %collective-permute-start.102 = (bf16[128,2048]{1,0:T(8,128)(2,1)}, bf16[128,2048]{1,0:T(8,128)(2,1)}, u32[]{:S(2)}, u32[]{:S(2)}) collective-permute-start(bf16[128,2048]{1,0:T(8,128)(2,1)} %get-tuple-element.560), channel_id=1, source_target_pairs={{0,16},{4,20},{8,24},{12,28},{16,0},{20,4},{24,8},{28,12},{1,17},{... | collective-permute-start | bytes 1572872 | tf_op jit(solution)/shard_map/ppermute | solution.py:35
  925.2 56.3 %collective-permute-start.108 = (bf16[1024,768]{1,0:T(8,128)(2,1)}, bf16[1024,768]{1,0:T(8,128)(2,1)}, u32[]{:S(2)}, u32[]{:S(2)}) collective-permute-start(bf16[1024,768]{1,0:T(8,128)(2,1)} %pad_maximum_fusion.6), channel_id=1, source_target_pairs={{0,4},{4,0},{8,12},{12,8},{16,20},{20,16},{24,28},{28,24},{1,5},{5... | collective-permute-start | bytes 4718600 | tf_op jit(solution)/shard_map/ppermute | solution.py:30
  (184 other events, 2709.1 us)

commit v4 on v3

--- a/solution.py
+++ b/solution.py
@@ -188,8 +188,8 @@
     probs_rest = (probs - probs_high.astype(F32)).astype(LOW)
     weight = jnp.dot(probs_high, select, preferred_element_type=F32)
     weight += jnp.dot(probs_rest, select, preferred_element_type=F32)
-    gate = jnp.dot(rows, gate_ref[...], preferred_element_type=F32)
-    up = jnp.dot(rows, up_ref[...], preferred_element_type=F32)
+    gate = lax.dot_general(rows, gate_ref[...], NT_DIMS, preferred_element_type=F32)
+    up = lax.dot_general(rows, up_ref[...], NT_DIMS, preferred_element_type=F32)
     d_hidden = (
         lax.dot_general(
             cotangents[:, :model_width], down_ref[...], NT_DIMS, preferred_element_type=F32
@@ -227,8 +227,8 @@
     store(dlog_ref, dlog)
     outs = jnp.dot(hidden_low, down_ref[...], preferred_element_type=F32).astype(LOW)
     store_either(out_keep_ref, out_send_ref, outs)
-    grads = lax.dot_general(d_gate, gate_ref[...], NT_DIMS, preferred_element_type=F32)
-    grads += lax.dot_general(d_up, up_ref[...], NT_DIMS, preferred_element_type=F32)
+    grads = jnp.dot(d_gate, gate_ref[...], preferred_element_type=F32)
+    grads += jnp.dot(d_up, up_ref[...], preferred_element_type=F32)
     grads += jnp.dot(dlog, router_t_ref[...], preferred_element_type=F32)
     store_either(grad_keep_ref, grad_send_ref, grads.astype(LOW))
 
@@ -571,10 +571,10 @@
     pairs = [pair] + [swap(pair, "ep", d) for d in range(1, SPAN)]
     wide_first = now(spread_next(wide_first))
     q_lin = jnp.dot(attn_low, q_weight, preferred_element_type=F32)
-    gate_cat = expert_gate.transpose(1, 0, 2).reshape(-1, width)
-    up_cat = expert_up.transpose(1, 0, 2).reshape(-1, width)
-    gate_cat, up_cat, q_lin, wide_first, wide_rows, pairs, wide_near = tie(
-        gate_cat, up_cat, q_lin, wide_first, wide_rows, pairs, wide_near
+    gate_cat = expert_gate.transpose(0, 2, 1).reshape(width, -1)
+    up_cat = expert_up.transpose(0, 2, 1).reshape(width, -1)
+    q_lin, wide_first, wide_rows, pairs, wide_near = tie(
+        q_lin, wide_first, wide_rows, pairs, wide_near
     )
     wide_far = fetch(wide_rows, groups[-1])
     wide_near = [now(spread_start(group)) for group in wide_near]
@@ -678,7 +678,7 @@
         return jnp.einsum("ta,tb->ab", left, right, preferred_element_type=F32)
 
     def split_experts(wide_grad):
-        return wide_grad.reshape(-1, local_experts, hidden_width).transpose(1, 0, 2)
+        return wide_grad.reshape(local_experts, hidden_width, -1).transpose(0, 2, 1)
 
     d_ffn = land(jnp.zeros_like(x_mid), 0, back[0])
     (back[1], back[2], back[3]), down_grad = step(
@@ -689,7 +689,7 @@
     down_grad = down_grad.reshape(expert_down.shape)
     d_ffn = land(d_ffn, 1, back[1])
     (back[2], back[3]), gate_grad = step(
-        [collect_last(back[2]), collect_next(back[3])], over_rows, (rows_all, d_gate_low)
+        [collect_last(back[2]), collect_next(back[3])], over_rows, (d_gate_low, rows_all)
     )
     d_ffn = land(d_ffn, 2, back[2])
     (back[3],), router_grad_t = step([collect_last(back[3])], over_rows, (dlog_low, rows_all))
@@ -773,7 +773,7 @@
         second_sum = now(halve_sum(second_sum, mask))
     for mask in masks[:0:-1]:
         first_sum = now(double(first_sum, mask))
-    up_grad = over_rows(rows_all, d_up_low)
+    up_grad = over_rows(d_up_low, rows_all)
     small = sum_tp(small)
     input_grad = join_rows(input_rows)
     first_sum, second_sum, o_sum, small, up_grad, out_first, out_second = tie(

time: 1010 us -> 999 us (0.989)
  waiting for transfers between devices: 356 us -> 380 us
  local copies, waits for them, and re-layouts: 105 us -> 81.5 us
    optimization_barrier x4 -> x0, local copies, waits for them, and re-layouts: 22.9 us -> none  [tie(): return lax.optimization_barrier(values)]
    ppermute x97, waiting for transfers between devices: 290 us -> 313 us  [swap(): return lax.ppermute(block, axis, [(i, i ^ mask) for i in devices])]
    unnamed x240 -> x238, local copies, waits for them, and re-layouts: 42.2 us -> 42.2 us
  transfers between devices with their start and end apart: 110 -> 110, of which waited for: 40 -> 42; matrix products, arithmetic and copies ran while one was open for 20% -> 18% of each run, Pallas kernels for 21% -> 21%
where the time goes in v4:
time: 999 us; the launch traced here: 985 us
  waiting for transfers between devices  380 us (38%)
  Pallas kernels  204 us (20%)
  starting transfers between devices  120 us (12%)
  other arithmetic  115 us (12%)
  matrix products  82.4 us (8%)
  local copies, waits for them, and re-layouts  81.5 us (8%)
    ppermute x97, waiting for transfers between devices, swap(): return lax.ppermute(block, axis, [(i, i ^ mask) for i in devices])  313 us
    pallas_call x4, Pallas kernels, expert_pass(): pl.pallas_call(expert_kernel, grid=(2 * half,), in_specs=in_specs + [pl.B...  151 us
    ppermute x97, starting transfers between devices, swap(): return lax.ppermute(block, axis, [(i, i ^ mask) for i in devices])  97.6 us
    ppermute x12, waiting for transfers between devices, turn(): lax.ppermute(block, 'ep', [(i, (i + 2 * step) % count) for i in range(cou...  61.3 us
    dot_general x4, matrix products, over_rows(): return jnp.einsum('ta,tb->ab', left, right, preferred_element_type=F32)  59.4 us
    unnamed x238, local copies, waits for them, and re-layouts  42.2 us
    convert_element_type x22, other arithmetic, add_low(): return (kept.astype(F32) + received.astype(F32)).astype(LOW)  38.7 us
    pallas_call x1, Pallas kernels, attend_back(): pl.pallas_call(attend_back_kernel, grid_spec=pltpu.PrefetchScalarGridSpec...  35 us
  transfers between devices with their start and end apart: 110, of which 42 were waited for; matrix products, arithmetic and copies ran while one was open for 18% of the time, Pallas kernels for 21%

profile of v4, /device:TPU:0, one launch (start us, length us, event | category | flops | bytes accessed | tf_op | source)
XLA Modules:
  0.0 985.5 jit_solution(8030420362281925081)
XLA Ops:
  30.2 7.5 collective-permute-done.2
  59.5 18.2 %attend.1 = (bf16[512,1024]{1,0:T(8,128)(2,1)}, f32[8,1,512]{2,1,0:T(1,128)}) custom-call(s32[6]{0:T(128)} %stack.57.place_ref, f32[512,1024]{1,0:T(8,128)} %fusion.72.q_ref, f32[1,128]{1,0:T(1,128)} %bitcast.318, f32[512,128]{1,0:T(8,128)} %get-tuple-element.636.cos_ref, f32[512,128]{1,0:T(8,128)} %get-tuple-element.543.sin_ref, ...), custom_call_target="tpu_custom_call" | custom-call | flops 4294967296 | bytes 4194304 | tf_op jit(solution)/shard_map/attend/pallas_call | solution.py:347
  100.9 19.3 %collective-permute-done.24 = bf16[256,2176]{1,0:T(8,128)(2,1)S(1)} collective-permute-done((bf16[256,2176]{1,0:T(8,128)(2,1)}, bf16[256,2176]{1,0:T(8,128)(2,1)S(1)}, u32[]{:S(2)}, u32[]{:S(2)}) %collective-permute-start.24) | collective-permute-done | bytes 1114144 | tf_op jit(solution)/shard_map/ppermute | solution.py:30
  123.5 8.3 collective-permute-done.13
  152.5 7.5 collective-permute-done.16
  162.0 20.3 %collective-permute-done.15 = bf16[128,2048]{1,0:T(8,128)(2,1)S(1)} collective-permute-done((bf16[128,2048]{1,0:T(8,128)(2,1)S(1)}, bf16[128,2048]{1,0:T(8,128)(2,1)S(1)}, u32[]{:S(2)}, u32[]{:S(2)}) %collective-permute-start.15) | collective-permute-done | bytes 524320 | tf_op jit(solution)/shard_map/ppermute | solution.py:35
  195.9 8.9 collective-permute-done.18
  215.9 8.6 collective-permute-done.34
  227.7 37.7 %expert_pass.4 = (bf16[512,2048]{1,0:T(8,128)(2,1)}, bf16[512,2048]{1,0:T(8,128)(2,1)}, bf16[8,4,64,2048]{3,2,1,0:T(8,128)(2,1)}, bf16[8,4,64,2048]{3,2,1,0:T(8,...) custom-call(bf16[512,2048]{1,0:T(8,128)(2,1)} %copy-done.77, ...), custom_call_target="tpu_custom_call" | custom-call | flops 19327352832 | bytes 20971520 | tf_op jit(solution)/shard_map/expert_pass/pallas_call | solution.py:274
  278.6 37.9 %expert_pass.5 = (bf16[512,2048]{1,0:T(8,128)(2,1)}, bf16[512,2048]{1,0:T(8,128)(2,1)}, bf16[8,4,64,2048]{3,2,1,0:T(8,128)(2,1)}, bf16[8,4,64,2048]{3,2,1,0:T(8,...) custom-call(bf16[512,2048]{1,0:T(8,128)(2,1)} %constant_dynamic-upda, ...), custom_call_target="tpu_custom_call", output_to_operand_aliasing={{2}: (10, {}), {3}: (11, {}), {4}: (12, {}), {5}: (13, {}),... | custom-call | flops 19327352832 | bytes 20971520 | tf_op jit(solution)/shard_map/expert_pass/pallas_call | solution.py:274
  321.1 8.8 collective-permute-done.41
  348.3 37.7 %expert_pass.6 = (bf16[512,2048]{1,0:T(8,128)(2,1)}, bf16[512,2048]{1,0:T(8,128)(2,1)}, bf16[8,4,64,2048]{3,2,1,0:T(8,128)(2,1)}, bf16[8,4,64,2048]{3,2,1,0:T(8,...) custom-call(bf16[512,2048]{1,0:T(8,128)(2,1)} %copy-done.27, ...), custom_call_target="tpu_custom_call", output_to_operand_aliasing={{2}: (10, {}), {3}: (11, {}), {4}: (12, {}), {5}: (13, {}),... | custom-call | flops 19327352832 | bytes 20971520 | tf_op jit(solution)/shard_map/expert_pass/pallas_call | solution.py:274
  399.0 37.8 %expert_pass.7 = (bf16[512,2048]{1,0:T(8,128)(2,1)}, bf16[512,2048]{1,0:T(8,128)(2,1)}, bf16[8,4,64,2048]{3,2,1,0:T(8,128)(2,1)}, bf16[8,4,64,2048]{3,2,1,0:T(8,...) custom-call(bf16[512,2048]{1,0:T(8,128)(2,1)} %constant_dynamic-upda, ...), custom_call_target="tpu_custom_call", output_to_operand_aliasing={{2}: (10, {}), {3}: (11, {}), {4}: (12, {}), {5}: (13, {}),... | custom-call | flops 19327352832 | bytes 20971520 | tf_op jit(solution)/shard_map/expert_pass/pallas_call | solution.py:274
  449.9 19.0 %fusion.95 = f32[768,2048]{1,0:T(8,128)} fusion(bf16[4096,768]{1,0:T(8,128)(2,1)S(1)} %bitcast.256, bf16[4096,2048]{1,0:T(8,128)(2,1)} %bitcast.253), kind=kOutput, calls=%fused_computation.321 | convolution fusion | flops 12884901888 | bytes 29360128 | tf_op jit(solution)/shard_map/ta,tb->ab/dot_general | solution.py:678
  485.2 16.1 %fusion.96 = f32[768,2048]{1,0:T(8,128)} fusion(bf16[4096,768]{1,0:T(8,128)(2,1)S(1)} %bitcast.259, bf16[4096,2048]{1,0:T(8,128)(2,1)S(1)} %bitcast.251), kind=kOutput, calls=%fused_computation.322 | convolution fusion | flops 12884901888 | bytes 29360128 | tf_op jit(solution)/shard_map/ta,tb->ab/dot_general | solution.py:678
  519.7 18.5 %collective-permute-done.68 = bf16[128,2048]{1,0:T(8,128)(2,1)S(1)} collective-permute-done((bf16[128,2048]{1,0:T(8,128)(2,1)S(1)}, bf16[128,2048]{1,0:T(8,128)(2,1)S(1)}, u32[]{:S(2)}, u32[]{:S(2)}) %collective-permute-start.68) | collective-permute-done | bytes 524320 | tf_op jit(solution)/shard_map/ppermute | solution.py:35
  542.5 13.2 %collective-permute-done.70 = bf16[128,2048]{1,0:T(8,128)(2,1)} collective-permute-done((bf16[128,2048]{1,0:T(8,128)(2,1)S(1)}, bf16[128,2048]{1,0:T(8,128)(2,1)}, u32[]{:S(2)}, u32[]{:S(2)}) %collective-permute-start.70) | collective-permute-done | bytes 524320 | tf_op jit(solution)/shard_map/ppermute | solution.py:30
  571.5 6.6 fusion
  586.9 35.0 %attend_back.1 = (bf16[512,1024]{1,0:T(8,128)(2,1)}, f32[2048,128]{1,0:T(8,128)}, f32[2048,128]{1,0:T(8,128)}, f32[1,128]{1,0:T(1,128)}) custom-call(s32[6]{0:T(128)} %stack.57.place_ref, f32[512,1024]{1,0:T(8,128)} %fusion.72.q_ref, bf16[512,1024]{1,0:T(8,128)(2,1)} %convolution_convert_fusion.3.d_ref, f32[1,128]{1,0:T(1,128)} %bitcast.319, ...), custom_call_target="tpu_custom_call" | custom-call | flops 21474836480 | bytes 4194304 | tf_op jit(solution)/shard_map/attend_back/pallas_call | solution.py:441
  621.9 9.4 collective-permute-done.73
  668.1 14.0 %collective-permute-done.81 = bf16[256,2048]{1,0:T(8,128)(2,1)S(1)} collective-permute-done((bf16[256,2048]{1,0:T(8,128)(2,1)S(1)}, bf16[256,2048]{1,0:T(8,128)(2,1)S(1)}, u32[]{:S(2)}, u32[]{:S(2)}) %collective-permute-start.81) | collective-permute-done | bytes 1048608 | tf_op jit(solution)/shard_map/ppermute | solution.py:30
  689.6 18.3 %collective-permute-done.82 = bf16[128,2048]{1,0:T(8,128)(2,1)S(1)} collective-permute-done((bf16[128,2048]{1,0:T(8,128)(2,1)S(1)}, bf16[128,2048]{1,0:T(8,128)(2,1)S(1)}, u32[]{:S(2)}, u32[]{:S(2)}) %collective-permute-start.82) | collective-permute-done | bytes 524320 | tf_op jit(solution)/shard_map/ppermute | solution.py:30
  712.0 32.4 %collective-permute-done.76 = bf16[256,512]{1,0:T(8,128)(2,1)S(1)} collective-permute-done((bf16[256,512]{1,0:T(8,128)(2,1)S(1)}, bf16[256,512]{1,0:T(8,128)(2,1)S(1)}, u32[]{:S(2)}, u32[]{:S(2)}) %collective-permute-start.76) | collective-permute-done | bytes 262176 | tf_op jit(solution)/shard_map/ppermute | solution.py:30
  751.7 18.6 %collective-permute-done.84 = bf16[256,2048]{1,0:T(8,128)(2,1)S(1)} collective-permute-done((bf16[256,2048]{1,0:T(8,128)(2,1)S(1)}, bf16[256,2048]{1,0:T(8,128)(2,1)S(1)}, u32[]{:S(2)}, u32[]{:S(2)}) %collective-permute-start.84) | collective-permute-done | bytes 1048608 | tf_op jit(solution)/shard_map/ppermute | solution.py:30
  777.4 8.8 collective-permute-done.88
  789.0 20.5 %convolution_bitcast_fusion = f32[768,2048]{1,0:T(8,128)} fusion(bf16[16,4,64,768]{3,2,1,0:T(8,128)(2,1)} %get-tuple-element.512, bf16[16,4,64,2048]{3,2,1,0:T(8,128)(2,1)} %get-tuple-element.468), kind=kOutput, calls=%fused_computation.16 | convolution fusion | flops 12884901888 | bytes 29360128 | tf_op jit(solution)/shard_map/ta,tb->ab/dot_general | solution.py:678
  814.9 16.2 %collective-permute-done.91 = bf16[256,768]{1,0:T(8,128)(2,1)S(1)} collective-permute-done((bf16[256,768]{1,0:T(8,128)(2,1)S(1)}, bf16[256,768]{1,0:T(8,128)(2,1)S(1)}, u32[]{:S(2)}, u32[]{:S(2)}) %collective-permute-start.91) | collective-permute-done | bytes 393248 | tf_op jit(solution)/shard_map/ppermute | solution.py:30
  837.4 16.3 %collective-permute-done.96 = bf16[256,768]{1,0:T(8,128)(2,1)S(1)} collective-permute-done((bf16[256,768]{1,0:T(8,128)(2,1)S(1)}, bf16[256,768]{1,0:T(8,128)(2,1)S(1)}, u32[]{:S(2)}, u32[]{:S(2)}) %collective-permute-start.96) | collective-permute-done | bytes 393248 | tf_op jit(solution)/shard_map/ppermute | solution.py:30
  860.0 22.1 %collective-permute-done.98 = bf16[256,2048]{1,0:T(8,128)(2,1)S(1)} collective-permute-done((bf16[256,2048]{1,0:T(8,128)(2,1)S(1)}, bf16[256,2048]{1,0:T(8,128)(2,1)S(1)}, u32[]{:S(2)}, u32[]{:S(2)}) %collective-permute-start.98) | collective-permute-done | bytes 1048608 | tf_op jit(solution)/shard_map/ppermute | solution.py:30
  882.4 21.1 %collective-permute-done.95 = bf16[1024,512]{1,0:T(8,128)(2,1)S(1)} collective-permute-done((bf16[1024,512]{1,0:T(8,128)(2,1)S(1)}, bf16[1024,512]{1,0:T(8,128)(2,1)S(1)}, u32[]{:S(2)}, u32[]{:S(2)}) %collective-permute-start.95) | collective-permute-done | bytes 1048608 | tf_op jit(solution)/shard_map/ppermute | solution.py:30
  922.1 25.0 %collective-permute-done.106 = f32[35,2048]{1,0:T(8,128)S(1)} collective-permute-done((f32[35,2048]{1,0:T(8,128)S(1)}, f32[35,2048]{1,0:T(8,128)S(1)}, u32[]{:S(2)}, u32[]{:S(2)}) %collective-permute-start.106) | collective-permute-done | bytes 286752 | tf_op jit(solution)/shard_map/ppermute | solution.py:30
  952.0 9.7 collective-permute-done.102
  (636 shorter events, 383.0 us)
Async XLA Ops:
  3.6 43.9 %collective-permute-start.7 = (bf16[128,2176]{1,0:T(8,128)(2,1)}, bf16[128,2176]{1,0:T(8,128)(2,1)}, u32[]{:S(2)}, u32[]{:S(2)}) collective-permute-start(bf16[128,2176]{1,0:T(8,128)(2,1)} %pad_maximum_fusion.13), channel_id=1, source_target_pairs={{0,24},{4,28},{8,0},{12,4},{16,8},{20,12},{24,16},{28,20},{1,25},{... | collective-permute-start | bytes 1671176 | tf_op jit(solution)/shard_map/ppermute | solution.py:35
  91.6 42.5 %collective-permute-start.14 = (bf16[128,2176]{1,0:T(8,128)(2,1)}, bf16[128,2176]{1,0:T(8,128)(2,1)S(1)}, u32[]{:S(2)}, u32[]{:S(2)}) collective-permute-start(bf16[128,2176]{1,0:T(8,128)(2,1)} %pad_maximum_fusion.13), channel_id=1, source_target_pairs={{0,16},{4,20},{8,24},{12,28},{16,0},{20,4},{24,8},{28,12},{1,17},{... | collective-permute-start | bytes 1671176 | tf_op jit(solution)/shard_map/ppermute | solution.py:35
  138.1 44.3 %collective-permute-start.15 = (bf16[128,2048]{1,0:T(8,128)(2,1)S(1)}, bf16[128,2048]{1,0:T(8,128)(2,1)S(1)}, u32[]{:S(2)}, u32[]{:S(2)}) collective-permute-start(bf16[128,2048]{1,0:T(8,128)(2,1)S(1)} %multiply_convert_fusion.1), channel_id=1, source_target_pairs={{0,16},{4,20},{8,24},{12,28},{16,0},{20,4},{24,8},{28,12},{1,17},{... | collective-permute-start | bytes 1572872 | tf_op jit(solution)/shard_map/ppermute | solution.py:35
  151.0 43.1 %collective-permute-start.23 = (bf16[64,2048]{1,0:T(8,128)(2,1)S(1)}, bf16[64,2048]{1,0:T(8,128)(2,1)S(1)}, u32[]{:S(2)}, u32[]{:S(2)}) collective-permute-start(bf16[64,2048]{1,0:T(8,128)(2,1)S(1)} %get-tuple-element.611), channel_id=1, source_target_pairs={{0,4},{4,0},{8,12},{12,8},{16,20},{20,16},{24,28},{28,24},{1,5},{5... | collective-permute-start | bytes 786440 | tf_op jit(solution)/shard_map/ppermute | solution.py:30
  209.3 56.1 %collective-permute-start.38 = (bf16[1024,2176]{1,0:T(8,128)(2,1)}, bf16[1024,2176]{1,0:T(8,128)(2,1)}, u32[]{:S(2)}, u32[]{:S(2)}) collective-permute-start(bf16[1024,2176]{1,0:T(8,128)(2,1)} %constant_dynamic-update-slice_fusion.6), channel_id=1, source_target_pairs={{0,1},{1,0},{2,3},{3,2},{4,5},{5,4},{6,7},{7,6},{8,9},{9,8},{10,11... | collective-permute-start | bytes 13369352 | tf_op jit(solution)/shard_map/ppermute | solution.py:30
  209.4 56.1 %collective-permute-start.31 = (bf16[512,2048]{1,0:T(8,128)(2,1)}, bf16[512,2048]{1,0:T(8,128)(2,1)}, u32[]{:S(2)}, u32[]{:S(2)}) collective-permute-start(bf16[512,2048]{1,0:T(8,128)(2,1)} %constant_dynamic-update-slice_fusion.own_ref), channel_id=1, source_target_pairs={{0,1},{1,0},{2,3},{3,2},{4,5},{5,4},{6,7},{7,6},{8,9},{9,8},{10,11... | collective-permute-start | bytes 6291464 | tf_op jit(solution)/shard_map/ppermute | solution.py:30
  224.5 40.9 %collective-permute-start.32 = (bf16[128,2048]{1,0:T(8,128)(2,1)}, bf16[128,2048]{1,0:T(8,128)(2,1)}, u32[]{:S(2)}, u32[]{:S(2)}) collective-permute-start(bf16[128,2048]{1,0:T(8,128)(2,1)} %pad_maximum_fusion.27), channel_id=1, source_target_pairs={{0,4},{4,0},{8,12},{12,8},{16,20},{20,16},{24,28},{28,24},{1,5},{5... | collective-permute-start | bytes 1572872 | tf_op jit(solution)/shard_map/ppermute | solution.py:30
  275.1 54.8 %collective-permute-start.39 = (bf16[512,2048]{1,0:T(8,128)(2,1)S(1)}, bf16[512,2048]{1,0:T(8,128)(2,1)}, u32[]{:S(2)}, u32[]{:S(2)}) collective-permute-start(bf16[512,2048]{1,0:T(8,128)(2,1)S(1)} %constant_dynamic-update-slice_fusion.16.own_ref), channel_id=1, source_target_pairs={{0,1},{1,0},{2,3},{3,2},{4,5},{5,4},{6,7},{7,6},{8,9},{9,8},{10,11... | collective-permute-start | bytes 6291464 | tf_op jit(solution)/shard_map/ppermute | solution.py:30
  275.2 54.8 %collective-permute-start.44 = (bf16[512,2048]{1,0:T(8,128)(2,1)}, bf16[512,2048]{1,0:T(8,128)(2,1)}, u32[]{:S(2)}, u32[]{:S(2)}) collective-permute-start(bf16[512,2048]{1,0:T(8,128)(2,1)} %get-tuple-element.336), channel_id=1, source_target_pairs={{0,1},{1,0},{2,3},{3,2},{4,5},{5,4},{6,7},{7,6},{8,9},{9,8},{10,11... | collective-permute-start | bytes 6291464 | tf_op jit(solution)/shard_map/ppermute | solution.py:30
  275.7 54.2 %collective-permute-start.42 = (bf16[128,2176]{1,0:T(8,128)(2,1)}, bf16[128,2176]{1,0:T(8,128)(2,1)}, u32[]{:S(2)}, u32[]{:S(2)}) collective-permute-start(bf16[128,2176]{1,0:T(8,128)(2,1)} %pad_maximum_fusion.19), channel_id=1, source_target_pairs={{0,4},{4,0},{8,12},{12,8},{16,20},{20,16},{24,28},{28,24},{1,5},{5... | collective-permute-start | bytes 1671176 | tf_op jit(solution)/shard_map/ppermute | solution.py:30
  277.0 52.9 %collective-permute-start.43 = (bf16[128,2176]{1,0:T(8,128)(2,1)}, bf16[128,2176]{1,0:T(8,128)(2,1)S(1)}, u32[]{:S(2)}, u32[]{:S(2)}) collective-permute-start(bf16[128,2176]{1,0:T(8,128)(2,1)} %pad_maximum_fusion.20), channel_id=1, source_target_pairs={{0,2},{1,3},{2,0},{3,1},{4,6},{5,7},{6,4},{7,5},{8,10},{9,11},{10,... | collective-permute-start | bytes 1671176 | tf_op jit(solution)/shard_map/ppermute | solution.py:30
  345.3 40.7 %collective-permute-start.46 = (bf16[512,2176]{1,0:T(8,128)(2,1)}, bf16[512,2176]{1,0:T(8,128)(2,1)}, u32[]{:S(2)}, u32[]{:S(2)}) collective-permute-start(bf16[512,2176]{1,0:T(8,128)(2,1)} %constant_dynamic-update-slice_fusion.28), channel_id=1, source_target_pairs={{0,1},{1,0},{2,3},{3,2},{4,5},{5,4},{6,7},{7,6},{8,9},{9,8},{10,11... | collective-permute-start | bytes 6684680 | tf_op jit(solution)/shard_map/ppermute | solution.py:30
  345.3 40.6 %collective-permute-start.45 = (bf16[512,2048]{1,0:T(8,128)(2,1)}, bf16[512,2048]{1,0:T(8,128)(2,1)}, u32[]{:S(2)}, u32[]{:S(2)}) collective-permute-start(bf16[512,2048]{1,0:T(8,128)(2,1)} %constant_dynamic-update-slice_fusion.22.own_ref), channel_id=1, source_target_pairs={{0,1},{1,0},{2,3},{3,2},{4,5},{5,4},{6,7},{7,6},{8,9},{9,8},{10,11... | collective-permute-start | bytes 6291464 | tf_op jit(solution)/shard_map/ppermute | solution.py:30
  345.8 40.1 %collective-permute-start.47 = (bf16[512,2048]{1,0:T(8,128)(2,1)}, bf16[512,2048]{1,0:T(8,128)(2,1)}, u32[]{:S(2)}, u32[]{:S(2)}) collective-permute-start(bf16[512,2048]{1,0:T(8,128)(2,1)} %get-tuple-element.377), channel_id=1, source_target_pairs={{0,1},{1,0},{2,3},{3,2},{4,5},{5,4},{6,7},{7,6},{8,9},{9,8},{10,11... | collective-permute-start | bytes 6291464 | tf_op jit(solution)/shard_map/ppermute | solution.py:30
  394.9 41.9 %collective-permute-start.50 = (bf16[512,2048]{1,0:T(8,128)(2,1)}, bf16[512,2048]{1,0:T(8,128)(2,1)}, u32[]{:S(2)}, u32[]{:S(2)}) collective-permute-start(bf16[512,2048]{1,0:T(8,128)(2,1)} %get-tuple-element.417), channel_id=1, source_target_pairs={{0,1},{1,0},{2,3},{3,2},{4,5},{5,4},{6,7},{7,6},{8,9},{9,8},{10,11... | collective-permute-start | bytes 6291464 | tf_op jit(solution)/shard_map/ppermute | solution.py:30
  394.9 41.9 %collective-permute-start.51 = (bf16[128,2048]{1,0:T(8,128)(2,1)}, bf16[128,2048]{1,0:T(8,128)(2,1)S(1)}, u32[]{:S(2)}, u32[]{:S(2)}) collective-permute-start(bf16[128,2048]{1,0:T(8,128)(2,1)} %get-tuple-element.418), channel_id=1, source_target_pairs={{0,4},{4,0},{8,12},{12,8},{16,20},{20,16},{24,28},{28,24},{1,5},{5... | collective-permute-start | bytes 1572872 | tf_op jit(solution)/shard_map/ppermute | solution.py:30
  395.7 41.2 %collective-permute-start.52 = (bf16[128,2048]{1,0:T(8,128)(2,1)}, bf16[128,2048]{1,0:T(8,128)(2,1)}, u32[]{:S(2)}, u32[]{:S(2)}) collective-permute-start(bf16[128,2048]{1,0:T(8,128)(2,1)} %get-tuple-element.419), channel_id=1, source_target_pairs={{0,2},{1,3},{2,0},{3,1},{4,6},{5,7},{6,4},{7,5},{8,10},{9,11},{10,... | collective-permute-start | bytes 1572872 | tf_op jit(solution)/shard_map/ppermute | solution.py:30
  396.6 40.2 %collective-permute-start.53 = (bf16[64,2048]{1,0:T(8,128)(2,1)}, bf16[64,2048]{1,0:T(8,128)(2,1)S(1)}, u32[]{:S(2)}, u32[]{:S(2)}) collective-permute-start(bf16[64,2048]{1,0:T(8,128)(2,1)} %slice.403), channel_id=1, source_target_pairs={{0,2},{1,3},{2,0},{3,1},{4,6},{5,7},{6,4},{7,5},{8,10},{9,11},{10,... | collective-permute-start | bytes 786440 | tf_op jit(solution)/shard_map/ppermute | solution.py:30
  472.2 45.4 %collective-permute-start.60 = (bf16[128,2048]{1,0:T(8,128)(2,1)}, bf16[128,2048]{1,0:T(8,128)(2,1)}, u32[]{:S(2)}, u32[]{:S(2)}) collective-permute-start(bf16[128,2048]{1,0:T(8,128)(2,1)} %maximum_bitcast_fusion.1), channel_id=1, source_target_pairs={{0,8},{4,12},{8,16},{12,20},{16,24},{20,28},{24,0},{28,4},{1,9},{5... | collective-permute-start | bytes 1572872 | tf_op jit(solution)/shard_map/ppermute | solution.py:35
  583.3 48.0 %collective-permute-start.73 = (bf16[512,2048]{1,0:T(8,128)(2,1)}, bf16[512,2048]{1,0:T(8,128)(2,1)}, u32[]{:S(2)}, u32[]{:S(2)}) collective-permute-start(bf16[512,2048]{1,0:T(8,128)(2,1)} %slice.359), channel_id=1, source_target_pairs={{0,2},{1,3},{2,0},{3,1},{4,6},{5,7},{6,4},{7,5},{8,10},{9,11},{10,... | collective-permute-start | bytes 6291464 | tf_op jit(solution)/shard_map/ppermute | solution.py:30
  586.1 49.6 %collective-permute-start.72 = (bf16[512,2048]{1,0:T(8,128)(2,1)}, bf16[512,2048]{1,0:T(8,128)(2,1)}, u32[]{:S(2)}, u32[]{:S(2)}) collective-permute-start(bf16[512,2048]{1,0:T(8,128)(2,1)} %dynamic-slice_bitcast_fusion), channel_id=1, source_target_pairs={{0,4},{4,0},{8,12},{12,8},{16,20},{20,16},{24,28},{28,24},{1,5},{5... | collective-permute-start | bytes 6291464 | tf_op jit(solution)/shard_map/ppermute | solution.py:30
  643.8 105.8 %collective-permute-start.87 = (bf16[2,256,2048]{2,1,0:T(8,128)(2,1)S(1)}, bf16[2,256,2048]{2,1,0:T(8,128)(2,1)S(1)}, u32[]{:S(2)}, u32[]{:S(2)}) collective-permute-start(bf16[2,256,2048]{2,1,0:T(8,128)(2,1)S(1)} %slice_bitcast_fusion), channel_id=1, source_target_pairs={{0,2},{1,3},{2,0},{3,1},{4,6},{5,7},{6,4},{7,5},{8,10},{9,11},{10,... | collective-permute-start | bytes 6291464 | tf_op jit(solution)/shard_map/ppermute | solution.py:30
  667.3 77.8 %collective-permute-start.80 = (bf16[1024,768]{1,0:T(8,128)(2,1)S(1)}, bf16[1024,768]{1,0:T(8,128)(2,1)S(1)}, u32[]{:S(2)}, u32[]{:S(2)}) collective-permute-start(bf16[1024,768]{1,0:T(8,128)(2,1)S(1)} %dynamic-slice_bitcast_fusion.1), channel_id=1, source_target_pairs={{0,4},{4,0},{8,12},{12,8},{16,20},{20,16},{24,28},{28,24},{1,5},{5... | collective-permute-start | bytes 4718600 | tf_op jit(solution)/shard_map/ppermute | solution.py:30
  774.2 57.0 %collective-permute-start.92 = (bf16[512,2048]{1,0:T(8,128)(2,1)}, bf16[512,2048]{1,0:T(8,128)(2,1)S(1)}, u32[]{:S(2)}, u32[]{:S(2)}) collective-permute-start(bf16[512,2048]{1,0:T(8,128)(2,1)} %pad_maximum_fusion.3), channel_id=1, source_target_pairs={{0,4},{4,0},{8,12},{12,8},{16,20},{20,16},{24,28},{28,24},{1,5},{5... | collective-permute-start | bytes 6291464 | tf_op jit(solution)/shard_map/ppermute | solution.py:30
  835.0 47.0 %collective-permute-start.98 = (bf16[256,2048]{1,0:T(8,128)(2,1)S(1)}, bf16[256,2048]{1,0:T(8,128)(2,1)S(1)}, u32[]{:S(2)}, u32[]{:S(2)}) collective-permute-start(bf16[256,2048]{1,0:T(8,128)(2,1)S(1)} %slice.371), channel_id=1, source_target_pairs={{0,4},{4,0},{8,12},{12,8},{16,20},{20,16},{24,28},{28,24},{1,5},{5... | collective-permute-start | bytes 3145736 | tf_op jit(solution)/shard_map/ppermute | solution.py:30
  836.5 78.0 %collective-permute-start.104 = (bf16[2,128,2048]{2,1,0:T(8,128)(2,1)S(1)}, bf16[2,128,2048]{2,1,0:T(8,128)(2,1)S(1)}, u32[]{:S(2)}, u32[]{:S(2)}) collective-permute-start(bf16[2,128,2048]{2,1,0:T(8,128)(2,1)S(1)} %pad_maximum_fusion.12), channel_id=1, source_target_pairs={{0,1},{1,0},{2,3},{3,2},{4,5},{5,4},{6,7},{7,6},{8,9},{9,8},{10,11... | collective-permute-start | bytes 3145736 | tf_op jit(solution)/shard_map/ppermute | solution.py:30
  836.6 67.0 %collective-permute-start.95 = (bf16[1024,512]{1,0:T(8,128)(2,1)S(1)}, bf16[1024,512]{1,0:T(8,128)(2,1)S(1)}, u32[]{:S(2)}, u32[]{:S(2)}) collective-permute-start(bf16[1024,512]{1,0:T(8,128)(2,1)S(1)} %pad_maximum_fusion.11), channel_id=1, source_target_pairs={{0,4},{4,0},{8,12},{12,8},{16,20},{20,16},{24,28},{28,24},{1,5},{5... | collective-permute-start | bytes 3145736 | tf_op jit(solution)/shard_map/ppermute | solution.py:30
  853.8 51.3 %collective-permute-start.97 = (bf16[512,768]{1,0:T(8,128)(2,1)S(1)}, bf16[512,768]{1,0:T(8,128)(2,1)S(1)}, u32[]{:S(2)}, u32[]{:S(2)}) collective-permute-start(bf16[512,768]{1,0:T(8,128)(2,1)S(1)} %pad_maximum_fusion.14), channel_id=1, source_target_pairs={{0,8},{4,12},{8,0},{12,4},{16,24},{20,28},{24,16},{28,20},{1,9},{5... | collective-permute-start | bytes 2359304 | tf_op jit(solution)/shard_map/ppermute | solution.py:30
  907.1 44.9 %collective-permute-start.100 = (bf16[128,2048]{1,0:T(8,128)(2,1)S(1)}, bf16[128,2048]{1,0:T(8,128)(2,1)S(1)}, u32[]{:S(2)}, u32[]{:S(2)}) collective-permute-start(bf16[128,2048]{1,0:T(8,128)(2,1)S(1)} %get-tuple-element.555), channel_id=1, source_target_pairs={{0,8},{4,12},{8,16},{12,20},{16,24},{20,28},{24,0},{28,4},{1,9},{5... | collective-permute-start | bytes 1572872 | tf_op jit(solution)/shard_map/ppermute | solution.py:35
  907.1 44.9 %collective-permute-start.101 = (bf16[128,2048]{1,0:T(8,128)(2,1)S(1)}, bf16[128,2048]{1,0:T(8,128)(2,1)S(1)}, u32[]{:S(2)}, u32[]{:S(2)}) collective-permute-start(bf16[128,2048]{1,0:T(8,128)(2,1)S(1)} %get-tuple-element.557), channel_id=1, source_target_pairs={{0,24},{4,28},{8,0},{12,4},{16,8},{20,12},{24,16},{28,20},{1,25},{... | collective-permute-start | bytes 1572872 | tf_op jit(solution)/shard_map/ppermute | solution.py:35
  910.9 50.8 %collective-permute-start.102 = (bf16[128,2048]{1,0:T(8,128)(2,1)S(1)}, bf16[128,2048]{1,0:T(8,128)(2,1)S(1)}, u32[]{:S(2)}, u32[]{:S(2)}) collective-permute-start(bf16[128,2048]{1,0:T(8,128)(2,1)S(1)} %get-tuple-element.556), channel_id=1, source_target_pairs={{0,16},{4,20},{8,24},{12,28},{16,0},{20,4},{24,8},{28,12},{1,17},{... | collective-permute-start | bytes 1572872 | tf_op jit(solution)/shard_map/ppermute | solution.py:35
  920.8 54.4 %collective-permute-start.108 = (bf16[1024,768]{1,0:T(8,128)(2,1)S(1)}, bf16[1024,768]{1,0:T(8,128)(2,1)}, u32[]{:S(2)}, u32[]{:S(2)}) collective-permute-start(bf16[1024,768]{1,0:T(8,128)(2,1)S(1)} %pad_maximum_fusion.6), channel_id=1, source_target_pairs={{0,4},{4,0},{8,12},{12,8},{16,20},{20,16},{24,28},{28,24},{1,5},{5... | collective-permute-start | bytes 4718600 | tf_op jit(solution)/shard_map/ppermute | solution.py:30
  (183 other events, 2673.8 us)
